TPU v7x, 256 devices: a whole 4x4x8 slice. The times are simulated.
256 devices in a mesh: grp: 16 (over x, y), ep: 16 (over z, core).
Axes of the slice: x: 4, y: 4, z: 8, core: 2. Of those that a mesh axis runs over, the one named last changes fastest.
Arguments:
- tokens: bfloat16 [16384, 1440], P(('grp', 'ep')), parts along dimension 0, may hold values from -6 to 6
- expert_ids: int32 [16384, 4], P(('grp', 'ep')), parts along dimension 0, may hold values from 0 to 15, as said below
- gate_weights: float32 [16384, 4], P(('grp', 'ep')), parts along dimension 0, may hold values from 0.1 to 1
- row_counts: int32 [256], P(('grp', 'ep')), parts along dimension 0, may hold values from 32 to 64, as said below
- w_gate: bfloat16 [16, 1440, 1440], P('ep'), may hold values from -0.15625 to 0.15625
- w_up: bfloat16 [16, 1440, 1440], P('ep'), may hold values from -0.15625 to 0.15625
- w_down: bfloat16 [16, 1440, 1440], P('ep'), may hold values from -0.15625 to 0.15625
Outputs:
- moe_out: bfloat16 [16384, 1440], P(('grp', 'ep')), parts along dimension 0
There are 16 independent parts, one for each index of `grp`. A program takes and returns all parts, laid end to end along the dimension named above; an argument that names none is the same for every part. Nothing has to cross between parts.
Inputs may be any that keep to these rules, and one draw needn't show every extreme that they name: `expert_ids`: each row names 4 different experts; in the 64 rows of one device one expert, the hot one, the same on every device of a group, is named exactly 48 times, and every other expert at most 14 times, some exactly 14 times. `row_counts`: live rows are the first ones of a device's block; some device of each group has all 64 live.
All inputs are finite; a program needn't handle non-finite values.
Results may differ from a plain program's by a relative error of at most 0.0058.
Values may be sent and summed in bfloat16 or wider, within the bound.
No kernel may reach another device: no remote copies, remote signals or barrier semaphores. Data moves between devices by JAX's collectives and lax.ppermute only.
A program may use at most 128 MiB of HBM per device.

v0:
```python
import jax
import jax.numpy as jnp
from jax import lax
from jax.sharding import PartitionSpec as P


def expert_apply(row_block, gate_matrix, up_matrix, down_matrix):
    gate = jnp.dot(row_block, gate_matrix, preferred_element_type=jnp.float32)
    up_value = jnp.dot(row_block, up_matrix, preferred_element_type=jnp.float32)
    hidden = ((up_value + 1.0) * gate * jax.nn.sigmoid(1.702 * gate)).astype(jnp.bfloat16)
    return jnp.dot(hidden, down_matrix, preferred_element_type=jnp.float32).astype(jnp.bfloat16)


def local(tokens, expert_ids, gate_weights, row_counts, w_gate, w_up, w_down):
    row_total, top_total = expert_ids.shape
    feature_width = tokens.shape[1]
    device_total = lax.axis_size("ep")
    expert_total = device_total * w_gate.shape[0]
    capacity = 3 * row_total // 4
    position = jnp.arange(row_total, dtype=jnp.int32)
    live_rows = position < row_counts[0]
    pair_live = jnp.repeat(live_rows, top_total)
    flat_ids = expert_ids.reshape(-1)
    pair_row = jnp.arange(row_total * top_total, dtype=jnp.int32) // top_total
    pair_weight = jnp.where(live_rows[:, None], gate_weights, 0.0).reshape(-1)
    expert_match = flat_ids[:, None] == jnp.arange(expert_total, dtype=jnp.int32)[None, :]
    extended = jnp.concatenate([tokens, jnp.zeros((1, feature_width), tokens.dtype)], axis=0)
    flags = (expert_match & pair_live[:, None]).astype(jnp.int32)
    slot = jnp.sum((jnp.cumsum(flags, axis=0) - flags) * flags, axis=1)
    target = jnp.where(pair_live, flat_ids * capacity + slot, expert_total * capacity)
    source_index = (
        jnp.full((expert_total * capacity,), row_total, jnp.int32)
        .at[target]
        .set(pair_row, mode="drop")
    )
    send_buffer = extended[source_index].reshape(expert_total, capacity, feature_width)
    send_buffer, pair_target = (send_buffer, target)
    received = lax.all_to_all(send_buffer, "ep", split_axis=0, concat_axis=0, tiled=True)
    item_count = received.shape[1]
    flat_rows = received.reshape(-1, feature_width)
    outputs = expert_apply(flat_rows, w_gate[0], w_up[0], w_down[0])
    returned = lax.all_to_all(
        outputs.reshape(device_total, item_count, feature_width),
        "ep",
        split_axis=0,
        concat_axis=0,
        tiled=True,
    )
    last_slot = expert_total * capacity - 1
    fetched = returned.reshape(-1, feature_width)[jnp.minimum(pair_target, last_slot)]
    weighted = fetched.astype(jnp.float32) * pair_weight[:, None]
    return jnp.sum(weighted.reshape(row_total, top_total, feature_width), axis=1).astype(
        jnp.bfloat16
    )


def solution(mesh):
    in_specs = (
        P(("grp", "ep"), None),
        P(("grp", "ep"), None),
        P(("grp", "ep"), None),
        P(("grp", "ep")),
        P("ep", None, None),
        P("ep", None, None),
        P("ep", None, None),
    )
    out_specs = P(("grp", "ep"), None)
    return jax.shard_map(local, mesh=mesh, in_specs=in_specs, out_specs=out_specs, check_vma=False)
```

profile of v0, /device:TPU:26, one launch (start us, length us, event | category | flops | bytes accessed | tf_op | source)
XLA Modules:
  0.0 167.0 jit_solution(12456038797936191221)
XLA Ops:
  0.0 0.8 copy.12
  0.8 0.1 eq.29
  0.9 0.1 eq.25
  1.7 0.1 broadcast_in_dim.33.clone
  1.7 0.1 and.21
  1.9 0.1 reshape.118
  2.0 0.7 broadcast_multiply_fusion
  2.7 0.1 broadcast_in_dim.34
  2.7 0.1 broadcast_in_dim.35
  2.9 0.6 reduce-window.6
  3.5 0.2 slice_reduce_fusion
  3.7 0.1 copy.11
  3.8 0.1 mul.46
  3.9 0.1 fusion.15
  4.0 1.4 scatter_custom_fusion
  5.5 0.9 concatenate.3
  6.4 2.9 %gather_fusion = bf16[768,1440]{1,0:T(8,128)(2,1)S(1)} fusion(bf16[65,1440]{1,0:T(8,128)(2,1)S(1)} %concatenate.3, s32[1024]{0:T(1024)S(1)} %pad_clamp_fusion.1), kind=kCustom, calls=%fused_computation | custom fusion | bytes 4426752 | tf_op jit(solution)/shard_map/gather | solution.py:36
  9.3 64.5 %all_to_all.10 = bf16[16,48,1440]{2,1,0:T(8,128)(2,1)S(1)} all-to-all(bf16[16,48,1440]{2,1,0:T(8,128)(2,1)S(1)} %bitcast.48), channel_id=1, replica_groups=mesh['grp'=16,'ep'=16] {'ep'}, dimensions={0} | all-to-all | bytes 4423680 | tf_op jit(solution)/shard_map/all_to_all | solution.py:38
  73.8 0.0 copy-start
  73.8 1.4 copy-done
  75.3 8.0 %fusion.4 = f32[768,1440]{0,1:T(8,128)} fusion(bf16[768,1440]{1,0:T(8,128)(2,1)S(1)} %bitcast.49, bf16[1,1440,1440]{2,1,0:T(8,128)(2,1)} %param.12), kind=kOutput, calls=%fused_computation.7 | convolution fusion | flops 3185049600 | bytes 10782720 | tf_op jit(solution)/shard_map/dot_general | solution.py:9
  83.3 19.1 %fusion.8 = bf16[768,1440]{0,1:T(8,128)(2,1)S(1)} fusion(bf16[1,1440,1440]{2,1,0:T(8,128)(2,1)} %param.13, f32[768,1440]{0,1:T(8,128)} %fusion.4, bf16[768,1440]{1,0:T(8,128)(2,1)} %bitcast.50, bf16[1,1440,1440]{2,1,0:T(8,128)(2,1)} %param.11), kind=kOutput, calls=%fused_computation.10 | convolution fusion | flops 6380052480 | bytes 17141760 | tf_op jit(solution)/shard_map/dot_general | solution.py:11
  102.4 0.0 copy-start.1
  102.4 2.4 %copy.16 = bf16[768,1440]{1,0:T(8,128)(2,1)} copy(bf16[768,1440]{0,1:T(8,128)(2,1)S(1)} %fusion.8) | data formatting | bytes 4423680 | tf_op jit(solution)/shard_map/convert_element_type | solution.py:11
  104.9 3.7 %all-to-all-start.1 = ((bf16[16,48,1440]{2,1,0:T(8,128)(2,1)}), bf16[16,48,1440]{2,1,0:T(8,128)(2,1)S(1)}, u32[]{:S(2)}, u32[]{:S(2)}) async-start(bf16[16,48,1440]{2,1,0:T(8,128)(2,1)} %bitcast.47), calls=%async_computation.1 | async-start | bytes 4718592 | tf_op jit(solution)/shard_map/all_to_all | solution.py:42
  108.6 0.0 copy-done.1
  108.6 0.1 copy.17
  108.7 54.7 %all-to-all-done.1 = bf16[16,48,1440]{2,1,0:T(8,128)(2,1)S(1)} async-done(((bf16[16,48,1440]{2,1,0:T(8,128)(2,1)}), bf16[16,48,1440]{2,1,0:T(8,128)(2,1)S(1)}, u32[]{:S(2)}, u32[]{:S(2)}) %all-to-all-start.1) | async-done | bytes 2211872 | tf_op jit(solution)/shard_map/all_to_all | solution.py:42
  163.5 1.3 gather_fusion.1
  164.7 0.5 reshape.124
  165.2 1.8 %multiply_reduce_fusion = bf16[64,1440]{1,0:T(8,128)(2,1)} fusion(f32[64,4,1440]{2,1,0:T(4,128)S(1)} %reshape.124, f32[64,4]{1,0:T(8,128)S(1)} %copy.17), kind=kLoop, calls=%fused_computation.11 | loop fusion | flops 645120 | bytes 1659904 | tf_op jit(solution)/shard_map/reduce_sum | solution.py:52
  (11 shorter events, 0.1 us)
Async XLA Ops:
  73.8 1.4 copy-start
  102.4 6.2 %copy-start.1 = (f32[64,4]{0,1:T(4,128)S(1)}, f32[64,4]{0,1:T(4,128)}, u32[]{:S(2)}) copy-start(f32[64,4]{0,1:T(4,128)} %param.9) | copy-start | bytes 3076
  104.9 58.6 %all-to-all-start.1 = ((bf16[16,48,1440]{2,1,0:T(8,128)(2,1)}), bf16[16,48,1440]{2,1,0:T(8,128)(2,1)S(1)}, u32[]{:S(2)}, u32[]{:S(2)}) async-start(bf16[16,48,1440]{2,1,0:T(8,128)(2,1)} %bitcast.47), calls=%async_computation.1 | async-start | bytes 4718592 | tf_op jit(solution)/shard_map/all_to_all | solution.py:42
where the time goes:
time: 168 us; the launch traced here: 167 us
  blocking collectives  64.5 us (38%)
  waiting for transfers between devices  54.7 us (33%)
  matrix products  27.1 us (16%)
  local copies, waits for them, and re-layouts  12.9 us (8%)
  starting transfers between devices  3.72 us (2%)
  other arithmetic  3.25 us (2%)
    all_to_all x1, blocking collectives, local(): lax.all_to_all(send_buffer, 'ep', split_axis=0, concat_axis=0, tiled=True)  64.5 us
    all_to_all x1, waiting for transfers between devices, local(): lax.all_to_all(outputs.reshape(device_total, item_count, feature_width),...  54.7 us
    dot_general x1, matrix products, expert_apply(): jnp.dot(hidden, down_matrix, preferred_element_type=jnp.float32)  19.1 us
    dot_general x1, matrix products, expert_apply(): up_value = jnp.dot(row_block, up_matrix, preferred_element_type=jnp.float32)  8.05 us
    all_to_all x1, starting transfers between devices, local(): lax.all_to_all(outputs.reshape(device_total, item_count, feature_width),...  3.72 us
  transfers between devices with their start and end apart: 1, of which 1 were waited for; matrix products, arithmetic and copies ran while one was open for 0% of the time, Pallas kernels for 0%

commit v1 on v0

v1 whole, which is shorter than its diff:
```python
import jax
import jax.numpy as jnp
from jax import lax
from jax.experimental import pallas as pl
from jax.experimental.pallas import tpu as pltpu
from jax.sharding import PartitionSpec as P

LANES = 128
BF16, F32 = jnp.bfloat16, jnp.float32


def pad_up(n, m):
    return -(-n // m) * m


def ring_pairs(n):
    chips = n // 2

    def odd(chip):
        return (chip - 1) % chips if chip % 2 == 0 else (chip + 1) % chips

    swap = [(i, i ^ 1) for i in range(n)]
    even_pairs = [(i, i ^ 2) for i in range(n)]
    odd_pairs = [(i, odd(i // 2) * 2 + i % 2) for i in range(n)]
    return swap, even_pairs, odd_pairs


def route_kernel(experts, count_ref, x_ref, ids_ref, gw_ref, out_ref):
    rows, width = x_ref.shape
    last = width // LANES * LANES
    start = width - last
    lane = lax.broadcasted_iota(jnp.int32, (rows, LANES), 1) - start
    expert = lane & (experts - 1)
    weight = jnp.zeros((rows, LANES), F32)
    ids, gw = ids_ref[...], gw_ref[...]
    for k in range(ids.shape[1]):
        weight += jnp.where(ids[:, k : k + 1] == expert, gw[:, k : k + 1], 0.0)
    live = lax.broadcasted_iota(jnp.int32, (rows, LANES), 0) < count_ref[0]
    weight = jnp.where(live, weight, 0.0)
    high = weight.astype(BF16).astype(F32)
    middle = (weight - high).astype(BF16).astype(F32)
    low = weight - high - middle
    part = jnp.where(lane < experts, high, jnp.where(lane < 2 * experts, middle, low))
    part = jnp.where((lane >= 0) & (lane < 3 * experts), part, 0.0)
    out_ref[:, :last] = x_ref[:, :last]
    tail = jnp.concatenate([x_ref[:, last:].astype(F32), jnp.zeros((rows, LANES - start), F32)], axis=1)
    out_ref[:, last:] = jnp.where(lane < 0, tail, part).astype(BF16)


def expert_kernel(experts, count, *refs):
    xs, (wg, wu, wd), ys, hidden = refs[:count], refs[count : count + 3], refs[count + 3 : -1], refs[-1]
    width, ff = wg.shape
    last = width // LANES * LANES
    start = width - last
    x = jnp.concatenate([r[:, :width] for r in xs], axis=0) if count > 1 else xs[0][:, :width]
    tail = jnp.concatenate([r[:, last : last + LANES] for r in xs], axis=0).astype(F32)
    lane = lax.broadcasted_iota(jnp.int32, tail.shape, 1) - start
    mine = (lane >= 0) & (lane < 3 * experts) & ((lane & (experts - 1)) == lax.axis_index("ep"))
    weight = jnp.sum(jnp.where(mine, tail, 0.0), axis=1, keepdims=True)
    for lo in range(0, ff, 256):
        hi = min(lo + 256, ff)
        gate = jnp.dot(x, wg[:, lo:hi], preferred_element_type=F32)
        up = jnp.dot(x, wu[:, lo:hi], preferred_element_type=F32)
        hidden[:, lo:hi] = ((up + 1.0) * gate * jax.nn.sigmoid(1.702 * gate)).astype(BF16)
    h = hidden[...]
    for lo in range(0, width, 256):
        hi = min(lo + 256, width)
        y = jnp.dot(h, wd[:, lo:hi], preferred_element_type=F32).astype(BF16).astype(F32)
        y = (y * weight).astype(BF16)
        at = 0
        for r in ys:
            r[:, lo:hi] = y[at : at + r.shape[0]]
            at += r.shape[0]


def experts_apply(experts, blocks, weights):
    width, ff = weights[0].shape
    total = sum(b.shape[0] for b in blocks)
    vmem = pl.BlockSpec(memory_space=pltpu.VMEM)
    return pl.pallas_call(
        lambda *refs: expert_kernel(experts, len(blocks), *refs),
        out_shape=[jax.ShapeDtypeStruct((b.shape[0], width), BF16) for b in blocks],
        in_specs=[vmem] * (len(blocks) + 3),
        out_specs=[vmem] * len(blocks),
        scratch_shapes=[pltpu.VMEM((total, ff), BF16)],
        compiler_params=pltpu.CompilerParams(vmem_limit_bytes=40 << 20),
        cost_estimate=pl.CostEstimate(flops=6 * total * width * ff, bytes_accessed=total * width * 4, transcendentals=total * ff),
        name="experts",
    )(*[pltpu.with_memory_space_constraint(b, pltpu.VMEM) for b in blocks], *weights)


def add(*terms):
    total = terms[0].astype(F32)
    for t in terms[1:]:
        total = total + t.astype(F32)
    return total.astype(BF16)


def local(tokens, expert_ids, gate_weights, row_counts, w_gate, w_up, w_down):
    n = lax.axis_size("ep")
    rows, width = tokens.shape
    half = rows // 2
    experts = n * w_gate.shape[0]
    swap, even, odd = ring_pairs(n)

    def send(x, pairs):
        return lax.ppermute(x, "ep", pairs)

    vmem = pl.BlockSpec(memory_space=pltpu.VMEM)
    weights = [pltpu.with_memory_space_constraint(w.reshape(w.shape[1:]), pltpu.VMEM) for w in (w_gate, w_up, w_down)]
    own = pl.pallas_call(
        lambda *refs: route_kernel(experts, *refs),
        out_shape=jax.ShapeDtypeStruct((rows, pad_up(width, LANES)), BF16),
        in_specs=[pl.BlockSpec(memory_space=pltpu.SMEM), vmem, vmem, vmem],
        out_specs=vmem,
        name="route",
    )(row_counts, tokens, expert_ids, gate_weights)

    def chip_sum(blocks):
        theirs = [send(b, swap) for b in blocks]
        out = experts_apply(experts, blocks + theirs, weights)
        k = len(blocks)
        return [add(out[i], send(out[k + i], swap)) for i in range(k)]

    e1, o1 = send(own, even), send(own, odd)
    (t0,) = chip_sum([own])
    e2, o2 = send(o1, even), send(e1, odd)
    te1, to1 = chip_sum([e1, o1])
    e3, o3 = send(o2, even), send(e2, odd)
    te2, to2 = chip_sum([e2, o2])
    e4, o4 = send(o3[:half], even), send(e3[half:], odd)
    te3, to3 = chip_sum([e3, o3])
    te4, to4 = chip_sum([e4, o4])
    re, ro = send(te4, even), send(to4, odd)
    ao3 = jnp.concatenate([add(to3[:half], re), to3[half:]], axis=0)
    ae3 = jnp.concatenate([te3[:half], add(te3[half:], ro)], axis=0)
    re, ro = send(ae3, even), send(ao3, odd)
    ao2, ae2 = add(to2, re), add(te2, ro)
    re, ro = send(ae2, even), send(ao2, odd)
    ao1, ae1 = add(to1, re), add(te1, ro)
    re, ro = send(ae1, even), send(ao1, odd)
    return add(t0, re, ro)


def solution(mesh):
    rows = P(("grp", "ep"), None)
    in_specs = (rows, rows, rows, P(("grp", "ep"))) + (P("ep", None, None),) * 3
    return jax.shard_map(local, mesh=mesh, in_specs=in_specs, out_specs=rows, check_vma=False)
```

time: 168 us -> 107 us (0.64)
  blocking collectives: 64.5 us -> 0 us
  matrix products: 27.1 us -> 0 us
  starting transfers between devices: 3.72 us -> 25.7 us
  Pallas kernels: 0 us -> 19.5 us
  waiting for transfers between devices: 54.7 us -> 44.2 us
  local copies, waits for them, and re-layouts: 12.9 us -> 15 us
  other arithmetic: 3.25 us -> 1.31 us
    all_to_all x1 -> x0, blocking collectives: 64.5 us -> none  [local(): lax.all_to_all(send_buffer, 'ep', split_axis=0, concat_axis=0, tiled=True)]
    all_to_all x1 -> x0, waiting for transfers between devices: 54.7 us -> none  [local(): lax.all_to_all(outputs.reshape(device_total, item_count, feature_width),...]
    ppermute x0 -> x34, waiting for transfers between devices: none -> 44.2 us  [send(): return lax.ppermute(x, 'ep', pairs)]
    dot_general x2 -> x0, matrix products: 27.1 us -> none  [the longest x1 19.1 us: expert_apply(): jnp.dot(hidden, down_matrix, preferred_element_type=jnp.float32)]
    ppermute x0 -> x34, starting transfers between devices: none -> 25.7 us  [send(): return lax.ppermute(x, 'ep', pairs)]
    pallas_call x0 -> x6, Pallas kernels: none -> 19.5 us  [the longest x5 17.7 us: experts_apply(): pl.pallas_call(lambda *refs: expert_kernel(experts, len(blocks), *refs),...]
    unnamed x5 -> x34, local copies, waits for them, and re-layouts: 2.22 us -> 15 us
    gather x2 -> x0, local copies, waits for them, and re-layouts: 4.19 us -> none  [the longest x1 2.94 us: local(): extended[source_index].reshape(expert_total, capacity, feature_width)]
  transfers between devices with their start and end apart: 1 -> 34, of which waited for: 1 -> 13; matrix products, arithmetic and copies ran while one was open for 0% -> 1% of each run, Pallas kernels for 0% -> 17%
where the time goes in v1:
time: 107 us
  waiting for transfers between devices  44.2 us (41%)
  starting transfers between devices  25.7 us (24%)
  Pallas kernels  19.5 us (18%)
  local copies, waits for them, and re-layouts  15 us (14%)
  other arithmetic  1.31 us (1%)
    ppermute x34, waiting for transfers between devices, send(): return lax.ppermute(x, 'ep', pairs)  44.2 us
    ppermute x34, starting transfers between devices, send(): return lax.ppermute(x, 'ep', pairs)  25.7 us
    pallas_call x5, Pallas kernels, experts_apply(): pl.pallas_call(lambda *refs: expert_kernel(experts, len(blocks), *refs),...  17.7 us
    unnamed x34, local copies, waits for them, and re-layouts  15 us
  transfers between devices with their start and end apart: 34, of which 13 were waited for; matrix products, arithmetic and copies ran while one was open for 1% of the time, Pallas kernels for 17%

profile of v1, /device:TPU:26, one launch (start us, length us, event | category | flops | bytes accessed | tf_op | source)
XLA Modules:
  0.0 106.6 jit_solution(8808913850599438717)
XLA Ops:
  0.0 1.4 %copy.8.refs_2_ = s32[64,4]{1,0:T(8,128)} copy(s32[64,4]{0,1:T(4,128)} %param.8) | data formatting | bytes 2048 | tf_op args[1]
  1.4 1.4 %copy.9.refs_3_ = f32[64,4]{1,0:T(8,128)} copy(f32[64,4]{0,1:T(4,128)} %param.9) | data formatting | bytes 2048 | tf_op args[2]
  3.4 1.8 %route.1.refs_0_ = bf16[64,1536]{1,0:T(8,128)(2,1)} custom-call(s32[1]{0:T(128)S(6)} %copy.10.refs_0_, bf16[64,1440]{1,0:T(8,128)(2,1)} %refs_1_.1, s32[64,4]{1,0:T(8,128)} %copy.8.refs_2_, f32[64,4]{1,0:T(8,128)} %copy.9.refs_3_), custom_call_target="tpu_custom_call" | custom-call | tf_op jit(solution)/shard_map/route/pallas_call | solution.py:111
  5.2 5.9 %collective-permute-start.3 = (bf16[64,1536]{1,0:T(8,128)(2,1)}, bf16[64,1536]{1,0:T(8,128)(2,1)S(1)}, u32[]{:S(2)}, u32[]{:S(2)}) collective-permute-start(bf16[64,1536]{1,0:T(8,128)(2,1)} %route.1.refs_0_), channel_id=1, source_target_pairs={{0,14},{1,15},{2,4},{3,5},{4,2},{5,3},{6,8},{7,9},{8,6},{9,7},{10,... | collective-permute-start | bytes 589832 | tf_op jit(solution)/shard_map/ppermute | solution.py:107
  11.1 5.1 %collective-permute-done.3.refs_1_ = bf16[64,1536]{1,0:T(8,128)(2,1)S(1)} collective-permute-done((bf16[64,1536]{1,0:T(8,128)(2,1)}, bf16[64,1536]{1,0:T(8,128)(2,1)S(1)}, u32[]{:S(2)}, u32[]{:S(2)}) %collective-permute-start.3) | collective-permute-done | bytes 196640 | tf_op jit(solution)/shard_map/ppermute | solution.py:107
  16.2 1.5 %collective-permute-done.2.refs_0_ = bf16[64,1536]{1,0:T(8,128)(2,1)S(1)} collective-permute-done((bf16[64,1536]{1,0:T(8,128)(2,1)}, bf16[64,1536]{1,0:T(8,128)(2,1)S(1)}, u32[]{:S(2)}, u32[]{:S(2)}) %collective-permute-start.2) | collective-permute-done | bytes 196640 | tf_op jit(solution)/shard_map/ppermute | solution.py:107
  17.7 1.5 %collective-permute-start.8 = (bf16[64,1536]{1,0:T(8,128)(2,1)S(1)}, bf16[64,1536]{1,0:T(8,128)(2,1)S(1)}, u32[]{:S(2)}, u32[]{:S(2)}) collective-permute-start(bf16[64,1536]{1,0:T(8,128)(2,1)S(1)} %collective-permute-done.2.refs_0_), channel_id=1, source_target_pairs={{0,14},{1,15},{2,4},{3,5},{4,2},{5,3},{6,8},{7,9},{8,6},{9,7},{10,... | collective-permute-start | bytes 589832 | tf_op jit(solution)/shard_map/ppermute | solution.py:107
  19.2 3.1 %collective-permute-done.7.refs_0_ = bf16[64,1536]{1,0:T(8,128)(2,1)S(1)} collective-permute-done((bf16[64,1536]{1,0:T(8,128)(2,1)S(1)}, bf16[64,1536]{1,0:T(8,128)(2,1)S(1)}, u32[]{:S(2)}, u32[]{:S(2)}) %collective-permute-start.7) | collective-permute-done | bytes 196640 | tf_op jit(solution)/shard_map/ppermute | solution.py:107
  22.3 2.6 %collective-permute-start.13 = (bf16[64,1536]{1,0:T(8,128)(2,1)S(1)}, bf16[64,1536]{1,0:T(8,128)(2,1)S(1)}, u32[]{:S(2)}, u32[]{:S(2)}) collective-permute-start(bf16[64,1536]{1,0:T(8,128)(2,1)S(1)} %collective-permute-done.7.refs_0_), channel_id=1, source_target_pairs={{0,14},{1,15},{2,4},{3,5},{4,2},{5,3},{6,8},{7,9},{8,6},{9,7},{10,... | collective-permute-start | bytes 589832 | tf_op jit(solution)/shard_map/ppermute | solution.py:107
  25.0 0.5 collective-permute-start.5
  25.5 2.3 %copy-done = bf16[1,1440,1440]{2,1,0:T(8,128)(2,1)S(1)} copy-done((bf16[1,1440,1440]{2,1,0:T(8,128)(2,1)S(1)}, bf16[1,1440,1440]{2,1,0:T(8,128)(2,1)}, u32[]{:S(2)}) %copy-start) | copy-done | bytes 4147224
  27.7 2.3 %copy-done.1 = bf16[1,1440,1440]{2,1,0:T(8,128)(2,1)S(1)} copy-done((bf16[1,1440,1440]{2,1,0:T(8,128)(2,1)S(1)}, bf16[1,1440,1440]{2,1,0:T(8,128)(2,1)}, u32[]{:S(2)}) %copy-start.1) | copy-done | bytes 4147224
  30.0 2.3 %copy-done.3 = bf16[1,1440,1440]{2,1,0:T(8,128)(2,1)S(1)} copy-done((bf16[1,1440,1440]{2,1,0:T(8,128)(2,1)S(1)}, bf16[1,1440,1440]{2,1,0:T(8,128)(2,1)}, u32[]{:S(2)}) %copy-start.3) | copy-done | bytes 4147224
  32.2 0.9 copy-done.5
  33.1 2.0 %experts.5 = (bf16[64,1440]{1,0:T(8,128)(2,1)S(1)}, bf16[64,1440]{1,0:T(8,128)(2,1)S(1)}) custom-call(bf16[64,1536]{1,0:T(8,128)(2,1)S(1)} %copy-done.5, bf16[64,1536]{1,0:T(8,128)(2,1)S(1)} %collective-permute-done.refs_1_, bf16[1440,1440]{1,0:T(8,128)(2,1)S(1)} %bitcast.3, bf16[1440,1440]{1,0:T(8,128)(2,1)S(1)} %bitcast.10, bf16[1440,1440]{1,0:T(8,128)(2,1)S(1)} %bitcast.17), custom_call_target="tpu_custom_call" | custom-call | flops 1592524800 | bytes 737280 | tf_op jit(solution)/shard_map/experts/pallas_call | solution.py:80
  35.4 0.4 collective-permute-start.10
  35.8 0.2 collective-permute-start.9
  36.0 2.1 %collective-permute-start.17 = (bf16[32,1536]{1,0:T(8,128)(2,1)S(1)}, bf16[32,1536]{1,0:T(8,128)(2,1)S(1)}, u32[]{:S(2)}, u32[]{:S(2)}) collective-permute-start(bf16[32,1536]{1,0:T(8,128)(2,1)S(1)} %slice.26), channel_id=1, source_target_pairs={{0,2},{1,3},{2,0},{3,1},{4,6},{5,7},{6,4},{7,5},{8,10},{9,11},{10,... | collective-permute-start | bytes 294920 | tf_op jit(solution)/shard_map/ppermute | solution.py:107
  38.1 1.2 %collective-permute-start.18 = (bf16[32,1536]{1,0:T(8,128)(2,1)S(1)}, bf16[32,1536]{1,0:T(8,128)(2,1)S(1)}, u32[]{:S(2)}, u32[]{:S(2)}) collective-permute-start(bf16[32,1536]{1,0:T(8,128)(2,1)S(1)} %slice.27), channel_id=1, source_target_pairs={{0,14},{1,15},{2,4},{3,5},{4,2},{5,3},{6,8},{7,9},{8,6},{9,7},{10,... | collective-permute-start | bytes 294920 | tf_op jit(solution)/shard_map/ppermute | solution.py:107
  39.3 2.3 %copy-done.2 = bf16[1,1440,1440]{2,1,0:T(8,128)(2,1)S(1)} copy-done((bf16[1,1440,1440]{2,1,0:T(8,128)(2,1)S(1)}, bf16[1,1440,1440]{2,1,0:T(8,128)(2,1)}, u32[]{:S(2)}) %copy-start.2) | copy-done | bytes 4147224
  41.6 2.3 %copy-done.4 = bf16[1,1440,1440]{2,1,0:T(8,128)(2,1)S(1)} copy-done((bf16[1,1440,1440]{2,1,0:T(8,128)(2,1)S(1)}, bf16[1,1440,1440]{2,1,0:T(8,128)(2,1)}, u32[]{:S(2)}) %copy-start.4) | copy-done | bytes 4147224
  43.8 4.6 %experts.6 = (bf16[64,1440]{1,0:T(8,128)(2,1)S(1)}, bf16[64,1440]{1,0:T(8,128)(2,1)S(1)}, bf16[64,1440]{1,0:T(8,128)(2,1)}, bf16[64,1440]{1,0:T(8,128)(2,1)}) custom-call(bf16[64,1536]{1,0:T(8,128)(2,1)S(1)} %collective-permute-done.2.refs_0_, bf16[64,1536]{1,0:T(8,128)(2,1)S(1)} %collective-permute-done.3.refs_1_, ...), custom_call_target="tpu_custom_call" | custom-call | flops 3185049600 | bytes 1474560 | tf_op jit(solution)/shard_map/experts/pallas_call | solution.py:80
  48.5 0.5 collective-permute-start.15
  49.1 0.4 collective-permute-start.20
  49.5 4.6 %experts.7 = (bf16[64,1440]{1,0:T(8,128)(2,1)S(1)}, bf16[64,1440]{1,0:T(8,128)(2,1)S(1)}, bf16[64,1440]{1,0:T(8,128)(2,1)}, bf16[64,1440]{1,0:T(8,128)(2,1)}) custom-call(bf16[64,1536]{1,0:T(8,128)(2,1)S(1)} %collective-permute-done.7.refs_0_, bf16[64,1536]{1,0:T(8,128)(2,1)S(1)} %collective-permute-done.8.refs_1_, ...), custom_call_target="tpu_custom_call" | custom-call | flops 3185049600 | bytes 1474560 | tf_op jit(solution)/shard_map/experts/pallas_call | solution.py:80
  54.2 0.5 collective-permute-start.26
  54.7 2.0 %experts.9 = (bf16[32,1440]{1,0:T(8,128)(2,1)S(1)}, bf16[32,1440]{1,0:T(8,128)(2,1)S(1)}, bf16[32,1440]{1,0:T(8,128)(2,1)S(1)}, bf16[32,1440]{1,0:T(8,128)(2,1)S(1)}) custom-call(bf16[32,1536]{1,0:T(8,128)(2,1)S(1)} %collective-permute-done.17.refs_0_, bf16[32,1536]{1,0:T(8,128)(2,1)S(1)} %collective-permute-done.18.refs_1_, ...), custom_call_target="tpu_custom_call" | custom-call | flops 1592524800 | bytes 737280 | tf_op jit(solution)/shard_map/experts/pallas_call | solution.py:80
  56.8 0.2 collective-permute-start.11
  57.0 0.4 collective-permute-start.21
  57.4 4.5 %experts.8 = (bf16[64,1440]{1,0:T(8,128)(2,1)S(1)}, bf16[64,1440]{1,0:T(8,128)(2,1)S(1)}, bf16[64,1440]{1,0:T(8,128)(2,1)}, bf16[64,1440]{1,0:T(8,128)(2,1)}) custom-call(bf16[64,1536]{1,0:T(8,128)(2,1)S(1)} %collective-permute-done.12.refs_0_, bf16[64,1536]{1,0:T(8,128)(2,1)S(1)} %collective-permute-done.13.refs_1_, ...), custom_call_target="tpu_custom_call" | custom-call | flops 3185049600 | bytes 1474560 | tf_op jit(solution)/shard_map/experts/pallas_call | solution.py:80
  61.9 0.3 collective-permute-start.29
  62.3 0.9 collective-permute-done.29
  63.2 0.3 collective-permute-start.16
  63.6 1.3 %collective-permute-done.16 = bf16[64,1440]{1,0:T(8,128)(2,1)S(1)} collective-permute-done((bf16[64,1440]{1,0:T(8,128)(2,1)}, bf16[64,1440]{1,0:T(8,128)(2,1)S(1)}, u32[]{:S(2)}, u32[]{:S(2)}) %collective-permute-start.16) | collective-permute-done | bytes 184352 | tf_op jit(solution)/shard_map/ppermute | solution.py:107
  64.9 2.0 %collective-permute-start.22 = (bf16[32,1440]{1,0:T(8,128)(2,1)S(1)}, bf16[32,1440]{1,0:T(8,128)(2,1)S(1)}, u32[]{:S(2)}, u32[]{:S(2)}) collective-permute-start(bf16[32,1440]{1,0:T(8,128)(2,1)S(1)} %add_convert_fusion.15), channel_id=1, source_target_pairs={{0,14},{1,15},{2,4},{3,5},{4,2},{5,3},{6,8},{7,9},{8,6},{9,7},{10,... | collective-permute-start | bytes 276488 | tf_op jit(solution)/shard_map/ppermute | solution.py:107
  67.0 4.2 %collective-permute-done.22 = bf16[32,1440]{1,0:T(8,128)(2,1)S(1)} collective-permute-done((bf16[32,1440]{1,0:T(8,128)(2,1)S(1)}, bf16[32,1440]{1,0:T(8,128)(2,1)S(1)}, u32[]{:S(2)}, u32[]{:S(2)}) %collective-permute-start.22) | collective-permute-done | bytes 92192 | tf_op jit(solution)/shard_map/ppermute | solution.py:107
  71.2 1.6 %collective-permute-done.28 = bf16[64,1440]{1,0:T(8,128)(2,1)S(1)} collective-permute-done((bf16[64,1440]{1,0:T(8,128)(2,1)}, bf16[64,1440]{1,0:T(8,128)(2,1)S(1)}, u32[]{:S(2)}, u32[]{:S(2)}) %collective-permute-start.28) | collective-permute-done | bytes 184352 | tf_op jit(solution)/shard_map/ppermute | solution.py:107
  72.9 4.7 %collective-permute-done.30 = bf16[32,1440]{1,0:T(8,128)(2,1)S(1)} collective-permute-done((bf16[32,1440]{1,0:T(8,128)(2,1)S(1)}, bf16[32,1440]{1,0:T(8,128)(2,1)S(1)}, u32[]{:S(2)}, u32[]{:S(2)}) %collective-permute-start.30) | collective-permute-done | bytes 92192 | tf_op jit(solution)/shard_map/ppermute | solution.py:107
  77.6 0.3 collective-permute-start.23
  78.1 5.7 %collective-permute-done.23 = bf16[64,1440]{1,0:T(8,128)(2,1)S(1)} collective-permute-done((bf16[64,1440]{1,0:T(8,128)(2,1)S(1)}, bf16[64,1440]{1,0:T(8,128)(2,1)S(1)}, u32[]{:S(2)}, u32[]{:S(2)}) %collective-permute-start.23) | collective-permute-done | bytes 184352 | tf_op jit(solution)/shard_map/ppermute | solution.py:107
  83.8 2.0 %collective-permute-start.31 = (bf16[64,1440]{1,0:T(8,128)(2,1)S(1)}, bf16[64,1440]{1,0:T(8,128)(2,1)S(1)}, u32[]{:S(2)}, u32[]{:S(2)}) collective-permute-start(bf16[64,1440]{1,0:T(8,128)(2,1)S(1)} %pad_maximum_fusion.1), channel_id=1, source_target_pairs={{0,14},{1,15},{2,4},{3,5},{4,2},{5,3},{6,8},{7,9},{8,6},{9,7},{10,... | collective-permute-start | bytes 552968 | tf_op jit(solution)/shard_map/ppermute | solution.py:107
  85.9 1.3 %collective-permute-start.24 = (bf16[64,1440]{1,0:T(8,128)(2,1)S(1)}, bf16[64,1440]{1,0:T(8,128)(2,1)S(1)}, u32[]{:S(2)}, u32[]{:S(2)}) collective-permute-start(bf16[64,1440]{1,0:T(8,128)(2,1)S(1)} %add_convert_fusion.7), channel_id=1, source_target_pairs={{0,14},{1,15},{2,4},{3,5},{4,2},{5,3},{6,8},{7,9},{8,6},{9,7},{10,... | collective-permute-start | bytes 552968 | tf_op jit(solution)/shard_map/ppermute | solution.py:107
  87.2 5.1 %collective-permute-done.31 = bf16[64,1440]{1,0:T(8,128)(2,1)S(1)} collective-permute-done((bf16[64,1440]{1,0:T(8,128)(2,1)S(1)}, bf16[64,1440]{1,0:T(8,128)(2,1)S(1)}, u32[]{:S(2)}, u32[]{:S(2)}) %collective-permute-start.31) | collective-permute-done | bytes 184352 | tf_op jit(solution)/shard_map/ppermute | solution.py:107
  92.5 1.9 %collective-permute-done.24 = bf16[64,1440]{1,0:T(8,128)(2,1)S(1)} collective-permute-done((bf16[64,1440]{1,0:T(8,128)(2,1)S(1)}, bf16[64,1440]{1,0:T(8,128)(2,1)S(1)}, u32[]{:S(2)}, u32[]{:S(2)}) %collective-permute-start.24) | collective-permute-done | bytes 184352 | tf_op jit(solution)/shard_map/ppermute | solution.py:107
  94.6 4.2 %collective-permute-done.32 = bf16[64,1440]{1,0:T(8,128)(2,1)S(1)} collective-permute-done((bf16[64,1440]{1,0:T(8,128)(2,1)S(1)}, bf16[64,1440]{1,0:T(8,128)(2,1)S(1)}, u32[]{:S(2)}, u32[]{:S(2)}) %collective-permute-start.32) | collective-permute-done | bytes 184352 | tf_op jit(solution)/shard_map/ppermute | solution.py:107
  98.9 2.1 %collective-permute-start.33 = (bf16[64,1440]{1,0:T(8,128)(2,1)S(1)}, bf16[64,1440]{1,0:T(8,128)(2,1)S(1)}, u32[]{:S(2)}, u32[]{:S(2)}) collective-permute-start(bf16[64,1440]{1,0:T(8,128)(2,1)S(1)} %add_convert_fusion.1), channel_id=1, source_target_pairs={{0,14},{1,15},{2,4},{3,5},{4,2},{5,3},{6,8},{7,9},{8,6},{9,7},{10,... | collective-permute-start | bytes 552968 | tf_op jit(solution)/shard_map/ppermute | solution.py:107
  101.0 4.9 %collective-permute-done.33 = bf16[64,1440]{1,0:T(8,128)(2,1)S(1)} collective-permute-done((bf16[64,1440]{1,0:T(8,128)(2,1)S(1)}, bf16[64,1440]{1,0:T(8,128)(2,1)S(1)}, u32[]{:S(2)}, u32[]{:S(2)}) %collective-permute-start.33) | collective-permute-done | bytes 184352 | tf_op jit(solution)/shard_map/ppermute | solution.py:107
  105.9 0.8 add_convert_fusion
  (80 shorter events, 1.5 us)
Async XLA Ops:
  3.4 35.9 %slice-start = ((s8[4423680]{0:T(1024)(128)(4,1)}), s8[229376]{0:T(1024)(128)(4,1)S(1)}, s32[]{:S(2)}) async-start(s8[4423680]{0:T(1024)(128)(4,1)} %bitcast.4), calls=%async_computation | async-start | bytes 458752
  5.2 11.0 %collective-permute-start.3 = (bf16[64,1536]{1,0:T(8,128)(2,1)}, bf16[64,1536]{1,0:T(8,128)(2,1)S(1)}, u32[]{:S(2)}, u32[]{:S(2)}) collective-permute-start(bf16[64,1536]{1,0:T(8,128)(2,1)} %route.1.refs_0_), channel_id=1, source_target_pairs={{0,14},{1,15},{2,4},{3,5},{4,2},{5,3},{6,8},{7,9},{8,6},{9,7},{10,... | collective-permute-start | bytes 589832 | tf_op jit(solution)/shard_map/ppermute | solution.py:107
  11.1 6.6 %collective-permute-start.2 = (bf16[64,1536]{1,0:T(8,128)(2,1)}, bf16[64,1536]{1,0:T(8,128)(2,1)S(1)}, u32[]{:S(2)}, u32[]{:S(2)}) collective-permute-start(bf16[64,1536]{1,0:T(8,128)(2,1)} %route.1.refs_0_), channel_id=1, source_target_pairs={{0,2},{1,3},{2,0},{3,1},{4,6},{5,7},{6,4},{7,5},{8,10},{9,11},{10,... | collective-permute-start | bytes 589832 | tf_op jit(solution)/shard_map/ppermute | solution.py:107
  16.2 6.1 %collective-permute-start.7 = (bf16[64,1536]{1,0:T(8,128)(2,1)S(1)}, bf16[64,1536]{1,0:T(8,128)(2,1)S(1)}, u32[]{:S(2)}, u32[]{:S(2)}) collective-permute-start(bf16[64,1536]{1,0:T(8,128)(2,1)S(1)} %collective-permute-done.3.refs_1_), channel_id=1, source_target_pairs={{0,2},{1,3},{2,0},{3,1},{4,6},{5,7},{6,4},{7,5},{8,10},{9,11},{10,... | collective-permute-start | bytes 589832 | tf_op jit(solution)/shard_map/ppermute | solution.py:107
  17.7 7.3 %collective-permute-start.8 = (bf16[64,1536]{1,0:T(8,128)(2,1)S(1)}, bf16[64,1536]{1,0:T(8,128)(2,1)S(1)}, u32[]{:S(2)}, u32[]{:S(2)}) collective-permute-start(bf16[64,1536]{1,0:T(8,128)(2,1)S(1)} %collective-permute-done.2.refs_0_), channel_id=1, source_target_pairs={{0,14},{1,15},{2,4},{3,5},{4,2},{5,3},{6,8},{7,9},{8,6},{9,7},{10,... | collective-permute-start | bytes 589832 | tf_op jit(solution)/shard_map/ppermute | solution.py:107
  19.2 6.3 %collective-permute-start = (bf16[64,1536]{1,0:T(8,128)(2,1)}, bf16[64,1536]{1,0:T(8,128)(2,1)S(1)}, u32[]{:S(2)}, u32[]{:S(2)}) collective-permute-start(bf16[64,1536]{1,0:T(8,128)(2,1)} %route.1.refs_0_), channel_id=1, source_target_pairs={{0,1},{1,0},{2,3},{3,2},{4,5},{5,4},{6,7},{7,6},{8,9},{9,8},{10,11... | collective-permute-start | bytes 589832 | tf_op jit(solution)/shard_map/ppermute | solution.py:107
  22.3 13.1 %collective-permute-start.13 = (bf16[64,1536]{1,0:T(8,128)(2,1)S(1)}, bf16[64,1536]{1,0:T(8,128)(2,1)S(1)}, u32[]{:S(2)}, u32[]{:S(2)}) collective-permute-start(bf16[64,1536]{1,0:T(8,128)(2,1)S(1)} %collective-permute-done.7.refs_0_), channel_id=1, source_target_pairs={{0,14},{1,15},{2,4},{3,5},{4,2},{5,3},{6,8},{7,9},{8,6},{9,7},{10,... | collective-permute-start | bytes 589832 | tf_op jit(solution)/shard_map/ppermute | solution.py:107
  24.9 10.8 %collective-permute-start.12 = (bf16[64,1536]{1,0:T(8,128)(2,1)S(1)}, bf16[64,1536]{1,0:T(8,128)(2,1)S(1)}, u32[]{:S(2)}, u32[]{:S(2)}) collective-permute-start(bf16[64,1536]{1,0:T(8,128)(2,1)S(1)} %collective-permute-done.8.refs_1_), channel_id=1, source_target_pairs={{0,2},{1,3},{2,0},{3,1},{4,6},{5,7},{6,4},{7,5},{8,10},{9,11},{10,... | collective-permute-start | bytes 589832 | tf_op jit(solution)/shard_map/ppermute | solution.py:107
  24.9 11.0 %collective-permute-start.4 = (bf16[64,1536]{1,0:T(8,128)(2,1)S(1)}, bf16[64,1536]{1,0:T(8,128)(2,1)S(1)}, u32[]{:S(2)}, u32[]{:S(2)}) collective-permute-start(bf16[64,1536]{1,0:T(8,128)(2,1)S(1)} %collective-permute-done.2.refs_0_), channel_id=1, source_target_pairs={{0,1},{1,0},{2,3},{3,2},{4,5},{5,4},{6,7},{7,6},{8,9},{9,8},{10,11... | collective-permute-start | bytes 589832 | tf_op jit(solution)/shard_map/ppermute | solution.py:107
  25.0 13.2 %collective-permute-start.5 = (bf16[64,1536]{1,0:T(8,128)(2,1)S(1)}, bf16[64,1536]{1,0:T(8,128)(2,1)S(1)}, u32[]{:S(2)}, u32[]{:S(2)}) collective-permute-start(bf16[64,1536]{1,0:T(8,128)(2,1)S(1)} %collective-permute-done.3.refs_1_), channel_id=1, source_target_pairs={{0,1},{1,0},{2,3},{3,2},{4,5},{5,4},{6,7},{7,6},{8,9},{9,8},{10,11... | collective-permute-start | bytes 589832 | tf_op jit(solution)/shard_map/ppermute | solution.py:107
  25.5 2.3 %copy-start = (bf16[1,1440,1440]{2,1,0:T(8,128)(2,1)S(1)}, bf16[1,1440,1440]{2,1,0:T(8,128)(2,1)}, u32[]{:S(2)}) copy-start(bf16[1,1440,1440]{2,1,0:T(8,128)(2,1)} %param.11) | copy-start | bytes 12441604
  27.7 2.3 %copy-start.1 = (bf16[1,1440,1440]{2,1,0:T(8,128)(2,1)S(1)}, bf16[1,1440,1440]{2,1,0:T(8,128)(2,1)}, u32[]{:S(2)}) copy-start(bf16[1,1440,1440]{2,1,0:T(8,128)(2,1)} %param.12) | copy-start | bytes 12441604
  33.1 6.2 %slice-start.1 = ((s8[4423680]{0:T(1024)(128)(4,1)}), s8[4194304]{0:T(1024)(128)(4,1)S(1)}, s32[]{:S(2)}) async-start(s8[4423680]{0:T(1024)(128)(4,1)} %bitcast.4), calls=%async_computation.1 | async-start | bytes 8388608
  35.2 65.8 %collective-permute-start.1 = (bf16[64,1440]{1,0:T(8,128)(2,1)S(1)}, bf16[64,1440]{1,0:T(8,128)(2,1)S(1)}, u32[]{:S(2)}, u32[]{:S(2)}) collective-permute-start(bf16[64,1440]{1,0:T(8,128)(2,1)S(1)} %get-tuple-element.24), channel_id=1, source_target_pairs={{0,1},{1,0},{2,3},{3,2},{4,5},{5,4},{6,7},{7,6},{8,9},{9,8},{10,11... | collective-permute-start | bytes 552968 | tf_op jit(solution)/shard_map/ppermute | solution.py:107
  35.4 13.1 %collective-permute-start.10 = (bf16[64,1536]{1,0:T(8,128)(2,1)S(1)}, bf16[64,1536]{1,0:T(8,128)(2,1)S(1)}, u32[]{:S(2)}, u32[]{:S(2)}) collective-permute-start(bf16[64,1536]{1,0:T(8,128)(2,1)S(1)} %collective-permute-done.8.refs_1_), channel_id=1, source_target_pairs={{0,1},{1,0},{2,3},{3,2},{4,5},{5,4},{6,7},{7,6},{8,9},{9,8},{10,11... | collective-permute-start | bytes 589832 | tf_op jit(solution)/shard_map/ppermute | solution.py:107
  35.8 12.7 %collective-permute-start.9 = (bf16[64,1536]{1,0:T(8,128)(2,1)S(1)}, bf16[64,1536]{1,0:T(8,128)(2,1)S(1)}, u32[]{:S(2)}, u32[]{:S(2)}) collective-permute-start(bf16[64,1536]{1,0:T(8,128)(2,1)S(1)} %collective-permute-done.7.refs_0_), channel_id=1, source_target_pairs={{0,1},{1,0},{2,3},{3,2},{4,5},{5,4},{6,7},{7,6},{8,9},{9,8},{10,11... | collective-permute-start | bytes 589832 | tf_op jit(solution)/shard_map/ppermute | solution.py:107
  36.0 13.0 %collective-permute-start.17 = (bf16[32,1536]{1,0:T(8,128)(2,1)S(1)}, bf16[32,1536]{1,0:T(8,128)(2,1)S(1)}, u32[]{:S(2)}, u32[]{:S(2)}) collective-permute-start(bf16[32,1536]{1,0:T(8,128)(2,1)S(1)} %slice.26), channel_id=1, source_target_pairs={{0,2},{1,3},{2,0},{3,1},{4,6},{5,7},{6,4},{7,5},{8,10},{9,11},{10,... | collective-permute-start | bytes 294920 | tf_op jit(solution)/shard_map/ppermute | solution.py:107
  38.1 11.0 %collective-permute-start.18 = (bf16[32,1536]{1,0:T(8,128)(2,1)S(1)}, bf16[32,1536]{1,0:T(8,128)(2,1)S(1)}, u32[]{:S(2)}, u32[]{:S(2)}) collective-permute-start(bf16[32,1536]{1,0:T(8,128)(2,1)S(1)} %slice.27), channel_id=1, source_target_pairs={{0,14},{1,15},{2,4},{3,5},{4,2},{5,3},{6,8},{7,9},{8,6},{9,7},{10,... | collective-permute-start | bytes 294920 | tf_op jit(solution)/shard_map/ppermute | solution.py:107
  39.3 2.3 %copy-start.2 = (bf16[1,1440,1440]{2,1,0:T(8,128)(2,1)S(1)}, bf16[1,1440,1440]{2,1,0:T(8,128)(2,1)}, u32[]{:S(2)}) copy-start(bf16[1,1440,1440]{2,1,0:T(8,128)(2,1)} %param.12) | copy-start | bytes 12441604
  41.6 2.3 %copy-start.4 = (bf16[1,1440,1440]{2,1,0:T(8,128)(2,1)S(1)}, bf16[1,1440,1440]{2,1,0:T(8,128)(2,1)}, u32[]{:S(2)}) copy-start(bf16[1,1440,1440]{2,1,0:T(8,128)(2,1)} %param.13) | copy-start | bytes 12441604
  43.8 10.9 %slice-start.4 = ((s8[4423680]{0:T(1024)(128)(4,1)}), s8[4194304]{0:T(1024)(128)(4,1)S(1)}, s32[]{:S(2)}) async-start(s8[4423680]{0:T(1024)(128)(4,1)} %bitcast.20), calls=%async_computation.4 | async-start | bytes 8388608
  48.4 5.7 %copy-start.7 = (bf16[64,1440]{1,0:T(8,128)(2,1)S(1)}, bf16[64,1440]{1,0:T(8,128)(2,1)}, u32[]{:S(2)}) copy-start(bf16[64,1440]{1,0:T(8,128)(2,1)} %get-tuple-element.26) | copy-start | bytes 552964
  48.4 5.8 %copy-start.6 = (bf16[64,1440]{1,0:T(8,128)(2,1)S(1)}, bf16[64,1440]{1,0:T(8,128)(2,1)}, u32[]{:S(2)}) copy-start(bf16[64,1440]{1,0:T(8,128)(2,1)} %get-tuple-element.34) | copy-start | bytes 552964
  48.4 6.3 %slice-start.5 = ((s8[4423680]{0:T(1024)(128)(4,1)}), s8[229376]{0:T(1024)(128)(4,1)S(1)}, s32[]{:S(2)}) async-start(s8[4423680]{0:T(1024)(128)(4,1)} %bitcast.20), calls=%async_computation.5 | async-start | bytes 458752
  48.4 8.3 %collective-permute-start.14 = (bf16[64,1536]{1,0:T(8,128)(2,1)S(1)}, bf16[64,1536]{1,0:T(8,128)(2,1)S(1)}, u32[]{:S(2)}, u32[]{:S(2)}) collective-permute-start(bf16[64,1536]{1,0:T(8,128)(2,1)S(1)} %collective-permute-done.12.refs_0_), channel_id=1, source_target_pairs={{0,1},{1,0},{2,3},{3,2},{4,5},{5,4},{6,7},{7,6},{8,9},{9,8},{10,11... | collective-permute-start | bytes 589832 | tf_op jit(solution)/shard_map/ppermute | solution.py:107
  48.5 8.4 %collective-permute-start.15 = (bf16[64,1536]{1,0:T(8,128)(2,1)S(1)}, bf16[64,1536]{1,0:T(8,128)(2,1)S(1)}, u32[]{:S(2)}, u32[]{:S(2)}) collective-permute-start(bf16[64,1536]{1,0:T(8,128)(2,1)S(1)} %collective-permute-done.13.refs_1_), channel_id=1, source_target_pairs={{0,1},{1,0},{2,3},{3,2},{4,5},{5,4},{6,7},{7,6},{8,9},{9,8},{10,11... | collective-permute-start | bytes 589832 | tf_op jit(solution)/shard_map/ppermute | solution.py:107
  49.0 5.1 %collective-permute-start.19 = (bf16[32,1536]{1,0:T(8,128)(2,1)S(1)}, bf16[32,1536]{1,0:T(8,128)(2,1)S(1)}, u32[]{:S(2)}, u32[]{:S(2)}) collective-permute-start(bf16[32,1536]{1,0:T(8,128)(2,1)S(1)} %collective-permute-done.17.refs_0_), channel_id=1, source_target_pairs={{0,1},{1,0},{2,3},{3,2},{4,5},{5,4},{6,7},{7,6},{8,9},{9,8},{10,11... | collective-permute-start | bytes 294920 | tf_op jit(solution)/shard_map/ppermute | solution.py:107
  49.1 5.1 %collective-permute-start.20 = (bf16[32,1536]{1,0:T(8,128)(2,1)S(1)}, bf16[32,1536]{1,0:T(8,128)(2,1)S(1)}, u32[]{:S(2)}, u32[]{:S(2)}) collective-permute-start(bf16[32,1536]{1,0:T(8,128)(2,1)S(1)} %collective-permute-done.18.refs_1_), channel_id=1, source_target_pairs={{0,1},{1,0},{2,3},{3,2},{4,5},{5,4},{6,7},{7,6},{8,9},{9,8},{10,11... | collective-permute-start | bytes 294920 | tf_op jit(solution)/shard_map/ppermute | solution.py:107
  54.1 38.3 %collective-permute-start.6 = (bf16[64,1440]{1,0:T(8,128)(2,1)S(1)}, bf16[64,1440]{1,0:T(8,128)(2,1)S(1)}, u32[]{:S(2)}, u32[]{:S(2)}) collective-permute-start(bf16[64,1440]{1,0:T(8,128)(2,1)S(1)} %copy-done.7), channel_id=1, source_target_pairs={{0,1},{1,0},{2,3},{3,2},{4,5},{5,4},{6,7},{7,6},{8,9},{9,8},{10,11... | collective-permute-start | bytes 552968 | tf_op jit(solution)/shard_map/ppermute | solution.py:107
  54.2 3.2 %slice-start.2 = ((s8[4423680]{0:T(1024)(128)(4,1)}), s8[4194304]{0:T(1024)(128)(4,1)S(1)}, s32[]{:S(2)}) async-start(s8[4423680]{0:T(1024)(128)(4,1)} %bitcast.14), calls=%async_computation.2 | async-start | bytes 8388608
  54.2 2.6 %copy-start.9 = (bf16[64,1440]{1,0:T(8,128)(2,1)S(1)}, bf16[64,1440]{1,0:T(8,128)(2,1)}, u32[]{:S(2)}) copy-start(bf16[64,1440]{1,0:T(8,128)(2,1)} %get-tuple-element.28) | copy-start | bytes 552964
  54.2 3.2 %slice-start.3 = ((s8[4423680]{0:T(1024)(128)(4,1)}), s8[229376]{0:T(1024)(128)(4,1)S(1)}, s32[]{:S(2)}) async-start(s8[4423680]{0:T(1024)(128)(4,1)} %bitcast.14), calls=%async_computation.3 | async-start | bytes 458752
  54.2 40.4 %collective-permute-start.26 = (bf16[64,1440]{1,0:T(8,128)(2,1)S(1)}, bf16[64,1440]{1,0:T(8,128)(2,1)S(1)}, u32[]{:S(2)}, u32[]{:S(2)}) collective-permute-start(bf16[64,1440]{1,0:T(8,128)(2,1)S(1)} %copy-done.6), channel_id=1, source_target_pairs={{0,1},{1,0},{2,3},{3,2},{4,5},{5,4},{6,7},{7,6},{8,9},{9,8},{10,11... | collective-permute-start | bytes 552968 | tf_op jit(solution)/shard_map/ppermute | solution.py:107
  56.8 21.2 %collective-permute-start.11 = (bf16[64,1440]{1,0:T(8,128)(2,1)S(1)}, bf16[64,1440]{1,0:T(8,128)(2,1)S(1)}, u32[]{:S(2)}, u32[]{:S(2)}) collective-permute-start(bf16[64,1440]{1,0:T(8,128)(2,1)S(1)} %copy-done.9), channel_id=1, source_target_pairs={{0,1},{1,0},{2,3},{3,2},{4,5},{5,4},{6,7},{7,6},{8,9},{9,8},{10,11... | collective-permute-start | bytes 552968 | tf_op jit(solution)/shard_map/ppermute | solution.py:107
  57.0 21.0 %copy-start.8 = (bf16[64,1440]{1,0:T(8,128)(2,1)S(1)}, bf16[64,1440]{1,0:T(8,128)(2,1)}, u32[]{:S(2)}) copy-start(bf16[64,1440]{1,0:T(8,128)(2,1)} %get-tuple-element.36) | copy-start | bytes 552964
  57.0 5.0 %collective-permute-start.21 = (bf16[32,1440]{1,0:T(8,128)(2,1)S(1)}, bf16[32,1440]{1,0:T(8,128)(2,1)S(1)}, u32[]{:S(2)}, u32[]{:S(2)}) collective-permute-start(bf16[32,1440]{1,0:T(8,128)(2,1)S(1)} %get-tuple-element.32), channel_id=1, source_target_pairs={{0,1},{1,0},{2,3},{3,2},{4,5},{5,4},{6,7},{7,6},{8,9},{9,8},{10,11... | collective-permute-start | bytes 276488 | tf_op jit(solution)/shard_map/ppermute | solution.py:107
  61.9 1.3 %collective-permute-start.29 = (bf16[32,1440]{1,0:T(8,128)(2,1)S(1)}, bf16[32,1440]{1,0:T(8,128)(2,1)S(1)}, u32[]{:S(2)}, u32[]{:S(2)}) collective-permute-start(bf16[32,1440]{1,0:T(8,128)(2,1)S(1)} %get-tuple-element.40), channel_id=1, source_target_pairs={{0,1},{1,0},{2,3},{3,2},{4,5},{5,4},{6,7},{7,6},{8,9},{9,8},{10,11... | collective-permute-start | bytes 276488 | tf_op jit(solution)/shard_map/ppermute | solution.py:107
  63.2 1.7 %collective-permute-start.16 = (bf16[64,1440]{1,0:T(8,128)(2,1)}, bf16[64,1440]{1,0:T(8,128)(2,1)S(1)}, u32[]{:S(2)}, u32[]{:S(2)}) collective-permute-start(bf16[64,1440]{1,0:T(8,128)(2,1)} %get-tuple-element.30), channel_id=1, source_target_pairs={{0,1},{1,0},{2,3},{3,2},{4,5},{5,4},{6,7},{7,6},{8,9},{9,8},{10,11... | collective-permute-start | bytes 552968 | tf_op jit(solution)/shard_map/ppermute | solution.py:107
  64.9 6.2 %collective-permute-start.22 = (bf16[32,1440]{1,0:T(8,128)(2,1)S(1)}, bf16[32,1440]{1,0:T(8,128)(2,1)S(1)}, u32[]{:S(2)}, u32[]{:S(2)}) collective-permute-start(bf16[32,1440]{1,0:T(8,128)(2,1)S(1)} %add_convert_fusion.15), channel_id=1, source_target_pairs={{0,14},{1,15},{2,4},{3,5},{4,2},{5,3},{6,8},{7,9},{8,6},{9,7},{10,... | collective-permute-start | bytes 276488 | tf_op jit(solution)/shard_map/ppermute | solution.py:107
  71.1 1.7 %collective-permute-start.28 = (bf16[64,1440]{1,0:T(8,128)(2,1)}, bf16[64,1440]{1,0:T(8,128)(2,1)S(1)}, u32[]{:S(2)}, u32[]{:S(2)}) collective-permute-start(bf16[64,1440]{1,0:T(8,128)(2,1)} %get-tuple-element.38), channel_id=1, source_target_pairs={{0,1},{1,0},{2,3},{3,2},{4,5},{5,4},{6,7},{7,6},{8,9},{9,8},{10,11... | collective-permute-start | bytes 552968 | tf_op jit(solution)/shard_map/ppermute | solution.py:107
  72.8 4.8 %collective-permute-start.30 = (bf16[32,1440]{1,0:T(8,128)(2,1)S(1)}, bf16[32,1440]{1,0:T(8,128)(2,1)S(1)}, u32[]{:S(2)}, u32[]{:S(2)}) collective-permute-start(bf16[32,1440]{1,0:T(8,128)(2,1)S(1)} %add_convert_fusion.13), channel_id=1, source_target_pairs={{0,2},{1,3},{2,0},{3,1},{4,6},{5,7},{6,4},{7,5},{8,10},{9,11},{10,... | collective-permute-start | bytes 276488 | tf_op jit(solution)/shard_map/ppermute | solution.py:107
  77.6 6.1 %collective-permute-start.23 = (bf16[64,1440]{1,0:T(8,128)(2,1)S(1)}, bf16[64,1440]{1,0:T(8,128)(2,1)S(1)}, u32[]{:S(2)}, u32[]{:S(2)}) collective-permute-start(bf16[64,1440]{1,0:T(8,128)(2,1)S(1)} %pad_maximum_fusion), channel_id=1, source_target_pairs={{0,2},{1,3},{2,0},{3,1},{4,6},{5,7},{6,4},{7,5},{8,10},{9,11},{10,... | collective-permute-start | bytes 552968 | tf_op jit(solution)/shard_map/ppermute | solution.py:107
  78.0 7.8 %collective-permute-start.27 = (bf16[64,1440]{1,0:T(8,128)(2,1)S(1)}, bf16[64,1440]{1,0:T(8,128)(2,1)S(1)}, u32[]{:S(2)}, u32[]{:S(2)}) collective-permute-start(bf16[64,1440]{1,0:T(8,128)(2,1)S(1)} %copy-done.8), channel_id=1, source_target_pairs={{0,1},{1,0},{2,3},{3,2},{4,5},{5,4},{6,7},{7,6},{8,9},{9,8},{10,11... | collective-permute-start | bytes 552968 | tf_op jit(solution)/shard_map/ppermute | solution.py:107
  83.8 8.5 %collective-permute-start.31 = (bf16[64,1440]{1,0:T(8,128)(2,1)S(1)}, bf16[64,1440]{1,0:T(8,128)(2,1)S(1)}, u32[]{:S(2)}, u32[]{:S(2)}) collective-permute-start(bf16[64,1440]{1,0:T(8,128)(2,1)S(1)} %pad_maximum_fusion.1), channel_id=1, source_target_pairs={{0,14},{1,15},{2,4},{3,5},{4,2},{5,3},{6,8},{7,9},{8,6},{9,7},{10,... | collective-permute-start | bytes 552968 | tf_op jit(solution)/shard_map/ppermute | solution.py:107
  85.9 8.5 %collective-permute-start.24 = (bf16[64,1440]{1,0:T(8,128)(2,1)S(1)}, bf16[64,1440]{1,0:T(8,128)(2,1)S(1)}, u32[]{:S(2)}, u32[]{:S(2)}) collective-permute-start(bf16[64,1440]{1,0:T(8,128)(2,1)S(1)} %add_convert_fusion.7), channel_id=1, source_target_pairs={{0,14},{1,15},{2,4},{3,5},{4,2},{5,3},{6,8},{7,9},{8,6},{9,7},{10,... | collective-permute-start | bytes 552968 | tf_op jit(solution)/shard_map/ppermute | solution.py:107
  92.3 6.5 %collective-permute-start.32 = (bf16[64,1440]{1,0:T(8,128)(2,1)S(1)}, bf16[64,1440]{1,0:T(8,128)(2,1)S(1)}, u32[]{:S(2)}, u32[]{:S(2)}) collective-permute-start(bf16[64,1440]{1,0:T(8,128)(2,1)S(1)} %add_convert_fusion.2), channel_id=1, source_target_pairs={{0,2},{1,3},{2,0},{3,1},{4,6},{5,7},{6,4},{7,5},{8,10},{9,11},{10,... | collective-permute-start | bytes 552968 | tf_op jit(solution)/shard_map/ppermute | solution.py:107
  94.5 6.5 %collective-permute-start.25 = (bf16[64,1440]{1,0:T(8,128)(2,1)S(1)}, bf16[64,1440]{1,0:T(8,128)(2,1)S(1)}, u32[]{:S(2)}, u32[]{:S(2)}) collective-permute-start(bf16[64,1440]{1,0:T(8,128)(2,1)S(1)} %add_convert_fusion.6), channel_id=1, source_target_pairs={{0,2},{1,3},{2,0},{3,1},{4,6},{5,7},{6,4},{7,5},{8,10},{9,11},{10,... | collective-permute-start | bytes 552968 | tf_op jit(solution)/shard_map/ppermute | solution.py:107
  98.9 7.0 %collective-permute-start.33 = (bf16[64,1440]{1,0:T(8,128)(2,1)S(1)}, bf16[64,1440]{1,0:T(8,128)(2,1)S(1)}, u32[]{:S(2)}, u32[]{:S(2)}) collective-permute-start(bf16[64,1440]{1,0:T(8,128)(2,1)S(1)} %add_convert_fusion.1), channel_id=1, source_target_pairs={{0,14},{1,15},{2,4},{3,5},{4,2},{5,3},{6,8},{7,9},{8,6},{9,7},{10,... | collective-permute-start | bytes 552968 | tf_op jit(solution)/shard_map/ppermute | solution.py:107
  (2 other events, 3.2 us)

commit v2 on v1

v2 whole, which is shorter than its diff:
```python
import jax
import jax.numpy as jnp
from jax import lax
from jax.experimental import pallas as pl
from jax.experimental.pallas import tpu as pltpu
from jax.sharding import PartitionSpec as P

LANES = 128
BF16, F32 = jnp.bfloat16, jnp.float32


def pad_up(n, m):
    return -(-n // m) * m


def ring_pairs(n):
    chips = n // 2

    def odd(chip):
        return (chip - 1) % chips if chip % 2 == 0 else (chip + 1) % chips

    swap = [(i, i ^ 1) for i in range(n)]
    even_pairs = [(i, i ^ 2) for i in range(n)]
    odd_pairs = [(i, odd(i // 2) * 2 + i % 2) for i in range(n)]
    return swap, even_pairs, odd_pairs


def route_kernel(experts, count_ref, x_ref, ids_ref, gw_ref, out_ref):
    rows, width = x_ref.shape
    last = width // LANES * LANES
    start = width - last
    column = lax.broadcasted_iota(jnp.int32, (LANES, rows), 0) - start
    expert = column & (experts - 1)
    weight = jnp.zeros((LANES, rows), F32)
    for k in range(ids_ref.shape[0]):
        weight += jnp.where(ids_ref[k : k + 1, :] == expert, gw_ref[k : k + 1, :], 0.0)
    live = lax.broadcasted_iota(jnp.int32, (LANES, rows), 1) < count_ref[0]
    weight = jnp.where(live, weight, 0.0)
    high = weight.astype(BF16).astype(F32)
    middle = (weight - high).astype(BF16).astype(F32)
    low = weight - high - middle
    part = jnp.where(column < experts, high, jnp.where(column < 2 * experts, middle, low))
    part = jnp.where((column >= 0) & (column < 3 * experts), part, 0.0).T
    out_ref[:, :last] = x_ref[:, :last]
    tail = jnp.concatenate([x_ref[:, last:].astype(F32), jnp.zeros((rows, LANES - start), F32)], axis=1)
    lane = lax.broadcasted_iota(jnp.int32, (rows, LANES), 1)
    out_ref[:, last:] = jnp.where(lane < start, tail, part).astype(BF16)


def expert_body(experts, xs, wg, wu, wd, ys, hidden, ready=lambda k: None):
    width, ff = wg.shape
    last = width // LANES * LANES
    start = width - last
    x = jnp.concatenate([r[:, :width] for r in xs], axis=0)
    tail = jnp.concatenate([r[:, last : last + LANES] for r in xs], axis=0).astype(F32)
    lane = lax.broadcasted_iota(jnp.int32, tail.shape, 1) - start
    mine = (lane >= 0) & (lane < 3 * experts) & ((lane & (experts - 1)) == lax.axis_index("ep"))
    weight = jnp.sum(jnp.where(mine, tail, 0.0), axis=1, keepdims=True)
    ready(0)
    for lo in range(0, ff, 256):
        hi = min(lo + 256, ff)
        gate = jnp.dot(x, wg[:, lo:hi], preferred_element_type=F32)
        up = jnp.dot(x, wu[:, lo:hi], preferred_element_type=F32)
        hidden[:, lo:hi] = ((up + 1.0) * gate * jax.nn.sigmoid(1.702 * gate)).astype(BF16)
    ready(1)
    h = hidden[...]
    for lo in range(0, width, 256):
        hi = min(lo + 256, width)
        y = jnp.dot(h, wd[:, lo:hi], preferred_element_type=F32).astype(BF16).astype(F32)
        y = (y * weight).astype(BF16)
        at = 0
        for r in ys:
            r[:, lo:hi] = y[at : at + r.shape[0]]
            at += r.shape[0]


def expert_kernel(experts, count, *refs):
    xs, (wg, wu, wd), ys, hidden = refs[:count], refs[count : count + 3], refs[count + 3 : -1], refs[-1]
    expert_body(experts, xs, wg, wu, wd, ys, hidden)


def first_kernel(experts, count, *refs):
    xs, far, ys = refs[:count], refs[count : count + 3], refs[count + 3 : 2 * count + 3]
    near, hidden, sems = refs[2 * count + 3 : 2 * count + 6], refs[-2], refs[-1]
    copies = [pltpu.make_async_copy(f.at[0], w, sems.at[k]) for k, (f, w) in enumerate(zip(far, near))]
    for c in copies:
        c.start()

    def ready(stage):
        for c in copies[:2] if stage == 0 else copies[2:]:
            c.wait()

    expert_body(experts, xs, *near, ys, hidden, ready)


def experts_apply(experts, blocks, weights):
    first = weights[0].ndim == 3
    width, ff = weights[0].shape[-2:]
    total, count = sum(b.shape[0] for b in blocks), len(blocks)
    vmem = pl.BlockSpec(memory_space=pltpu.VMEM)
    out_shape = [pltpu.VMEM((b.shape[0], width), BF16) for b in blocks]
    scratch = [pltpu.VMEM((total, ff), BF16)]
    if first:
        out_shape += [pltpu.VMEM(w.shape[1:], BF16) for w in weights]
        scratch += [pltpu.SemaphoreType.DMA((3,))]
        weights = [pltpu.with_memory_space_constraint(w, pltpu.HBM) for w in weights]
    else:
        weights = [pltpu.with_memory_space_constraint(w, pltpu.VMEM) for w in weights]
    kernel = first_kernel if first else expert_kernel
    out = pl.pallas_call(
        lambda *refs: kernel(experts, count, *refs),
        out_shape=out_shape,
        in_specs=[vmem] * count + [pl.BlockSpec(memory_space=pltpu.HBM if first else pltpu.VMEM)] * 3,
        out_specs=[vmem] * len(out_shape),
        scratch_shapes=scratch,
        compiler_params=pltpu.CompilerParams(vmem_limit_bytes=16 << 20),
        cost_estimate=pl.CostEstimate(flops=6 * total * width * ff, bytes_accessed=total * width * 4, transcendentals=total * ff),
        name="experts",
    )(*[pltpu.with_memory_space_constraint(b, pltpu.VMEM) for b in blocks], *weights)
    return (out[:count], out[count:]) if first else (out, None)


def add(*terms):
    total = terms[0].astype(F32)
    for t in terms[1:]:
        total = total + t.astype(F32)
    return total.astype(BF16)


def local(tokens, expert_ids, gate_weights, row_counts, w_gate, w_up, w_down):
    n = lax.axis_size("ep")
    rows, width = tokens.shape
    half = rows // 2
    experts = n * w_gate.shape[0]
    swap, even, odd = ring_pairs(n)

    def send(x, pairs):
        return lax.ppermute(x, "ep", pairs)

    def swapped(blocks):
        return [send(b, swap) for b in blocks]

    def chip_sum(out):
        k = len(out) // 2
        return [add(mine, theirs) for mine, theirs in zip(out[:k], swapped(out[k:]))]

    vmem = pl.BlockSpec(memory_space=pltpu.VMEM)
    own = pl.pallas_call(
        lambda *refs: route_kernel(experts, *refs),
        out_shape=pltpu.VMEM((rows, pad_up(width, LANES)), BF16),
        in_specs=[pl.BlockSpec(memory_space=pltpu.SMEM), vmem, vmem, vmem],
        out_specs=vmem,
        name="route",
    )(row_counts, tokens, expert_ids.T, gate_weights.T)

    e, o = send(own, even), send(own, odd)
    out, weights = experts_apply(experts, [own] + swapped([own]), [w_gate, w_up, w_down])
    sums = []
    for step in range(3):
        e, o, out = lax.optimization_barrier((e, o, out))
        if step < 2:
            next_e, next_o = send(o, even), send(e, odd)
        else:
            next_e, next_o = send(o[:half], even), send(e[half:], odd)
        sums.append(chip_sum(out))
        out, _ = experts_apply(experts, [e, o] + swapped([e, o]), weights)
        e, o = next_e, next_o
    e, o, out = lax.optimization_barrier((e, o, out))
    sums.append(chip_sum(out))
    out, _ = experts_apply(experts, [e, o] + swapped([e, o]), weights)
    (t0,), (te1, to1), (te2, to2), (te3, to3) = sums
    te4, to4 = chip_sum(out)
    te4, to4 = lax.optimization_barrier((te4, to4))
    re, ro = send(te4, even), send(to4, odd)
    ao3 = jnp.concatenate([add(to3[:half], re), to3[half:]], axis=0)
    ae3 = jnp.concatenate([te3[:half], add(te3[half:], ro)], axis=0)
    ae3, ao3 = lax.optimization_barrier((ae3, ao3))
    re, ro = send(ae3, even), send(ao3, odd)
    ao2, ae2 = lax.optimization_barrier((add(to2, re), add(te2, ro)))
    re, ro = send(ae2, even), send(ao2, odd)
    ao1, ae1 = lax.optimization_barrier((add(to1, re), add(te1, ro)))
    re, ro = send(ae1, even), send(ao1, odd)
    return add(t0, re, ro)


def solution(mesh):
    rows = P(("grp", "ep"), None)
    in_specs = (rows, rows, rows, P(("grp", "ep"))) + (P("ep", None, None),) * 3
    return jax.shard_map(local, mesh=mesh, in_specs=in_specs, out_specs=rows, check_vma=False)
```

time: 107 us -> 78.2 us (0.73)
  local copies, waits for them, and re-layouts: 15 us -> 0.03 us
  waiting for transfers between devices: 44.2 us -> 30.4 us
    unnamed x34 -> x0, local copies, waits for them, and re-layouts: 15 us -> none
    ppermute x34, waiting for transfers between devices: 44.2 us -> 30.4 us  [send(): return lax.ppermute(x, 'ep', pairs)]
  transfers between devices with their start and end apart: 34 -> 34, of which waited for: 13 -> 17; matrix products, arithmetic and copies ran while one was open for 1% -> 1% of each run, Pallas kernels for 17% -> 25%
where the time goes in v2:
time: 78.2 us; the launch traced here: 78.1 us
  waiting for transfers between devices  30.4 us (39%)
  starting transfers between devices  25.1 us (32%)
  Pallas kernels  20.4 us (26%)
  other arithmetic  1.31 us (2%)
  between operations  0.86 us (1%)
    ppermute x34, waiting for transfers between devices, send(): return lax.ppermute(x, 'ep', pairs)  30.4 us
    ppermute x34, starting transfers between devices, send(): return lax.ppermute(x, 'ep', pairs)  25.1 us
    pallas_call x5, Pallas kernels, experts_apply(): pl.pallas_call(lambda *refs: kernel(experts, count, *refs), out_shape=out...  19.3 us
  transfers between devices with their start and end apart: 34, of which 17 were waited for; matrix products, arithmetic and copies ran while one was open for 1% of the time, Pallas kernels for 25%

profile of v2, /device:TPU:26, one launch (start us, length us, event | category | flops | bytes accessed | tf_op | source)
XLA Modules:
  0.0 78.1 jit_solution(2965717608364851463)
XLA Ops:
  0.7 1.0 %route.1.refs_0_ = bf16[64,1536]{1,0:T(8,128)(2,1)S(1)} custom-call(s32[1]{0:T(128)S(6)} %copy.8.refs_0_, bf16[64,1440]{1,0:T(8,128)(2,1)} %refs_1_.1, s32[4,64]{1,0:T(4,128)} %bitcast.2, f32[4,64]{1,0:T(4,128)} %bitcast.3), custom_call_target="tpu_custom_call" | custom-call | tf_op jit(solution)/shard_map/route/pallas_call | solution.py:148
  1.7 0.1 collective-permute-start.2
  1.8 2.0 %collective-permute-start = (bf16[64,1536]{1,0:T(8,128)(2,1)S(1)}, bf16[64,1536]{1,0:T(8,128)(2,1)S(1)}, u32[]{:S(2)}, u32[]{:S(2)}) collective-permute-start(bf16[64,1536]{1,0:T(8,128)(2,1)S(1)} %route.1.refs_0_), channel_id=1, source_target_pairs={{0,2},{1,3},{2,0},{3,1},{4,6},{5,7},{6,4},{7,5},{8,10},{9,11},{10,... | collective-permute-start | bytes 589832 | tf_op jit(solution)/shard_map/ppermute | solution.py:138
  3.8 4.9 %collective-permute-start.1 = (bf16[64,1536]{1,0:T(8,128)(2,1)S(1)}, bf16[64,1536]{1,0:T(8,128)(2,1)S(1)}, u32[]{:S(2)}, u32[]{:S(2)}) collective-permute-start(bf16[64,1536]{1,0:T(8,128)(2,1)S(1)} %route.1.refs_0_), channel_id=1, source_target_pairs={{0,14},{1,15},{2,4},{3,5},{4,2},{5,3},{6,8},{7,9},{8,6},{9,7},{10,... | collective-permute-start | bytes 589832 | tf_op jit(solution)/shard_map/ppermute | solution.py:138
  8.8 5.8 %experts.5 = (bf16[64,1440]{1,0:T(8,128)(2,1)S(1)}, bf16[64,1440]{1,0:T(8,128)(2,1)S(1)}, bf16[1440,1440]{1,0:T(8,128)(2,1)S(1)}, bf16[1440,1440]{1,0:T(8,128)(2,1)S(1)}, bf16[1440,1440]{1,0:T(8,128)(2,1)S(1)}) custom-call(bf16[64,1536]{1,0:T(8,128)(2,1)S(1)} %route.1.refs_0_, bf16[64,1536]{1,0:T(8,128)(2,1)S(1)} %collective-permute-done.2.refs_1_, ...), custom_call_target="tpu_custom_call" | custom-call | flops 1592524800 | bytes 737280 | tf_op jit(solution)/shard_map/experts/pallas_call | solution.py:110
  14.6 0.1 collective-permute-start.6
  14.7 0.5 collective-permute-start.7
  15.2 2.2 %collective-permute-start.5 = (bf16[64,1536]{1,0:T(8,128)(2,1)S(1)}, bf16[64,1536]{1,0:T(8,128)(2,1)S(1)}, u32[]{:S(2)}, u32[]{:S(2)}) collective-permute-start(bf16[64,1536]{1,0:T(8,128)(2,1)S(1)} %collective-permute-done.refs_0_), channel_id=1, source_target_pairs={{0,14},{1,15},{2,4},{3,5},{4,2},{5,3},{6,8},{7,9},{8,6},{9,7},{10,... | collective-permute-start | bytes 589832 | tf_op jit(solution)/shard_map/ppermute | solution.py:138
  17.4 3.8 %experts.6 = (bf16[64,1440]{1,0:T(8,128)(2,1)S(1)}, bf16[64,1440]{1,0:T(8,128)(2,1)S(1)}, bf16[64,1440]{1,0:T(8,128)(2,1)S(1)}, bf16[64,1440]{1,0:T(8,128)(2,1)S(1)}) custom-call(bf16[64,1536]{1,0:T(8,128)(2,1)S(1)} %collective-permute-done.refs_0_, bf16[64,1536]{1,0:T(8,128)(2,1)S(1)} %collective-permute-done.1.refs_1_, ...), custom_call_target="tpu_custom_call" | custom-call | flops 3185049600 | bytes 1474560 | tf_op jit(solution)/shard_map/experts/pallas_call | solution.py:110
  21.3 0.9 %collective-permute-done.4.refs_0_ = bf16[64,1536]{1,0:T(8,128)(2,1)S(1)} collective-permute-done((bf16[64,1536]{1,0:T(8,128)(2,1)S(1)}, bf16[64,1536]{1,0:T(8,128)(2,1)S(1)}, u32[]{:S(2)}, u32[]{:S(2)}) %collective-permute-start.4) | collective-permute-done | bytes 196640 | tf_op jit(solution)/shard_map/ppermute | solution.py:138
  22.1 1.2 %collective-permute-done.5.refs_1_ = bf16[64,1536]{1,0:T(8,128)(2,1)S(1)} collective-permute-done((bf16[64,1536]{1,0:T(8,128)(2,1)S(1)}, bf16[64,1536]{1,0:T(8,128)(2,1)S(1)}, u32[]{:S(2)}, u32[]{:S(2)}) %collective-permute-start.5) | collective-permute-done | bytes 196640 | tf_op jit(solution)/shard_map/ppermute | solution.py:138
  23.4 0.5 collective-permute-start.12
  23.9 2.1 %collective-permute-start.10 = (bf16[64,1536]{1,0:T(8,128)(2,1)S(1)}, bf16[64,1536]{1,0:T(8,128)(2,1)S(1)}, u32[]{:S(2)}, u32[]{:S(2)}) collective-permute-start(bf16[64,1536]{1,0:T(8,128)(2,1)S(1)} %collective-permute-done.4.refs_0_), channel_id=1, source_target_pairs={{0,14},{1,15},{2,4},{3,5},{4,2},{5,3},{6,8},{7,9},{8,6},{9,7},{10,... | collective-permute-start | bytes 589832 | tf_op jit(solution)/shard_map/ppermute | solution.py:138
  26.0 3.8 %experts.7 = (bf16[64,1440]{1,0:T(8,128)(2,1)S(1)}, bf16[64,1440]{1,0:T(8,128)(2,1)S(1)}, bf16[64,1440]{1,0:T(8,128)(2,1)S(1)}, bf16[64,1440]{1,0:T(8,128)(2,1)S(1)}) custom-call(bf16[64,1536]{1,0:T(8,128)(2,1)S(1)} %collective-permute-done.4.refs_0_, bf16[64,1536]{1,0:T(8,128)(2,1)S(1)} %collective-permute-done.5.refs_1_, ...), custom_call_target="tpu_custom_call" | custom-call | flops 3185049600 | bytes 1474560 | tf_op jit(solution)/shard_map/experts/pallas_call | solution.py:110
  29.8 2.1 %collective-permute-done.10.refs_1_ = bf16[64,1536]{1,0:T(8,128)(2,1)S(1)} collective-permute-done((bf16[64,1536]{1,0:T(8,128)(2,1)S(1)}, bf16[64,1536]{1,0:T(8,128)(2,1)S(1)}, u32[]{:S(2)}, u32[]{:S(2)}) %collective-permute-start.10) | collective-permute-done | bytes 196640 | tf_op jit(solution)/shard_map/ppermute | solution.py:138
  31.9 0.6 collective-permute-done.9.refs_0_
  32.5 0.5 collective-permute-start.17
  33.0 0.4 collective-permute-start.14
  33.4 1.3 %collective-permute-start.15 = (bf16[32,1536]{1,0:T(8,128)(2,1)S(1)}, bf16[32,1536]{1,0:T(8,128)(2,1)S(1)}, u32[]{:S(2)}, u32[]{:S(2)}) collective-permute-start(bf16[32,1536]{1,0:T(8,128)(2,1)S(1)} %slice.19), channel_id=1, source_target_pairs={{0,14},{1,15},{2,4},{3,5},{4,2},{5,3},{6,8},{7,9},{8,6},{9,7},{10,... | collective-permute-start | bytes 294920 | tf_op jit(solution)/shard_map/ppermute | solution.py:138
  34.7 3.8 %experts.8 = (bf16[64,1440]{1,0:T(8,128)(2,1)S(1)}, bf16[64,1440]{1,0:T(8,128)(2,1)S(1)}, bf16[64,1440]{1,0:T(8,128)(2,1)S(1)}, bf16[64,1440]{1,0:T(8,128)(2,1)S(1)}) custom-call(bf16[64,1536]{1,0:T(8,128)(2,1)S(1)} %collective-permute-done.9.refs_0_, bf16[64,1536]{1,0:T(8,128)(2,1)S(1)} %collective-permute-done.10.refs_1_, ...), custom_call_target="tpu_custom_call" | custom-call | flops 3185049600 | bytes 1474560 | tf_op jit(solution)/shard_map/experts/pallas_call | solution.py:110
  38.5 0.7 collective-permute-done.15.refs_1_
  39.2 0.5 collective-permute-start.20
  39.7 0.5 collective-permute-start.27
  40.2 0.3 collective-permute-done.19.refs_2_
  40.5 0.2 collective-permute-done.20.refs_3_
  40.7 2.0 %experts.9 = (bf16[32,1440]{1,0:T(8,128)(2,1)S(1)}, bf16[32,1440]{1,0:T(8,128)(2,1)S(1)}, bf16[32,1440]{1,0:T(8,128)(2,1)S(1)}, bf16[32,1440]{1,0:T(8,128)(2,1)S(1)}) custom-call(bf16[32,1536]{1,0:T(8,128)(2,1)S(1)} %collective-permute-done.14.refs_0_, bf16[32,1536]{1,0:T(8,128)(2,1)S(1)} %collective-permute-done.15.refs_1_, ...), custom_call_target="tpu_custom_call" | custom-call | flops 1592524800 | bytes 737280 | tf_op jit(solution)/shard_map/experts/pallas_call | solution.py:110
  42.7 0.4 collective-permute-start.22
  43.1 0.2 collective-permute-start.21
  43.4 0.7 collective-permute-done.22
  44.1 0.3 collective-permute-done.21
  44.5 1.0 %collective-permute-start.25 = (bf16[32,1440]{1,0:T(8,128)(2,1)S(1)}, bf16[32,1440]{1,0:T(8,128)(2,1)S(1)}, u32[]{:S(2)}, u32[]{:S(2)}) collective-permute-start(bf16[32,1440]{1,0:T(8,128)(2,1)S(1)} %add_convert_fusion.15), channel_id=1, source_target_pairs={{0,2},{1,3},{2,0},{3,1},{4,6},{5,7},{6,4},{7,5},{8,10},{9,11},{10,... | collective-permute-start | bytes 276488 | tf_op jit(solution)/shard_map/ppermute | solution.py:138
  45.5 1.6 %collective-permute-start.23 = (bf16[32,1440]{1,0:T(8,128)(2,1)S(1)}, bf16[32,1440]{1,0:T(8,128)(2,1)S(1)}, u32[]{:S(2)}, u32[]{:S(2)}) collective-permute-start(bf16[32,1440]{1,0:T(8,128)(2,1)S(1)} %add_convert_fusion.14), channel_id=1, source_target_pairs={{0,14},{1,15},{2,4},{3,5},{4,2},{5,3},{6,8},{7,9},{8,6},{9,7},{10,... | collective-permute-start | bytes 276488 | tf_op jit(solution)/shard_map/ppermute | solution.py:138
  47.1 2.3 %collective-permute-done.25 = bf16[32,1440]{1,0:T(8,128)(2,1)S(1)} collective-permute-done((bf16[32,1440]{1,0:T(8,128)(2,1)S(1)}, bf16[32,1440]{1,0:T(8,128)(2,1)S(1)}, u32[]{:S(2)}, u32[]{:S(2)}) %collective-permute-start.25) | collective-permute-done | bytes 92192 | tf_op jit(solution)/shard_map/ppermute | solution.py:138
  49.5 2.0 %collective-permute-done.23 = bf16[32,1440]{1,0:T(8,128)(2,1)S(1)} collective-permute-done((bf16[32,1440]{1,0:T(8,128)(2,1)S(1)}, bf16[32,1440]{1,0:T(8,128)(2,1)S(1)}, u32[]{:S(2)}, u32[]{:S(2)}) %collective-permute-start.23) | collective-permute-done | bytes 92192 | tf_op jit(solution)/shard_map/ppermute | solution.py:138
  51.5 1.6 %collective-permute-start.28 = (bf16[64,1440]{1,0:T(8,128)(2,1)S(1)}, bf16[64,1440]{1,0:T(8,128)(2,1)S(1)}, u32[]{:S(2)}, u32[]{:S(2)}) collective-permute-start(bf16[64,1440]{1,0:T(8,128)(2,1)S(1)} %pad_maximum_fusion.1), channel_id=1, source_target_pairs={{0,14},{1,15},{2,4},{3,5},{4,2},{5,3},{6,8},{7,9},{8,6},{9,7},{10,... | collective-permute-start | bytes 552968 | tf_op jit(solution)/shard_map/ppermute | solution.py:138
  53.1 0.5 collective-permute-start.13
  53.6 4.9 %collective-permute-done.28 = bf16[64,1440]{1,0:T(8,128)(2,1)S(1)} collective-permute-done((bf16[64,1440]{1,0:T(8,128)(2,1)S(1)}, bf16[64,1440]{1,0:T(8,128)(2,1)S(1)}, u32[]{:S(2)}, u32[]{:S(2)}) %collective-permute-start.28) | collective-permute-done | bytes 184352 | tf_op jit(solution)/shard_map/ppermute | solution.py:138
  58.5 1.8 %collective-permute-done.26 = bf16[64,1440]{1,0:T(8,128)(2,1)S(1)} collective-permute-done((bf16[64,1440]{1,0:T(8,128)(2,1)S(1)}, bf16[64,1440]{1,0:T(8,128)(2,1)S(1)}, u32[]{:S(2)}, u32[]{:S(2)}) %collective-permute-start.26) | collective-permute-done | bytes 184352 | tf_op jit(solution)/shard_map/ppermute | solution.py:138
  60.5 1.8 %collective-permute-start.31 = (bf16[64,1440]{1,0:T(8,128)(2,1)S(1)}, bf16[64,1440]{1,0:T(8,128)(2,1)S(1)}, u32[]{:S(2)}, u32[]{:S(2)}) collective-permute-start(bf16[64,1440]{1,0:T(8,128)(2,1)S(1)} %add_convert_fusion.6), channel_id=1, source_target_pairs={{0,14},{1,15},{2,4},{3,5},{4,2},{5,3},{6,8},{7,9},{8,6},{9,7},{10,... | collective-permute-start | bytes 552968 | tf_op jit(solution)/shard_map/ppermute | solution.py:138
  62.3 0.5 collective-permute-start.8
  62.8 4.9 %collective-permute-done.31 = bf16[64,1440]{1,0:T(8,128)(2,1)S(1)} collective-permute-done((bf16[64,1440]{1,0:T(8,128)(2,1)S(1)}, bf16[64,1440]{1,0:T(8,128)(2,1)S(1)}, u32[]{:S(2)}, u32[]{:S(2)}) %collective-permute-start.31) | collective-permute-done | bytes 184352 | tf_op jit(solution)/shard_map/ppermute | solution.py:138
  67.8 1.8 %collective-permute-done.29 = bf16[64,1440]{1,0:T(8,128)(2,1)S(1)} collective-permute-done((bf16[64,1440]{1,0:T(8,128)(2,1)S(1)}, bf16[64,1440]{1,0:T(8,128)(2,1)S(1)}, u32[]{:S(2)}, u32[]{:S(2)}) %collective-permute-start.29) | collective-permute-done | bytes 184352 | tf_op jit(solution)/shard_map/ppermute | solution.py:138
  69.6 0.1 add_convert_fusion.3
  69.7 0.4 collective-permute-start.32
  70.1 1.5 %collective-permute-start.33 = (bf16[64,1440]{1,0:T(8,128)(2,1)S(1)}, bf16[64,1440]{1,0:T(8,128)(2,1)S(1)}, u32[]{:S(2)}, u32[]{:S(2)}) collective-permute-start(bf16[64,1440]{1,0:T(8,128)(2,1)S(1)} %add_convert_fusion.3), channel_id=1, source_target_pairs={{0,14},{1,15},{2,4},{3,5},{4,2},{5,3},{6,8},{7,9},{8,6},{9,7},{10,... | collective-permute-start | bytes 552968 | tf_op jit(solution)/shard_map/ppermute | solution.py:138
  71.6 4.2 %collective-permute-done.32 = bf16[64,1440]{1,0:T(8,128)(2,1)S(1)} collective-permute-done((bf16[64,1440]{1,0:T(8,128)(2,1)S(1)}, bf16[64,1440]{1,0:T(8,128)(2,1)S(1)}, u32[]{:S(2)}, u32[]{:S(2)}) %collective-permute-start.32) | collective-permute-done | bytes 184352 | tf_op jit(solution)/shard_map/ppermute | solution.py:138
  75.7 1.5 %collective-permute-done.33 = bf16[64,1440]{1,0:T(8,128)(2,1)S(1)} collective-permute-done((bf16[64,1440]{1,0:T(8,128)(2,1)S(1)}, bf16[64,1440]{1,0:T(8,128)(2,1)S(1)}, u32[]{:S(2)}, u32[]{:S(2)}) %collective-permute-start.33) | collective-permute-done | bytes 184352 | tf_op jit(solution)/shard_map/ppermute | solution.py:138
  77.3 0.8 add_convert_fusion
  (43 shorter events, 0.6 us)
Async XLA Ops:
  1.7 7.1 %collective-permute-start.2 = (bf16[64,1536]{1,0:T(8,128)(2,1)S(1)}, bf16[64,1536]{1,0:T(8,128)(2,1)S(1)}, u32[]{:S(2)}, u32[]{:S(2)}) collective-permute-start(bf16[64,1536]{1,0:T(8,128)(2,1)S(1)} %route.1.refs_0_), channel_id=1, source_target_pairs={{0,1},{1,0},{2,3},{3,2},{4,5},{5,4},{6,7},{7,6},{8,9},{9,8},{10,11... | collective-permute-start | bytes 589832 | tf_op jit(solution)/shard_map/ppermute | solution.py:138
  1.8 12.8 %collective-permute-start = (bf16[64,1536]{1,0:T(8,128)(2,1)S(1)}, bf16[64,1536]{1,0:T(8,128)(2,1)S(1)}, u32[]{:S(2)}, u32[]{:S(2)}) collective-permute-start(bf16[64,1536]{1,0:T(8,128)(2,1)S(1)} %route.1.refs_0_), channel_id=1, source_target_pairs={{0,2},{1,3},{2,0},{3,1},{4,6},{5,7},{6,4},{7,5},{8,10},{9,11},{10,... | collective-permute-start | bytes 589832 | tf_op jit(solution)/shard_map/ppermute | solution.py:138
  3.8 10.8 %collective-permute-start.1 = (bf16[64,1536]{1,0:T(8,128)(2,1)S(1)}, bf16[64,1536]{1,0:T(8,128)(2,1)S(1)}, u32[]{:S(2)}, u32[]{:S(2)}) collective-permute-start(bf16[64,1536]{1,0:T(8,128)(2,1)S(1)} %route.1.refs_0_), channel_id=1, source_target_pairs={{0,14},{1,15},{2,4},{3,5},{4,2},{5,3},{6,8},{7,9},{8,6},{9,7},{10,... | collective-permute-start | bytes 589832 | tf_op jit(solution)/shard_map/ppermute | solution.py:138
  14.6 2.8 %collective-permute-start.6 = (bf16[64,1536]{1,0:T(8,128)(2,1)S(1)}, bf16[64,1536]{1,0:T(8,128)(2,1)S(1)}, u32[]{:S(2)}, u32[]{:S(2)}) collective-permute-start(bf16[64,1536]{1,0:T(8,128)(2,1)S(1)} %collective-permute-done.refs_0_), channel_id=1, source_target_pairs={{0,1},{1,0},{2,3},{3,2},{4,5},{5,4},{6,7},{7,6},{8,9},{9,8},{10,11... | collective-permute-start | bytes 589832 | tf_op jit(solution)/shard_map/ppermute | solution.py:138
  14.7 2.7 %collective-permute-start.7 = (bf16[64,1536]{1,0:T(8,128)(2,1)S(1)}, bf16[64,1536]{1,0:T(8,128)(2,1)S(1)}, u32[]{:S(2)}, u32[]{:S(2)}) collective-permute-start(bf16[64,1536]{1,0:T(8,128)(2,1)S(1)} %collective-permute-done.1.refs_1_), channel_id=1, source_target_pairs={{0,1},{1,0},{2,3},{3,2},{4,5},{5,4},{6,7},{7,6},{8,9},{9,8},{10,11... | collective-permute-start | bytes 589832 | tf_op jit(solution)/shard_map/ppermute | solution.py:138
  15.2 6.9 %collective-permute-start.4 = (bf16[64,1536]{1,0:T(8,128)(2,1)S(1)}, bf16[64,1536]{1,0:T(8,128)(2,1)S(1)}, u32[]{:S(2)}, u32[]{:S(2)}) collective-permute-start(bf16[64,1536]{1,0:T(8,128)(2,1)S(1)} %collective-permute-done.1.refs_1_), channel_id=1, source_target_pairs={{0,2},{1,3},{2,0},{3,1},{4,6},{5,7},{6,4},{7,5},{8,10},{9,11},{10,... | collective-permute-start | bytes 589832 | tf_op jit(solution)/shard_map/ppermute | solution.py:138
  15.2 8.1 %collective-permute-start.5 = (bf16[64,1536]{1,0:T(8,128)(2,1)S(1)}, bf16[64,1536]{1,0:T(8,128)(2,1)S(1)}, u32[]{:S(2)}, u32[]{:S(2)}) collective-permute-start(bf16[64,1536]{1,0:T(8,128)(2,1)S(1)} %collective-permute-done.refs_0_), channel_id=1, source_target_pairs={{0,14},{1,15},{2,4},{3,5},{4,2},{5,3},{6,8},{7,9},{8,6},{9,7},{10,... | collective-permute-start | bytes 589832 | tf_op jit(solution)/shard_map/ppermute | solution.py:138
  23.3 2.6 %collective-permute-start.11 = (bf16[64,1536]{1,0:T(8,128)(2,1)S(1)}, bf16[64,1536]{1,0:T(8,128)(2,1)S(1)}, u32[]{:S(2)}, u32[]{:S(2)}) collective-permute-start(bf16[64,1536]{1,0:T(8,128)(2,1)S(1)} %collective-permute-done.4.refs_0_), channel_id=1, source_target_pairs={{0,1},{1,0},{2,3},{3,2},{4,5},{5,4},{6,7},{7,6},{8,9},{9,8},{10,11... | collective-permute-start | bytes 589832 | tf_op jit(solution)/shard_map/ppermute | solution.py:138
  23.4 2.6 %collective-permute-start.12 = (bf16[64,1536]{1,0:T(8,128)(2,1)S(1)}, bf16[64,1536]{1,0:T(8,128)(2,1)S(1)}, u32[]{:S(2)}, u32[]{:S(2)}) collective-permute-start(bf16[64,1536]{1,0:T(8,128)(2,1)S(1)} %collective-permute-done.5.refs_1_), channel_id=1, source_target_pairs={{0,1},{1,0},{2,3},{3,2},{4,5},{5,4},{6,7},{7,6},{8,9},{9,8},{10,11... | collective-permute-start | bytes 589832 | tf_op jit(solution)/shard_map/ppermute | solution.py:138
  23.9 8.0 %collective-permute-start.10 = (bf16[64,1536]{1,0:T(8,128)(2,1)S(1)}, bf16[64,1536]{1,0:T(8,128)(2,1)S(1)}, u32[]{:S(2)}, u32[]{:S(2)}) collective-permute-start(bf16[64,1536]{1,0:T(8,128)(2,1)S(1)} %collective-permute-done.4.refs_0_), channel_id=1, source_target_pairs={{0,14},{1,15},{2,4},{3,5},{4,2},{5,3},{6,8},{7,9},{8,6},{9,7},{10,... | collective-permute-start | bytes 589832 | tf_op jit(solution)/shard_map/ppermute | solution.py:138
  26.0 6.5 %collective-permute-start.9 = (bf16[64,1536]{1,0:T(8,128)(2,1)S(1)}, bf16[64,1536]{1,0:T(8,128)(2,1)S(1)}, u32[]{:S(2)}, u32[]{:S(2)}) collective-permute-start(bf16[64,1536]{1,0:T(8,128)(2,1)S(1)} %collective-permute-done.5.refs_1_), channel_id=1, source_target_pairs={{0,2},{1,3},{2,0},{3,1},{4,6},{5,7},{6,4},{7,5},{8,10},{9,11},{10,... | collective-permute-start | bytes 589832 | tf_op jit(solution)/shard_map/ppermute | solution.py:138
  32.5 2.2 %collective-permute-start.16 = (bf16[64,1536]{1,0:T(8,128)(2,1)S(1)}, bf16[64,1536]{1,0:T(8,128)(2,1)S(1)}, u32[]{:S(2)}, u32[]{:S(2)}) collective-permute-start(bf16[64,1536]{1,0:T(8,128)(2,1)S(1)} %collective-permute-done.9.refs_0_), channel_id=1, source_target_pairs={{0,1},{1,0},{2,3},{3,2},{4,5},{5,4},{6,7},{7,6},{8,9},{9,8},{10,11... | collective-permute-start | bytes 589832 | tf_op jit(solution)/shard_map/ppermute | solution.py:138
  32.5 2.2 %collective-permute-start.17 = (bf16[64,1536]{1,0:T(8,128)(2,1)S(1)}, bf16[64,1536]{1,0:T(8,128)(2,1)S(1)}, u32[]{:S(2)}, u32[]{:S(2)}) collective-permute-start(bf16[64,1536]{1,0:T(8,128)(2,1)S(1)} %collective-permute-done.10.refs_1_), channel_id=1, source_target_pairs={{0,1},{1,0},{2,3},{3,2},{4,5},{5,4},{6,7},{7,6},{8,9},{9,8},{10,11... | collective-permute-start | bytes 589832 | tf_op jit(solution)/shard_map/ppermute | solution.py:138
  33.0 5.5 %collective-permute-start.14 = (bf16[32,1536]{1,0:T(8,128)(2,1)S(1)}, bf16[32,1536]{1,0:T(8,128)(2,1)S(1)}, u32[]{:S(2)}, u32[]{:S(2)}) collective-permute-start(bf16[32,1536]{1,0:T(8,128)(2,1)S(1)} %slice.18), channel_id=1, source_target_pairs={{0,2},{1,3},{2,0},{3,1},{4,6},{5,7},{6,4},{7,5},{8,10},{9,11},{10,... | collective-permute-start | bytes 294920 | tf_op jit(solution)/shard_map/ppermute | solution.py:138
  33.4 5.8 %collective-permute-start.15 = (bf16[32,1536]{1,0:T(8,128)(2,1)S(1)}, bf16[32,1536]{1,0:T(8,128)(2,1)S(1)}, u32[]{:S(2)}, u32[]{:S(2)}) collective-permute-start(bf16[32,1536]{1,0:T(8,128)(2,1)S(1)} %slice.19), channel_id=1, source_target_pairs={{0,14},{1,15},{2,4},{3,5},{4,2},{5,3},{6,8},{7,9},{8,6},{9,7},{10,... | collective-permute-start | bytes 294920 | tf_op jit(solution)/shard_map/ppermute | solution.py:138
  39.2 1.3 %collective-permute-start.19 = (bf16[32,1536]{1,0:T(8,128)(2,1)S(1)}, bf16[32,1536]{1,0:T(8,128)(2,1)S(1)}, u32[]{:S(2)}, u32[]{:S(2)}) collective-permute-start(bf16[32,1536]{1,0:T(8,128)(2,1)S(1)} %collective-permute-done.14.refs_0_), channel_id=1, source_target_pairs={{0,1},{1,0},{2,3},{3,2},{4,5},{5,4},{6,7},{7,6},{8,9},{9,8},{10,11... | collective-permute-start | bytes 294920 | tf_op jit(solution)/shard_map/ppermute | solution.py:138
  39.2 1.5 %collective-permute-start.20 = (bf16[32,1536]{1,0:T(8,128)(2,1)S(1)}, bf16[32,1536]{1,0:T(8,128)(2,1)S(1)}, u32[]{:S(2)}, u32[]{:S(2)}) collective-permute-start(bf16[32,1536]{1,0:T(8,128)(2,1)S(1)} %collective-permute-done.15.refs_1_), channel_id=1, source_target_pairs={{0,1},{1,0},{2,3},{3,2},{4,5},{5,4},{6,7},{7,6},{8,9},{9,8},{10,11... | collective-permute-start | bytes 294920 | tf_op jit(solution)/shard_map/ppermute | solution.py:138
  39.7 3.6 %collective-permute-start.24 = (bf16[64,1440]{1,0:T(8,128)(2,1)S(1)}, bf16[64,1440]{1,0:T(8,128)(2,1)S(1)}, u32[]{:S(2)}, u32[]{:S(2)}) collective-permute-start(bf16[64,1440]{1,0:T(8,128)(2,1)S(1)} %get-tuple-element.95), channel_id=1, source_target_pairs={{0,1},{1,0},{2,3},{3,2},{4,5},{5,4},{6,7},{7,6},{8,9},{9,8},{10,11... | collective-permute-start | bytes 552968 | tf_op jit(solution)/shard_map/ppermute | solution.py:138
  39.7 13.8 %collective-permute-start.27 = (bf16[64,1440]{1,0:T(8,128)(2,1)S(1)}, bf16[64,1440]{1,0:T(8,128)(2,1)S(1)}, u32[]{:S(2)}, u32[]{:S(2)}) collective-permute-start(bf16[64,1440]{1,0:T(8,128)(2,1)S(1)} %get-tuple-element.99), channel_id=1, source_target_pairs={{0,1},{1,0},{2,3},{3,2},{4,5},{5,4},{6,7},{7,6},{8,9},{9,8},{10,11... | collective-permute-start | bytes 552968 | tf_op jit(solution)/shard_map/ppermute | solution.py:138
  40.2 5.2 %collective-permute-start.18 = (bf16[64,1440]{1,0:T(8,128)(2,1)S(1)}, bf16[64,1440]{1,0:T(8,128)(2,1)S(1)}, u32[]{:S(2)}, u32[]{:S(2)}) collective-permute-start(bf16[64,1440]{1,0:T(8,128)(2,1)S(1)} %get-tuple-element.86), channel_id=1, source_target_pairs={{0,1},{1,0},{2,3},{3,2},{4,5},{5,4},{6,7},{7,6},{8,9},{9,8},{10,11... | collective-permute-start | bytes 552968 | tf_op jit(solution)/shard_map/ppermute | solution.py:138
  42.7 1.4 %collective-permute-start.22 = (bf16[32,1440]{1,0:T(8,128)(2,1)S(1)}, bf16[32,1440]{1,0:T(8,128)(2,1)S(1)}, u32[]{:S(2)}, u32[]{:S(2)}) collective-permute-start(bf16[32,1440]{1,0:T(8,128)(2,1)S(1)} %get-tuple-element.92), channel_id=1, source_target_pairs={{0,1},{1,0},{2,3},{3,2},{4,5},{5,4},{6,7},{7,6},{8,9},{9,8},{10,11... | collective-permute-start | bytes 276488 | tf_op jit(solution)/shard_map/ppermute | solution.py:138
  43.1 1.3 %collective-permute-start.21 = (bf16[32,1440]{1,0:T(8,128)(2,1)S(1)}, bf16[32,1440]{1,0:T(8,128)(2,1)S(1)}, u32[]{:S(2)}, u32[]{:S(2)}) collective-permute-start(bf16[32,1440]{1,0:T(8,128)(2,1)S(1)} %get-tuple-element.90), channel_id=1, source_target_pairs={{0,1},{1,0},{2,3},{3,2},{4,5},{5,4},{6,7},{7,6},{8,9},{9,8},{10,11... | collective-permute-start | bytes 276488 | tf_op jit(solution)/shard_map/ppermute | solution.py:138
  44.5 4.9 %collective-permute-start.25 = (bf16[32,1440]{1,0:T(8,128)(2,1)S(1)}, bf16[32,1440]{1,0:T(8,128)(2,1)S(1)}, u32[]{:S(2)}, u32[]{:S(2)}) collective-permute-start(bf16[32,1440]{1,0:T(8,128)(2,1)S(1)} %add_convert_fusion.15), channel_id=1, source_target_pairs={{0,2},{1,3},{2,0},{3,1},{4,6},{5,7},{6,4},{7,5},{8,10},{9,11},{10,... | collective-permute-start | bytes 276488 | tf_op jit(solution)/shard_map/ppermute | solution.py:138
  45.5 5.9 %collective-permute-start.23 = (bf16[32,1440]{1,0:T(8,128)(2,1)S(1)}, bf16[32,1440]{1,0:T(8,128)(2,1)S(1)}, u32[]{:S(2)}, u32[]{:S(2)}) collective-permute-start(bf16[32,1440]{1,0:T(8,128)(2,1)S(1)} %add_convert_fusion.14), channel_id=1, source_target_pairs={{0,14},{1,15},{2,4},{3,5},{4,2},{5,3},{6,8},{7,9},{8,6},{9,7},{10,... | collective-permute-start | bytes 276488 | tf_op jit(solution)/shard_map/ppermute | solution.py:138
  51.5 7.0 %collective-permute-start.28 = (bf16[64,1440]{1,0:T(8,128)(2,1)S(1)}, bf16[64,1440]{1,0:T(8,128)(2,1)S(1)}, u32[]{:S(2)}, u32[]{:S(2)}) collective-permute-start(bf16[64,1440]{1,0:T(8,128)(2,1)S(1)} %pad_maximum_fusion.1), channel_id=1, source_target_pairs={{0,14},{1,15},{2,4},{3,5},{4,2},{5,3},{6,8},{7,9},{8,6},{9,7},{10,... | collective-permute-start | bytes 552968 | tf_op jit(solution)/shard_map/ppermute | solution.py:138
  53.1 9.7 %collective-permute-start.30 = (bf16[64,1440]{1,0:T(8,128)(2,1)S(1)}, bf16[64,1440]{1,0:T(8,128)(2,1)S(1)}, u32[]{:S(2)}, u32[]{:S(2)}) collective-permute-start(bf16[64,1440]{1,0:T(8,128)(2,1)S(1)} %get-tuple-element.103), channel_id=1, source_target_pairs={{0,1},{1,0},{2,3},{3,2},{4,5},{5,4},{6,7},{7,6},{8,9},{9,8},{10,11... | collective-permute-start | bytes 552968 | tf_op jit(solution)/shard_map/ppermute | solution.py:138
  53.1 5.5 %collective-permute-start.13 = (bf16[64,1440]{1,0:T(8,128)(2,1)S(1)}, bf16[64,1440]{1,0:T(8,128)(2,1)S(1)}, u32[]{:S(2)}, u32[]{:S(2)}) collective-permute-start(bf16[64,1440]{1,0:T(8,128)(2,1)S(1)} %get-tuple-element.78), channel_id=1, source_target_pairs={{0,1},{1,0},{2,3},{3,2},{4,5},{5,4},{6,7},{7,6},{8,9},{9,8},{10,11... | collective-permute-start | bytes 552968 | tf_op jit(solution)/shard_map/ppermute | solution.py:138
  53.6 6.8 %collective-permute-start.26 = (bf16[64,1440]{1,0:T(8,128)(2,1)S(1)}, bf16[64,1440]{1,0:T(8,128)(2,1)S(1)}, u32[]{:S(2)}, u32[]{:S(2)}) collective-permute-start(bf16[64,1440]{1,0:T(8,128)(2,1)S(1)} %pad_maximum_fusion), channel_id=1, source_target_pairs={{0,2},{1,3},{2,0},{3,1},{4,6},{5,7},{6,4},{7,5},{8,10},{9,11},{10,... | collective-permute-start | bytes 552968 | tf_op jit(solution)/shard_map/ppermute | solution.py:138
  60.5 7.3 %collective-permute-start.31 = (bf16[64,1440]{1,0:T(8,128)(2,1)S(1)}, bf16[64,1440]{1,0:T(8,128)(2,1)S(1)}, u32[]{:S(2)}, u32[]{:S(2)}) collective-permute-start(bf16[64,1440]{1,0:T(8,128)(2,1)S(1)} %add_convert_fusion.6), channel_id=1, source_target_pairs={{0,14},{1,15},{2,4},{3,5},{4,2},{5,3},{6,8},{7,9},{8,6},{9,7},{10,... | collective-permute-start | bytes 552968 | tf_op jit(solution)/shard_map/ppermute | solution.py:138
  62.3 9.3 %collective-permute-start.3 = (bf16[64,1440]{1,0:T(8,128)(2,1)S(1)}, bf16[64,1440]{1,0:T(8,128)(2,1)S(1)}, u32[]{:S(2)}, u32[]{:S(2)}) collective-permute-start(bf16[64,1440]{1,0:T(8,128)(2,1)S(1)} %get-tuple-element.59), channel_id=1, source_target_pairs={{0,1},{1,0},{2,3},{3,2},{4,5},{5,4},{6,7},{7,6},{8,9},{9,8},{10,11... | collective-permute-start | bytes 552968 | tf_op jit(solution)/shard_map/ppermute | solution.py:138
  62.3 5.5 %collective-permute-start.8 = (bf16[64,1440]{1,0:T(8,128)(2,1)S(1)}, bf16[64,1440]{1,0:T(8,128)(2,1)S(1)}, u32[]{:S(2)}, u32[]{:S(2)}) collective-permute-start(bf16[64,1440]{1,0:T(8,128)(2,1)S(1)} %get-tuple-element.70), channel_id=1, source_target_pairs={{0,1},{1,0},{2,3},{3,2},{4,5},{5,4},{6,7},{7,6},{8,9},{9,8},{10,11... | collective-permute-start | bytes 552968 | tf_op jit(solution)/shard_map/ppermute | solution.py:138
  62.8 6.8 %collective-permute-start.29 = (bf16[64,1440]{1,0:T(8,128)(2,1)S(1)}, bf16[64,1440]{1,0:T(8,128)(2,1)S(1)}, u32[]{:S(2)}, u32[]{:S(2)}) collective-permute-start(bf16[64,1440]{1,0:T(8,128)(2,1)S(1)} %add_convert_fusion.4), channel_id=1, source_target_pairs={{0,2},{1,3},{2,0},{3,1},{4,6},{5,7},{6,4},{7,5},{8,10},{9,11},{10,... | collective-permute-start | bytes 552968 | tf_op jit(solution)/shard_map/ppermute | solution.py:138
  69.7 6.0 %collective-permute-start.32 = (bf16[64,1440]{1,0:T(8,128)(2,1)S(1)}, bf16[64,1440]{1,0:T(8,128)(2,1)S(1)}, u32[]{:S(2)}, u32[]{:S(2)}) collective-permute-start(bf16[64,1440]{1,0:T(8,128)(2,1)S(1)} %add_convert_fusion.1), channel_id=1, source_target_pairs={{0,2},{1,3},{2,0},{3,1},{4,6},{5,7},{6,4},{7,5},{8,10},{9,11},{10,... | collective-permute-start | bytes 552968 | tf_op jit(solution)/shard_map/ppermute | solution.py:138
  70.1 7.2 %collective-permute-start.33 = (bf16[64,1440]{1,0:T(8,128)(2,1)S(1)}, bf16[64,1440]{1,0:T(8,128)(2,1)S(1)}, u32[]{:S(2)}, u32[]{:S(2)}) collective-permute-start(bf16[64,1440]{1,0:T(8,128)(2,1)S(1)} %add_convert_fusion.3), channel_id=1, source_target_pairs={{0,14},{1,15},{2,4},{3,5},{4,2},{5,3},{6,8},{7,9},{8,6},{9,7},{10,... | collective-permute-start | bytes 552968 | tf_op jit(solution)/shard_map/ppermute | solution.py:138

commit v3 on v1

v3 whole, which is shorter than its diff:
```python
import jax
import jax.numpy as jnp
from jax import lax
from jax.experimental import pallas as pl
from jax.experimental.pallas import tpu as pltpu
from jax.sharding import PartitionSpec as P

LANES = 128
LOAD_COLUMNS = 512
LEAST_ROWS = 128
BF16, F32 = jnp.bfloat16, jnp.float32


def pad_up(n, m):
    return -(-n // m) * m


def ring_pairs(n):
    chips = n // 2

    def odd(chip):
        return (chip - 1) % chips if chip % 2 == 0 else (chip + 1) % chips

    swap = [(i, i ^ 1) for i in range(n)]
    even_pairs = [(i, i ^ 2) for i in range(n)]
    odd_pairs = [(i, odd(i // 2) * 2 + i % 2) for i in range(n)]
    across = [(i, (i + n // 2) % n) for i in range(n)]
    return swap, even_pairs, odd_pairs, across


def route_kernel(experts, count_ref, x_ref, ids_ref, gw_ref, out_ref):
    rows, width = x_ref.shape
    last = width // LANES * LANES
    start = width - last
    column = lax.broadcasted_iota(jnp.int32, (LANES, rows), 0) - start
    expert = column & (experts - 1)
    weight = jnp.zeros((LANES, rows), F32)
    for k in range(ids_ref.shape[0]):
        weight += jnp.where(ids_ref[k : k + 1, :] == expert, gw_ref[k : k + 1, :], 0.0)
    live = lax.broadcasted_iota(jnp.int32, (LANES, rows), 1) < count_ref[0]
    weight = jnp.where(live, weight, 0.0)
    high = weight.astype(BF16).astype(F32)
    middle = (weight - high).astype(BF16).astype(F32)
    low = weight - high - middle
    part = jnp.where(column < experts, high, jnp.where(column < 2 * experts, middle, low))
    part = jnp.where((column >= 0) & (column < 3 * experts), part, 0.0).T
    out_ref[:, :last] = x_ref[:, :last]
    tail = jnp.concatenate([x_ref[:, last:].astype(F32), jnp.zeros((rows, LANES - start), F32)], axis=1)
    lane = lax.broadcasted_iota(jnp.int32, (rows, LANES), 1)
    out_ref[:, last:] = jnp.where(lane < start, tail, part).astype(BF16)


def expert_body(experts, xs, parts, hidden, ready, partials, ys):
    width, ff = parts[0][1].shape
    last = width // LANES * LANES
    start = width - last
    x = jnp.concatenate([r[:, :width] for r in xs], axis=0)
    filler = LEAST_ROWS - x.shape[0]
    if filler > 0:
        x = jnp.concatenate([x, jnp.zeros((filler, width), x.dtype)], axis=0)
    tail = jnp.concatenate([r[:, last : last + LANES] for r in xs], axis=0).astype(F32)
    lane = lax.broadcasted_iota(jnp.int32, tail.shape, 1) - start
    rows = x.shape[0]
    weight = []
    for k, (who, wg, wu, _) in enumerate(parts):
        mine = (lane >= 0) & (lane < 3 * experts) & ((lane & (experts - 1)) == who)
        weight.append(jnp.sum(jnp.where(mine, tail, 0.0), axis=1, keepdims=True))
        for lo in range(0, ff, 256):
            hi = min(lo + 256, ff)
            ready(k, lo, (0, 1))
            gate = jnp.dot(x, wg[:, lo:hi], preferred_element_type=F32)
            up = jnp.dot(x, wu[:, lo:hi], preferred_element_type=F32)
            hidden[k * rows : (k + 1) * rows, lo:hi] = ((up + 1.0) * gate * jax.nn.sigmoid(1.702 * gate)).astype(BF16)
    for lo in range(0, width, 256):
        hi = min(lo + 256, width)
        total = jnp.concatenate([r[:, lo:hi] for r in partials], axis=0) if partials else 0.0
        for k, (_, _, _, wd) in enumerate(parts):
            ready(k, lo, (2,))
            y = jnp.dot(hidden[k * rows : (k + 1) * rows, :], wd[:, lo:hi], preferred_element_type=F32)
            total = total + y[: tail.shape[0]].astype(BF16).astype(F32) * weight[k]
        at = 0
        for r in ys:
            r[:, lo:hi] = total[at : at + r.shape[0]].astype(r.dtype)
            at += r.shape[0]


def experts_apply(experts, blocks, near, far, partials, cut, dtype, fetch=()):
    sets = [w for w in (near, far) if w is not None]
    load = sets[0][0].ndim == 3
    width, ff = sets[0][0].shape[-2:]
    total, count = sum(b.shape[0] for b in blocks), len(blocks)
    vmem = pl.BlockSpec(memory_space=pltpu.VMEM)
    hbm = pl.BlockSpec(memory_space=pltpu.HBM)
    pieces = total // cut
    held = [*(sets[0] if load else ()), *fetch]
    out_shape = [pltpu.VMEM((cut, width), dtype)] * pieces + [pltpu.VMEM(w.shape[1:], BF16) for w in held]
    rows = max(total, LEAST_ROWS)
    scratch = [pltpu.VMEM((rows * len(sets), ff), BF16)]
    cuts = list(range(0, ff, LOAD_COLUMNS))
    if held:
        scratch += [pltpu.SemaphoreType.DMA((len(held), len(cuts)))]

    def body(*refs):
        refs = list(refs)

        def take(k):
            out = refs[:k]
            del refs[:k]
            return out

        xs, ps = take(count), take(len(partials))
        weights = [take(3) for _ in sets]
        sources = [*(weights[0] if load else ()), *take(len(fetch))]
        ys, targets = take(pieces), take(len(held))
        copies = {}
        for j, (source, target) in enumerate(zip(sources, targets)):
            for c, lo in enumerate(cuts):
                part = pl.ds(lo, min(LOAD_COLUMNS, ff - lo))
                copies[j, lo] = pltpu.make_async_copy(source.at[0, :, part], target.at[:, part], refs[-1].at[j, c])
        for j, lo in sorted(copies, key=lambda key: (key[0] // 2, key[1])):
            copies[j, lo].start()
        waited = set()

        def ready(k, lo, which):
            for j in which:
                if load and k == 0 and (j, lo) in copies:
                    copies[j, lo].wait()
                    waited.add((j, lo))

        if load:
            weights[0] = targets[:3]
        me = lax.axis_index("ep")
        who = ([me] if near is not None else []) + ([me ^ 1] if far is not None else [])
        expert_body(experts, xs, [(i, *w) for i, w in zip(who, weights)], refs[0], ready, ps, ys)
        for key in copies:
            if key not in waited:
                copies[key].wait()

    def hold(arrays, space):
        return [pltpu.with_memory_space_constraint(a, space) for a in arrays]

    out = pl.pallas_call(
        body,
        out_shape=out_shape,
        in_specs=[vmem] * (count + len(partials))
        + [hbm if load else vmem] * 3
        + [vmem] * (3 * len(sets) - 3)
        + [hbm] * len(fetch),
        out_specs=[vmem] * len(out_shape),
        scratch_shapes=scratch,
        compiler_params=pltpu.CompilerParams(vmem_limit_bytes=12 << 20),
        cost_estimate=pl.CostEstimate(
            flops=6 * total * width * ff * len(sets), bytes_accessed=total * width * 4, transcendentals=total * ff
        ),
        name="experts",
    )(
        *hold([*blocks, *partials], pltpu.VMEM),
        *hold(sets[0], pltpu.HBM if load else pltpu.VMEM),
        *[a for w in sets[1:] for a in hold(w, pltpu.VMEM)],
        *hold(fetch, pltpu.HBM),
    )
    return (out[:pieces], out[pieces:]) if held else out


def add(*terms):
    total = terms[0].astype(F32)
    for t in terms[1:]:
        total = total + t.astype(F32)
    return total.astype(BF16)


def local(tokens, expert_ids, gate_weights, row_counts, w_gate, w_up, w_down):
    n = lax.axis_size("ep")
    rows, width = tokens.shape
    half = rows // 2
    experts = n * w_gate.shape[0]
    swap, even, odd, across = ring_pairs(n)

    def send(x, pairs):
        return lax.ppermute(x, "ep", pairs)

    vmem = pl.BlockSpec(memory_space=pltpu.VMEM)
    own = pl.pallas_call(
        lambda *refs: route_kernel(experts, *refs),
        out_shape=pltpu.VMEM((rows, pad_up(width, LANES)), BF16),
        in_specs=[pl.BlockSpec(memory_space=pltpu.SMEM), vmem, vmem, vmem],
        out_specs=vmem,
        compiler_params=pltpu.CompilerParams(vmem_limit_bytes=4 << 20),
        name="route",
    )(row_counts, *[pltpu.with_memory_space_constraint(x, pltpu.HBM) for x in (tokens, expert_ids.T, gate_weights.T)])

    fence = lax.optimization_barrier
    far = [send(w.reshape(w.shape[1:]), swap) for w in (w_gate, w_up, w_down)]

    e1, o1 = send(own, even), send(own, odd)
    p0, near = experts_apply(experts, [own], [w_gate, w_up, w_down], None, [], rows, F32)
    e1, o1, p0 = fence((e1, o1, p0))
    e2, o2 = send(o1, even), send(e1, odd)
    p1 = experts_apply(experts, [e1, o1], near, None, [], rows, F32)
    e2, o2, p1 = fence((e2, o2, p1))
    e3, o3 = send(o2, even), send(e2, odd)
    p2 = experts_apply(experts, [e2, o2], near, None, [], rows, F32)
    p2, p1, far = fence((p2, p1, far))
    t0, te1, to1 = experts_apply(experts, [own, e1, o1], None, far, [*p0, *p1], rows, BF16)
    e3, o3, p2, t0 = fence((e3, o3, p2, t0))
    e4, o4 = send(o3[:half], even), send(e3[half:], odd)
    te3, to3 = experts_apply(experts, [e3, o3], near, far, [], rows, BF16)
    te3, to3, e4, o4 = fence((te3, to3, e4, o4))
    re, ro = send(te3, even), send(to3, odd)
    (t4,) = experts_apply(experts, [e4, o4], near, far, [], rows, BF16)
    r4 = send(t4, across)
    te2, to2 = experts_apply(experts, [e2, o2], None, far, p2, rows, BF16)
    te2, to2, re, ro = fence((te2, to2, re, ro))
    re, ro = send(add(te2, ro), even), send(add(to2, re), odd)
    re, ro = send(add(te1, ro), even), send(add(to1, re), odd)
    return add(t0, r4, re, ro)


def solution(mesh):
    rows = P(("grp", "ep"), None)
    in_specs = (rows, rows, rows, P(("grp", "ep"))) + (P("ep", None, None),) * 3
    return jax.shard_map(local, mesh=mesh, in_specs=in_specs, out_specs=rows, check_vma=False)
```

time: 107 us -> 68.5 us (0.64)
  waiting for transfers between devices: 44.2 us -> 18.9 us
  local copies, waits for them, and re-layouts: 15 us -> 0.02 us
  Pallas kernels: 19.5 us -> 23.2 us
  starting transfers between devices: 25.7 us -> 24.5 us
    ppermute x34 -> x18, waiting for transfers between devices: 44.2 us -> 18.9 us  [send(): return lax.ppermute(x, 'ep', pairs)]
    unnamed x34 -> x0, local copies, waits for them, and re-layouts: 15 us -> none
    pallas_call x6 -> x8, Pallas kernels: 19.5 us -> 23.2 us  [the longest x7 22.1 us: experts_apply(): pl.pallas_call(body, out_shape=out_shape, in_specs=[vmem] * (count + len(...]
    ppermute x34 -> x18, starting transfers between devices: 25.7 us -> 24.5 us  [send(): return lax.ppermute(x, 'ep', pairs)]
  transfers between devices with their start and end apart: 34 -> 18, of which waited for: 13 -> 6; matrix products, arithmetic and copies ran while one was open for 1% -> 0% of each run, Pallas kernels for 17% -> 34%
where the time goes in v3:
time: 68.5 us; the launch traced here: 68.3 us
  starting transfers between devices  24.5 us (36%)
  Pallas kernels  23.2 us (34%)
  waiting for transfers between devices  18.9 us (28%)
  other arithmetic  0.97 us (1%)
  between operations  0.83 us (1%)
    ppermute x18, starting transfers between devices, send(): return lax.ppermute(x, 'ep', pairs)  24.5 us
    pallas_call x7, Pallas kernels, experts_apply(): pl.pallas_call(body, out_shape=out_shape, in_specs=[vmem] * (count + len(...  22.1 us
    ppermute x18, waiting for transfers between devices, send(): return lax.ppermute(x, 'ep', pairs)  18.9 us
  transfers between devices with their start and end apart: 18, of which 6 were waited for; matrix products, arithmetic and copies ran while one was open for 0% of the time, Pallas kernels for 34%

profile of v3, /device:TPU:26, one launch (start us, length us, event | category | flops | bytes accessed | tf_op | source)
XLA Modules:
  0.0 68.3 jit_solution(14037621373924238323)
XLA Ops:
  0.0 0.0 collective-permute-start.6
  0.0 0.5 collective-permute-start.7
  0.5 0.0 collective-permute-start.8
  1.2 1.0 %route.1.refs_0_ = bf16[64,1536]{1,0:T(8,128)(2,1)S(1)} custom-call(s32[1]{0:T(128)S(6)} %copy.8.refs_0_, bf16[64,1440]{1,0:T(8,128)(2,1)} %refs_1_.2, s32[4,64]{1,0:T(4,128)} %bitcast.8, f32[4,64]{1,0:T(4,128)} %bitcast.9), custom_call_target="tpu_custom_call" | custom-call | tf_op jit(solution)/shard_map/route/pallas_call | solution.py:183
  2.2 2.0 %collective-permute-start = (bf16[64,1536]{1,0:T(8,128)(2,1)S(1)}, bf16[64,1536]{1,0:T(8,128)(2,1)S(1)}, u32[]{:S(2)}, u32[]{:S(2)}) collective-permute-start(bf16[64,1536]{1,0:T(8,128)(2,1)S(1)} %route.1.refs_0_), channel_id=1, source_target_pairs={{0,2},{1,3},{2,0},{3,1},{4,6},{5,7},{6,4},{7,5},{8,10},{9,11},{10,... | collective-permute-start | bytes 589832 | tf_op jit(solution)/shard_map/ppermute | solution.py:180
  4.2 4.9 %collective-permute-start.1 = (bf16[64,1536]{1,0:T(8,128)(2,1)S(1)}, bf16[64,1536]{1,0:T(8,128)(2,1)S(1)}, u32[]{:S(2)}, u32[]{:S(2)}) collective-permute-start(bf16[64,1536]{1,0:T(8,128)(2,1)S(1)} %route.1.refs_0_), channel_id=1, source_target_pairs={{0,14},{1,15},{2,4},{3,5},{4,2},{5,3},{6,8},{7,9},{8,6},{9,7},{10,... | collective-permute-start | bytes 589832 | tf_op jit(solution)/shard_map/ppermute | solution.py:180
  9.2 5.4 %experts.7 = (f32[64,1440]{1,0:T(8,128)S(1)}, bf16[1440,1440]{1,0:T(8,128)(2,1)S(1)}, bf16[1440,1440]{1,0:T(8,128)(2,1)S(1)}, bf16[1440,1440]{1,0:T(8,128)(2,1)S(1)}) custom-call(bf16[64,1536]{1,0:T(8,128)(2,1)S(1)} %route.1.refs_0_, bf16[1,1440,1440]{2,1,0:T(8,128)(2,1)} %refs_1_.3, bf16[1,1440,1440]{2,1,0:T(8,128)(2,1)} %refs_2_.1, ...), custom_call_target="tpu_custom_call" | custom-call | flops 796262400 | bytes 368640 | tf_op jit(solution)/shard_map/experts/pallas_call | solution.py:142
  14.6 0.0 collective-permute-done.refs_0_.refs_1_
  14.6 0.0 collective-permute-done.1.refs_1_.refs_2_
  14.6 0.1 collective-permute-start.2
  14.7 2.7 %collective-permute-start.3 = (bf16[64,1536]{1,0:T(8,128)(2,1)S(1)}, bf16[64,1536]{1,0:T(8,128)(2,1)S(1)}, u32[]{:S(2)}, u32[]{:S(2)}) collective-permute-start(bf16[64,1536]{1,0:T(8,128)(2,1)S(1)} %collective-permute-done.refs_0_.refs_1_), channel_id=1, source_target_pairs={{0,14},{1,15},{2,4},{3,5},{4,2},{5,3},{6,8},{7,9},{8,6},{9,7},{10,... | collective-permute-start | bytes 589832 | tf_op jit(solution)/shard_map/ppermute | solution.py:180
  17.4 2.0 %experts.8 = (f32[64,1440]{1,0:T(8,128)S(1)}, f32[64,1440]{1,0:T(8,128)S(1)}) custom-call(bf16[64,1536]{1,0:T(8,128)(2,1)S(1)} %collective-permute-done.refs_0_.refs_1_, bf16[64,1536]{1,0:T(8,128)(2,1)S(1)} %collective-permute-done.1.refs_1_.refs_2_, bf16[1440,1440]{1,0:T(8,128)(2,1)S(1)} %get-tuple-element.50.refs_2_, ...), custom_call_target="tpu_custom_call" | custom-call | flops 1592524800 | bytes 737280 | tf_op jit(solution)/shard_map/experts/pallas_call | solution.py:142
  19.4 2.0 %collective-permute-done.2.refs_0_ = bf16[64,1536]{1,0:T(8,128)(2,1)S(1)} collective-permute-done((bf16[64,1536]{1,0:T(8,128)(2,1)S(1)}, bf16[64,1536]{1,0:T(8,128)(2,1)S(1)}, u32[]{:S(2)}, u32[]{:S(2)}) %collective-permute-start.2) | collective-permute-done | bytes 196640 | tf_op jit(solution)/shard_map/ppermute | solution.py:180
  21.5 1.3 %collective-permute-done.3.refs_1_ = bf16[64,1536]{1,0:T(8,128)(2,1)S(1)} collective-permute-done((bf16[64,1536]{1,0:T(8,128)(2,1)S(1)}, bf16[64,1536]{1,0:T(8,128)(2,1)S(1)}, u32[]{:S(2)}, u32[]{:S(2)}) %collective-permute-start.3) | collective-permute-done | bytes 196640 | tf_op jit(solution)/shard_map/ppermute | solution.py:180
  22.8 0.4 collective-permute-start.4
  23.2 2.2 %collective-permute-start.5 = (bf16[64,1536]{1,0:T(8,128)(2,1)S(1)}, bf16[64,1536]{1,0:T(8,128)(2,1)S(1)}, u32[]{:S(2)}, u32[]{:S(2)}) collective-permute-start(bf16[64,1536]{1,0:T(8,128)(2,1)S(1)} %collective-permute-done.2.refs_0_), channel_id=1, source_target_pairs={{0,14},{1,15},{2,4},{3,5},{4,2},{5,3},{6,8},{7,9},{8,6},{9,7},{10,... | collective-permute-start | bytes 589832 | tf_op jit(solution)/shard_map/ppermute | solution.py:180
  25.4 2.0 %experts.9 = (f32[64,1440]{1,0:T(8,128)S(1)}, f32[64,1440]{1,0:T(8,128)S(1)}) custom-call(bf16[64,1536]{1,0:T(8,128)(2,1)S(1)} %collective-permute-done.2.refs_0_, bf16[64,1536]{1,0:T(8,128)(2,1)S(1)} %collective-permute-done.3.refs_1_, bf16[1440,1440]{1,0:T(8,128)(2,1)S(1)} %get-tuple-element.50.refs_2_, bf16[1440,1440]{1,0:T(8,128)(2,1)S(1)} %get-tuple-element.51.refs_3_, ...), custom_call_target="tpu_custom_call" | custom-call | flops 1592524800 | bytes 737280 | tf_op jit(solution)/shard_map/experts/pallas_call | solution.py:142
  27.4 0.0 collective-permute-done.6.refs_6_.refs_5_.refs_4_
  27.4 0.0 collective-permute-done.7.refs_7_.refs_6_.refs_5_
  27.4 0.0 collective-permute-done.8.refs_8_.refs_7_.refs_6_
  27.4 2.9 %experts.10 = (bf16[64,1440]{1,0:T(8,128)(2,1)S(1)}, bf16[64,1440]{1,0:T(8,128)(2,1)S(1)}, bf16[64,1440]{1,0:T(8,128)(2,1)S(1)}) custom-call(bf16[64,1536]{1,0:T(8,128)(2,1)S(1)} %route.1.refs_0_, bf16[64,1536]{1,0:T(8,128)(2,1)S(1)} %collective-permute-done.refs_0_.refs_1_, bf16[64,1536]{1,0:T(8,128)(2,1)S(1)} %collective-permute-done.1.refs_1_.refs_2_, ...), custom_call_target="tpu_custom_call" | custom-call | flops 2388787200 | bytes 1105920 | tf_op jit(solution)/shard_map/experts/pallas_call | solution.py:142
  30.4 0.0 collective-permute-done.4.refs_0_
  30.4 0.0 collective-permute-done.5.refs_1_
  30.4 2.0 %collective-permute-start.10 = (bf16[32,1536]{1,0:T(8,128)(2,1)S(1)}, bf16[32,1536]{1,0:T(8,128)(2,1)S(1)}, u32[]{:S(2)}, u32[]{:S(2)}) collective-permute-start(bf16[32,1536]{1,0:T(8,128)(2,1)S(1)} %slice.7), channel_id=1, source_target_pairs={{0,14},{1,15},{2,4},{3,5},{4,2},{5,3},{6,8},{7,9},{8,6},{9,7},{10,... | collective-permute-start | bytes 294920 | tf_op jit(solution)/shard_map/ppermute | solution.py:180
  32.4 0.1 collective-permute-start.9
  32.5 3.9 %experts.11 = (bf16[64,1440]{1,0:T(8,128)(2,1)S(1)}, bf16[64,1440]{1,0:T(8,128)(2,1)S(1)}) custom-call(bf16[64,1536]{1,0:T(8,128)(2,1)S(1)} %collective-permute-done.4.refs_0_, bf16[64,1536]{1,0:T(8,128)(2,1)S(1)} %collective-permute-done.5.refs_1_, bf16[1440,1440]{1,0:T(8,128)(2,1)S(1)} %get-tuple-element.50.refs_2_, ...), custom_call_target="tpu_custom_call" | custom-call | flops 3185049600 | bytes 737280 | tf_op jit(solution)/shard_map/experts/pallas_call | solution.py:142
  36.3 0.0 collective-permute-done.10.refs_1_
  36.3 1.3 %collective-permute-done.9.refs_0_ = bf16[32,1536]{1,0:T(8,128)(2,1)S(1)} collective-permute-done((bf16[32,1536]{1,0:T(8,128)(2,1)S(1)}, bf16[32,1536]{1,0:T(8,128)(2,1)S(1)}, u32[]{:S(2)}, u32[]{:S(2)}) %collective-permute-start.9) | collective-permute-done | bytes 98336 | tf_op jit(solution)/shard_map/ppermute | solution.py:180
  37.6 0.8 %collective-permute-start.12 = (bf16[64,1440]{1,0:T(8,128)(2,1)S(1)}, bf16[64,1440]{1,0:T(8,128)(2,1)S(1)}, u32[]{:S(2)}, u32[]{:S(2)}) collective-permute-start(bf16[64,1440]{1,0:T(8,128)(2,1)S(1)} %get-tuple-element.82), channel_id=1, source_target_pairs={{0,2},{1,3},{2,0},{3,1},{4,6},{5,7},{6,4},{7,5},{8,10},{9,11},{10,... | collective-permute-start | bytes 552968 | tf_op jit(solution)/shard_map/ppermute | solution.py:180
  38.4 1.4 %collective-permute-start.13 = (bf16[64,1440]{1,0:T(8,128)(2,1)S(1)}, bf16[64,1440]{1,0:T(8,128)(2,1)S(1)}, u32[]{:S(2)}, u32[]{:S(2)}) collective-permute-start(bf16[64,1440]{1,0:T(8,128)(2,1)S(1)} %get-tuple-element.83), channel_id=1, source_target_pairs={{0,14},{1,15},{2,4},{3,5},{4,2},{5,3},{6,8},{7,9},{8,6},{9,7},{10,... | collective-permute-start | bytes 552968 | tf_op jit(solution)/shard_map/ppermute | solution.py:180
  39.8 2.0 %experts.13 = (bf16[64,1440]{1,0:T(8,128)(2,1)S(1)}, bf16[64,1440]{1,0:T(8,128)(2,1)S(1)}) custom-call(bf16[64,1536]{1,0:T(8,128)(2,1)S(1)} %collective-permute-done.2.refs_0_, bf16[64,1536]{1,0:T(8,128)(2,1)S(1)} %collective-permute-done.3.refs_1_, f32[64,1440]{1,0:T(8,128)S(1)} %get-tuple-element.78.refs_2_, f32[64,1440]{1,0:T(8,128)S(1)} %get-tuple-element.79.refs_3_, ...), custom_call_target="tpu_custom_call" | custom-call | flops 1592524800 | bytes 737280 | tf_op jit(solution)/shard_map/experts/pallas_call | solution.py:142
  41.8 3.9 %experts.12 = bf16[64,1440]{1,0:T(8,128)(2,1)S(1)} custom-call(bf16[32,1536]{1,0:T(8,128)(2,1)S(1)} %collective-permute-done.9.refs_0_, bf16[32,1536]{1,0:T(8,128)(2,1)S(1)} %collective-permute-done.10.refs_1_, bf16[1440,1440]{1,0:T(8,128)(2,1)S(1)} %get-tuple-element.50.refs_2_, bf16[1440,1440]{1,0:T(8,128)(2,1)S(1)} %get-tuple-element.51.refs_3_, ...), custom_call_target="tpu_custom_call" | custom-call | flops 1592524800 | bytes 368640 | tf_op jit(solution)/shard_map/experts/pallas_call | solution.py:142
  45.7 3.3 %collective-permute-start.11 = (bf16[64,1440]{1,0:T(8,128)(2,1)S(1)}, bf16[64,1440]{1,0:T(8,128)(2,1)S(1)}, u32[]{:S(2)}, u32[]{:S(2)}) collective-permute-start(bf16[64,1440]{1,0:T(8,128)(2,1)S(1)} %experts.12), channel_id=1, source_target_pairs={{0,8},{1,9},{2,10},{3,11},{4,12},{5,13},{6,14},{7,15},{8,0},{9,1},... | collective-permute-start | bytes 552968 | tf_op jit(solution)/shard_map/ppermute | solution.py:180
  49.0 0.0 collective-permute-done.12
  49.0 0.0 collective-permute-done.13
  49.1 1.5 %collective-permute-start.14 = (bf16[64,1440]{1,0:T(8,128)(2,1)S(1)}, bf16[64,1440]{1,0:T(8,128)(2,1)S(1)}, u32[]{:S(2)}, u32[]{:S(2)}) collective-permute-start(bf16[64,1440]{1,0:T(8,128)(2,1)S(1)} %add_convert_fusion.4), channel_id=1, source_target_pairs={{0,14},{1,15},{2,4},{3,5},{4,2},{5,3},{6,8},{7,9},{8,6},{9,7},{10,... | collective-permute-start | bytes 552968 | tf_op jit(solution)/shard_map/ppermute | solution.py:180
  50.6 0.1 collective-permute-start.16
  50.7 9.1 %collective-permute-done.14 = bf16[64,1440]{1,0:T(8,128)(2,1)S(1)} collective-permute-done((bf16[64,1440]{1,0:T(8,128)(2,1)S(1)}, bf16[64,1440]{1,0:T(8,128)(2,1)S(1)}, u32[]{:S(2)}, u32[]{:S(2)}) %collective-permute-start.14) | collective-permute-done | bytes 184352 | tf_op jit(solution)/shard_map/ppermute | solution.py:180
  59.8 0.1 add_convert_fusion.3
  59.8 0.7 %collective-permute-start.15 = (bf16[64,1440]{1,0:T(8,128)(2,1)S(1)}, bf16[64,1440]{1,0:T(8,128)(2,1)S(1)}, u32[]{:S(2)}, u32[]{:S(2)}) collective-permute-start(bf16[64,1440]{1,0:T(8,128)(2,1)S(1)} %add_convert_fusion.3), channel_id=1, source_target_pairs={{0,2},{1,3},{2,0},{3,1},{4,6},{5,7},{6,4},{7,5},{8,10},{9,11},{10,... | collective-permute-start | bytes 552968 | tf_op jit(solution)/shard_map/ppermute | solution.py:180
  60.5 0.0 collective-permute-done.16
  60.5 0.1 add_convert_fusion.1
  60.6 1.9 %collective-permute-start.17 = (bf16[64,1440]{1,0:T(8,128)(2,1)S(1)}, bf16[64,1440]{1,0:T(8,128)(2,1)S(1)}, u32[]{:S(2)}, u32[]{:S(2)}) collective-permute-start(bf16[64,1440]{1,0:T(8,128)(2,1)S(1)} %add_convert_fusion.1), channel_id=1, source_target_pairs={{0,14},{1,15},{2,4},{3,5},{4,2},{5,3},{6,8},{7,9},{8,6},{9,7},{10,... | collective-permute-start | bytes 552968 | tf_op jit(solution)/shard_map/ppermute | solution.py:180
  62.5 0.0 collective-permute-done.11
  62.5 3.1 %collective-permute-done.15 = bf16[64,1440]{1,0:T(8,128)(2,1)S(1)} collective-permute-done((bf16[64,1440]{1,0:T(8,128)(2,1)S(1)}, bf16[64,1440]{1,0:T(8,128)(2,1)S(1)}, u32[]{:S(2)}, u32[]{:S(2)}) %collective-permute-start.15) | collective-permute-done | bytes 184352 | tf_op jit(solution)/shard_map/ppermute | solution.py:180
  65.6 2.0 %collective-permute-done.17 = bf16[64,1440]{1,0:T(8,128)(2,1)S(1)} collective-permute-done((bf16[64,1440]{1,0:T(8,128)(2,1)S(1)}, bf16[64,1440]{1,0:T(8,128)(2,1)S(1)}, u32[]{:S(2)}, u32[]{:S(2)}) %collective-permute-start.17) | collective-permute-done | bytes 184352 | tf_op jit(solution)/shard_map/ppermute | solution.py:180
  67.6 0.8 %add_convert_fusion = bf16[64,1440]{1,0:T(8,128)(2,1)} fusion(bf16[64,1440]{1,0:T(8,128)(2,1)S(1)} %collective-permute-done.17, bf16[64,1440]{1,0:T(8,128)(2,1)S(1)} %collective-permute-done.15, bf16[64,1440]{1,0:T(8,128)(2,1)S(1)} %collective-permute-done.11, bf16[64,1440]{1,0:T(8,128)(2,1)S(1)} %get-tuple-element.70), kind=kLoop, calls=%fused_computation | loop fusion | flops 737280 | bytes 921600 | tf_op jit(solution)/shard_map/convert_element_type | solution.py:169
  (4 shorter events, 0.1 us)
Async XLA Ops:
  0.0 27.4 %collective-permute-start.6 = (bf16[1440,1440]{1,0:T(8,128)(2,1)}, bf16[1440,1440]{1,0:T(8,128)(2,1)S(1)}, u32[]{:S(2)}, u32[]{:S(2)}) collective-permute-start(bf16[1440,1440]{1,0:T(8,128)(2,1)} %bitcast.5), channel_id=1, source_target_pairs={{0,1},{1,0},{2,3},{3,2},{4,5},{5,4},{6,7},{7,6},{8,9},{9,8},{10,11... | collective-permute-start | bytes 12441608 | tf_op jit(solution)/shard_map/ppermute | solution.py:180
  0.0 27.4 %collective-permute-start.7 = (bf16[1440,1440]{1,0:T(8,128)(2,1)}, bf16[1440,1440]{1,0:T(8,128)(2,1)S(1)}, u32[]{:S(2)}, u32[]{:S(2)}) collective-permute-start(bf16[1440,1440]{1,0:T(8,128)(2,1)} %bitcast.6), channel_id=1, source_target_pairs={{0,1},{1,0},{2,3},{3,2},{4,5},{5,4},{6,7},{7,6},{8,9},{9,8},{10,11... | collective-permute-start | bytes 12441608 | tf_op jit(solution)/shard_map/ppermute | solution.py:180
  0.5 26.9 %collective-permute-start.8 = (bf16[1440,1440]{1,0:T(8,128)(2,1)}, bf16[1440,1440]{1,0:T(8,128)(2,1)S(1)}, u32[]{:S(2)}, u32[]{:S(2)}) collective-permute-start(bf16[1440,1440]{1,0:T(8,128)(2,1)} %bitcast.7), channel_id=1, source_target_pairs={{0,1},{1,0},{2,3},{3,2},{4,5},{5,4},{6,7},{7,6},{8,9},{9,8},{10,11... | collective-permute-start | bytes 12441608 | tf_op jit(solution)/shard_map/ppermute | solution.py:180
  2.2 12.4 %collective-permute-start = (bf16[64,1536]{1,0:T(8,128)(2,1)S(1)}, bf16[64,1536]{1,0:T(8,128)(2,1)S(1)}, u32[]{:S(2)}, u32[]{:S(2)}) collective-permute-start(bf16[64,1536]{1,0:T(8,128)(2,1)S(1)} %route.1.refs_0_), channel_id=1, source_target_pairs={{0,2},{1,3},{2,0},{3,1},{4,6},{5,7},{6,4},{7,5},{8,10},{9,11},{10,... | collective-permute-start | bytes 589832 | tf_op jit(solution)/shard_map/ppermute | solution.py:180
  4.2 10.4 %collective-permute-start.1 = (bf16[64,1536]{1,0:T(8,128)(2,1)S(1)}, bf16[64,1536]{1,0:T(8,128)(2,1)S(1)}, u32[]{:S(2)}, u32[]{:S(2)}) collective-permute-start(bf16[64,1536]{1,0:T(8,128)(2,1)S(1)} %route.1.refs_0_), channel_id=1, source_target_pairs={{0,14},{1,15},{2,4},{3,5},{4,2},{5,3},{6,8},{7,9},{8,6},{9,7},{10,... | collective-permute-start | bytes 589832 | tf_op jit(solution)/shard_map/ppermute | solution.py:180
  14.6 6.8 %collective-permute-start.2 = (bf16[64,1536]{1,0:T(8,128)(2,1)S(1)}, bf16[64,1536]{1,0:T(8,128)(2,1)S(1)}, u32[]{:S(2)}, u32[]{:S(2)}) collective-permute-start(bf16[64,1536]{1,0:T(8,128)(2,1)S(1)} %collective-permute-done.1.refs_1_.refs_2_), channel_id=1, source_target_pairs={{0,2},{1,3},{2,0},{3,1},{4,6},{5,7},{6,4},{7,5},{8,10},{9,11},{10,... | collective-permute-start | bytes 589832 | tf_op jit(solution)/shard_map/ppermute | solution.py:180
  14.7 8.0 %collective-permute-start.3 = (bf16[64,1536]{1,0:T(8,128)(2,1)S(1)}, bf16[64,1536]{1,0:T(8,128)(2,1)S(1)}, u32[]{:S(2)}, u32[]{:S(2)}) collective-permute-start(bf16[64,1536]{1,0:T(8,128)(2,1)S(1)} %collective-permute-done.refs_0_.refs_1_), channel_id=1, source_target_pairs={{0,14},{1,15},{2,4},{3,5},{4,2},{5,3},{6,8},{7,9},{8,6},{9,7},{10,... | collective-permute-start | bytes 589832 | tf_op jit(solution)/shard_map/ppermute | solution.py:180
  22.8 7.6 %collective-permute-start.4 = (bf16[64,1536]{1,0:T(8,128)(2,1)S(1)}, bf16[64,1536]{1,0:T(8,128)(2,1)S(1)}, u32[]{:S(2)}, u32[]{:S(2)}) collective-permute-start(bf16[64,1536]{1,0:T(8,128)(2,1)S(1)} %collective-permute-done.3.refs_1_), channel_id=1, source_target_pairs={{0,2},{1,3},{2,0},{3,1},{4,6},{5,7},{6,4},{7,5},{8,10},{9,11},{10,... | collective-permute-start | bytes 589832 | tf_op jit(solution)/shard_map/ppermute | solution.py:180
  23.2 7.2 %collective-permute-start.5 = (bf16[64,1536]{1,0:T(8,128)(2,1)S(1)}, bf16[64,1536]{1,0:T(8,128)(2,1)S(1)}, u32[]{:S(2)}, u32[]{:S(2)}) collective-permute-start(bf16[64,1536]{1,0:T(8,128)(2,1)S(1)} %collective-permute-done.2.refs_0_), channel_id=1, source_target_pairs={{0,14},{1,15},{2,4},{3,5},{4,2},{5,3},{6,8},{7,9},{8,6},{9,7},{10,... | collective-permute-start | bytes 589832 | tf_op jit(solution)/shard_map/ppermute | solution.py:180
  30.4 5.9 %collective-permute-start.10 = (bf16[32,1536]{1,0:T(8,128)(2,1)S(1)}, bf16[32,1536]{1,0:T(8,128)(2,1)S(1)}, u32[]{:S(2)}, u32[]{:S(2)}) collective-permute-start(bf16[32,1536]{1,0:T(8,128)(2,1)S(1)} %slice.7), channel_id=1, source_target_pairs={{0,14},{1,15},{2,4},{3,5},{4,2},{5,3},{6,8},{7,9},{8,6},{9,7},{10,... | collective-permute-start | bytes 294920 | tf_op jit(solution)/shard_map/ppermute | solution.py:180
  32.4 5.3 %collective-permute-start.9 = (bf16[32,1536]{1,0:T(8,128)(2,1)S(1)}, bf16[32,1536]{1,0:T(8,128)(2,1)S(1)}, u32[]{:S(2)}, u32[]{:S(2)}) collective-permute-start(bf16[32,1536]{1,0:T(8,128)(2,1)S(1)} %slice.6), channel_id=1, source_target_pairs={{0,2},{1,3},{2,0},{3,1},{4,6},{5,7},{6,4},{7,5},{8,10},{9,11},{10,... | collective-permute-start | bytes 294920 | tf_op jit(solution)/shard_map/ppermute | solution.py:180
  37.6 11.4 %collective-permute-start.12 = (bf16[64,1440]{1,0:T(8,128)(2,1)S(1)}, bf16[64,1440]{1,0:T(8,128)(2,1)S(1)}, u32[]{:S(2)}, u32[]{:S(2)}) collective-permute-start(bf16[64,1440]{1,0:T(8,128)(2,1)S(1)} %get-tuple-element.82), channel_id=1, source_target_pairs={{0,2},{1,3},{2,0},{3,1},{4,6},{5,7},{6,4},{7,5},{8,10},{9,11},{10,... | collective-permute-start | bytes 552968 | tf_op jit(solution)/shard_map/ppermute | solution.py:180
  38.4 10.6 %collective-permute-start.13 = (bf16[64,1440]{1,0:T(8,128)(2,1)S(1)}, bf16[64,1440]{1,0:T(8,128)(2,1)S(1)}, u32[]{:S(2)}, u32[]{:S(2)}) collective-permute-start(bf16[64,1440]{1,0:T(8,128)(2,1)S(1)} %get-tuple-element.83), channel_id=1, source_target_pairs={{0,14},{1,15},{2,4},{3,5},{4,2},{5,3},{6,8},{7,9},{8,6},{9,7},{10,... | collective-permute-start | bytes 552968 | tf_op jit(solution)/shard_map/ppermute | solution.py:180
  45.7 16.8 %collective-permute-start.11 = (bf16[64,1440]{1,0:T(8,128)(2,1)S(1)}, bf16[64,1440]{1,0:T(8,128)(2,1)S(1)}, u32[]{:S(2)}, u32[]{:S(2)}) collective-permute-start(bf16[64,1440]{1,0:T(8,128)(2,1)S(1)} %experts.12), channel_id=1, source_target_pairs={{0,8},{1,9},{2,10},{3,11},{4,12},{5,13},{6,14},{7,15},{8,0},{9,1},... | collective-permute-start | bytes 552968 | tf_op jit(solution)/shard_map/ppermute | solution.py:180
  49.1 10.7 %collective-permute-start.14 = (bf16[64,1440]{1,0:T(8,128)(2,1)S(1)}, bf16[64,1440]{1,0:T(8,128)(2,1)S(1)}, u32[]{:S(2)}, u32[]{:S(2)}) collective-permute-start(bf16[64,1440]{1,0:T(8,128)(2,1)S(1)} %add_convert_fusion.4), channel_id=1, source_target_pairs={{0,14},{1,15},{2,4},{3,5},{4,2},{5,3},{6,8},{7,9},{8,6},{9,7},{10,... | collective-permute-start | bytes 552968 | tf_op jit(solution)/shard_map/ppermute | solution.py:180
  50.6 10.0 %collective-permute-start.16 = (bf16[64,1440]{1,0:T(8,128)(2,1)S(1)}, bf16[64,1440]{1,0:T(8,128)(2,1)S(1)}, u32[]{:S(2)}, u32[]{:S(2)}) collective-permute-start(bf16[64,1440]{1,0:T(8,128)(2,1)S(1)} %add_convert_fusion.2), channel_id=1, source_target_pairs={{0,2},{1,3},{2,0},{3,1},{4,6},{5,7},{6,4},{7,5},{8,10},{9,11},{10,... | collective-permute-start | bytes 552968 | tf_op jit(solution)/shard_map/ppermute | solution.py:180
  59.8 5.8 %collective-permute-start.15 = (bf16[64,1440]{1,0:T(8,128)(2,1)S(1)}, bf16[64,1440]{1,0:T(8,128)(2,1)S(1)}, u32[]{:S(2)}, u32[]{:S(2)}) collective-permute-start(bf16[64,1440]{1,0:T(8,128)(2,1)S(1)} %add_convert_fusion.3), channel_id=1, source_target_pairs={{0,2},{1,3},{2,0},{3,1},{4,6},{5,7},{6,4},{7,5},{8,10},{9,11},{10,... | collective-permute-start | bytes 552968 | tf_op jit(solution)/shard_map/ppermute | solution.py:180
  60.6 7.0 %collective-permute-start.17 = (bf16[64,1440]{1,0:T(8,128)(2,1)S(1)}, bf16[64,1440]{1,0:T(8,128)(2,1)S(1)}, u32[]{:S(2)}, u32[]{:S(2)}) collective-permute-start(bf16[64,1440]{1,0:T(8,128)(2,1)S(1)} %add_convert_fusion.1), channel_id=1, source_target_pairs={{0,14},{1,15},{2,4},{3,5},{4,2},{5,3},{6,8},{7,9},{8,6},{9,7},{10,... | collective-permute-start | bytes 552968 | tf_op jit(solution)/shard_map/ppermute | solution.py:180

commit v4 on v3

--- a/solution.py
+++ b/solution.py
@@ -199,20 +199,19 @@
     p1 = experts_apply(experts, [e1, o1], near, None, [], rows, F32)
     e2, o2, p1 = fence((e2, o2, p1))
     e3, o3 = send(o2, even), send(e2, odd)
-    p2 = experts_apply(experts, [e2, o2], near, None, [], rows, F32)
-    p2, p1, far = fence((p2, p1, far))
-    t0, te1, to1 = experts_apply(experts, [own, e1, o1], None, far, [*p0, *p1], rows, BF16)
-    e3, o3, p2, t0 = fence((e3, o3, p2, t0))
+    te2, to2 = experts_apply(experts, [e2, o2], near, far, [], rows, BF16)
+    e3, o3, te2, to2 = fence((e3, o3, te2, to2))
     e4, o4 = send(o3[:half], even), send(e3[half:], odd)
     te3, to3 = experts_apply(experts, [e3, o3], near, far, [], rows, BF16)
     te3, to3, e4, o4 = fence((te3, to3, e4, o4))
     re, ro = send(te3, even), send(to3, odd)
     (t4,) = experts_apply(experts, [e4, o4], near, far, [], rows, BF16)
+    te2, to2, t4, p0, p1 = fence((add(te2, ro), add(to2, re), t4, p0, p1))
+    re, ro = send(te2, even), send(to2, odd)
     r4 = send(t4, across)
-    te2, to2 = experts_apply(experts, [e2, o2], None, far, p2, rows, BF16)
-    te2, to2, re, ro = fence((te2, to2, re, ro))
-    re, ro = send(add(te2, ro), even), send(add(to2, re), odd)
-    re, ro = send(add(te1, ro), even), send(add(to1, re), odd)
+    t0, te1, to1 = experts_apply(experts, [own, e1, o1], None, far, [*p0, *p1], rows, BF16)
+    te1, to1, t0 = fence((add(te1, ro), add(to1, re), t0))
+    re, ro = send(te1, even), send(to1, odd)
     return add(t0, r4, re, ro)
 
 

time: 68.5 us -> 66.8 us (0.975)
  waiting for transfers between devices: 18.9 us -> 16.3 us
  starting transfers between devices: 24.5 us -> 25.6 us
    ppermute x18, waiting for transfers between devices: 18.9 us -> 16.3 us  [send(): return lax.ppermute(x, 'ep', pairs)]
    ppermute x18, starting transfers between devices: 24.5 us -> 25.6 us  [send(): return lax.ppermute(x, 'ep', pairs)]
    pallas_call x7 -> x6, Pallas kernels: 22.1 us -> 22 us  [experts_apply(): pl.pallas_call(body, out_shape=out_shape, in_specs=[vmem] * (count + len(...]
  transfers between devices with their start and end apart: 18 -> 18, of which waited for: 6 -> 9; matrix products, arithmetic and copies ran while one was open for 0% -> 0% of each run, Pallas kernels for 34% -> 34%
where the time goes in v4:
time: 66.8 us; the launch traced here: 66.7 us
  starting transfers between devices  25.6 us (38%)
  Pallas kernels  23 us (34%)
  waiting for transfers between devices  16.3 us (24%)
  other arithmetic  0.97 us (1%)
  between operations  0.8 us (1%)
    ppermute x18, starting transfers between devices, send(): return lax.ppermute(x, 'ep', pairs)  25.6 us
    pallas_call x6, Pallas kernels, experts_apply(): pl.pallas_call(body, out_shape=out_shape, in_specs=[vmem] * (count + len(...  22 us
    ppermute x18, waiting for transfers between devices, send(): return lax.ppermute(x, 'ep', pairs)  16.3 us
  transfers between devices with their start and end apart: 18, of which 9 were waited for; matrix products, arithmetic and copies ran while one was open for 0% of the time, Pallas kernels for 34%

profile of v4, /device:TPU:26, one launch (start us, length us, event | category | flops | bytes accessed | tf_op | source)
XLA Modules:
  0.0 66.7 jit_solution(14374073773738251284)
XLA Ops:
  0.0 0.0 collective-permute-start.6
  0.0 0.5 collective-permute-start.7
  0.5 0.0 collective-permute-start.8
  1.2 1.0 %route.1.refs_0_ = bf16[64,1536]{1,0:T(8,128)(2,1)S(1)} custom-call(s32[1]{0:T(128)S(6)} %copy.8.refs_0_, bf16[64,1440]{1,0:T(8,128)(2,1)} %refs_1_.2, s32[4,64]{1,0:T(4,128)} %bitcast.8, f32[4,64]{1,0:T(4,128)} %bitcast.9), custom_call_target="tpu_custom_call" | custom-call | tf_op jit(solution)/shard_map/route/pallas_call | solution.py:183
  2.2 2.0 %collective-permute-start = (bf16[64,1536]{1,0:T(8,128)(2,1)S(1)}, bf16[64,1536]{1,0:T(8,128)(2,1)S(1)}, u32[]{:S(2)}, u32[]{:S(2)}) collective-permute-start(bf16[64,1536]{1,0:T(8,128)(2,1)S(1)} %route.1.refs_0_), channel_id=1, source_target_pairs={{0,2},{1,3},{2,0},{3,1},{4,6},{5,7},{6,4},{7,5},{8,10},{9,11},{10,... | collective-permute-start | bytes 589832 | tf_op jit(solution)/shard_map/ppermute | solution.py:180
  4.2 4.9 %collective-permute-start.1 = (bf16[64,1536]{1,0:T(8,128)(2,1)S(1)}, bf16[64,1536]{1,0:T(8,128)(2,1)S(1)}, u32[]{:S(2)}, u32[]{:S(2)}) collective-permute-start(bf16[64,1536]{1,0:T(8,128)(2,1)S(1)} %route.1.refs_0_), channel_id=1, source_target_pairs={{0,14},{1,15},{2,4},{3,5},{4,2},{5,3},{6,8},{7,9},{8,6},{9,7},{10,... | collective-permute-start | bytes 589832 | tf_op jit(solution)/shard_map/ppermute | solution.py:180
  9.2 5.4 %experts.6 = (f32[64,1440]{1,0:T(8,128)S(1)}, bf16[1440,1440]{1,0:T(8,128)(2,1)S(1)}, bf16[1440,1440]{1,0:T(8,128)(2,1)S(1)}, bf16[1440,1440]{1,0:T(8,128)(2,1)S(1)}) custom-call(bf16[64,1536]{1,0:T(8,128)(2,1)S(1)} %route.1.refs_0_, bf16[1,1440,1440]{2,1,0:T(8,128)(2,1)} %refs_1_.3, bf16[1,1440,1440]{2,1,0:T(8,128)(2,1)} %refs_2_.1, ...), custom_call_target="tpu_custom_call" | custom-call | flops 796262400 | bytes 368640 | tf_op jit(solution)/shard_map/experts/pallas_call | solution.py:142
  14.6 0.0 collective-permute-done.refs_0_.refs_1_
  14.6 0.0 collective-permute-done.1.refs_1_.refs_2_
  14.6 0.1 collective-permute-start.2
  14.7 2.7 %collective-permute-start.3 = (bf16[64,1536]{1,0:T(8,128)(2,1)S(1)}, bf16[64,1536]{1,0:T(8,128)(2,1)S(1)}, u32[]{:S(2)}, u32[]{:S(2)}) collective-permute-start(bf16[64,1536]{1,0:T(8,128)(2,1)S(1)} %collective-permute-done.refs_0_.refs_1_), channel_id=1, source_target_pairs={{0,14},{1,15},{2,4},{3,5},{4,2},{5,3},{6,8},{7,9},{8,6},{9,7},{10,... | collective-permute-start | bytes 589832 | tf_op jit(solution)/shard_map/ppermute | solution.py:180
  17.4 2.0 %experts.7 = (f32[64,1440]{1,0:T(8,128)S(1)}, f32[64,1440]{1,0:T(8,128)S(1)}) custom-call(bf16[64,1536]{1,0:T(8,128)(2,1)S(1)} %collective-permute-done.refs_0_.refs_1_, bf16[64,1536]{1,0:T(8,128)(2,1)S(1)} %collective-permute-done.1.refs_1_.refs_2_, bf16[1440,1440]{1,0:T(8,128)(2,1)S(1)} %get-tuple-element.45.refs_2_, ...), custom_call_target="tpu_custom_call" | custom-call | flops 1592524800 | bytes 737280 | tf_op jit(solution)/shard_map/experts/pallas_call | solution.py:142
  19.4 2.0 %collective-permute-done.2.refs_0_ = bf16[64,1536]{1,0:T(8,128)(2,1)S(1)} collective-permute-done((bf16[64,1536]{1,0:T(8,128)(2,1)S(1)}, bf16[64,1536]{1,0:T(8,128)(2,1)S(1)}, u32[]{:S(2)}, u32[]{:S(2)}) %collective-permute-start.2) | collective-permute-done | bytes 196640 | tf_op jit(solution)/shard_map/ppermute | solution.py:180
  21.5 1.3 %collective-permute-done.3.refs_1_ = bf16[64,1536]{1,0:T(8,128)(2,1)S(1)} collective-permute-done((bf16[64,1536]{1,0:T(8,128)(2,1)S(1)}, bf16[64,1536]{1,0:T(8,128)(2,1)S(1)}, u32[]{:S(2)}, u32[]{:S(2)}) %collective-permute-start.3) | collective-permute-done | bytes 196640 | tf_op jit(solution)/shard_map/ppermute | solution.py:180
  22.8 0.4 collective-permute-start.4
  23.2 2.2 %collective-permute-start.5 = (bf16[64,1536]{1,0:T(8,128)(2,1)S(1)}, bf16[64,1536]{1,0:T(8,128)(2,1)S(1)}, u32[]{:S(2)}, u32[]{:S(2)}) collective-permute-start(bf16[64,1536]{1,0:T(8,128)(2,1)S(1)} %collective-permute-done.2.refs_0_), channel_id=1, source_target_pairs={{0,14},{1,15},{2,4},{3,5},{4,2},{5,3},{6,8},{7,9},{8,6},{9,7},{10,... | collective-permute-start | bytes 589832 | tf_op jit(solution)/shard_map/ppermute | solution.py:180
  25.4 0.0 collective-permute-done.6.refs_5_.refs_6_
  25.4 0.0 collective-permute-done.7.refs_6_.refs_7_
  25.4 0.0 collective-permute-done.8.refs_7_.refs_8_
  25.4 3.9 %experts.8 = (bf16[64,1440]{1,0:T(8,128)(2,1)S(1)}, bf16[64,1440]{1,0:T(8,128)(2,1)S(1)}) custom-call(bf16[64,1536]{1,0:T(8,128)(2,1)S(1)} %collective-permute-done.2.refs_0_, bf16[64,1536]{1,0:T(8,128)(2,1)S(1)} %collective-permute-done.3.refs_1_, bf16[1440,1440]{1,0:T(8,128)(2,1)S(1)} %get-tuple-element.45.refs_2_, ...), custom_call_target="tpu_custom_call" | custom-call | flops 3185049600 | bytes 737280 | tf_op jit(solution)/shard_map/experts/pallas_call | solution.py:142
  29.2 0.0 collective-permute-done.4.refs_0_
  29.3 0.8 %collective-permute-done.5.refs_1_ = bf16[64,1536]{1,0:T(8,128)(2,1)S(1)} collective-permute-done((bf16[64,1536]{1,0:T(8,128)(2,1)S(1)}, bf16[64,1536]{1,0:T(8,128)(2,1)S(1)}, u32[]{:S(2)}, u32[]{:S(2)}) %collective-permute-start.5) | collective-permute-done | bytes 196640 | tf_op jit(solution)/shard_map/ppermute | solution.py:180
  30.1 2.2 %collective-permute-start.10 = (bf16[32,1536]{1,0:T(8,128)(2,1)S(1)}, bf16[32,1536]{1,0:T(8,128)(2,1)S(1)}, u32[]{:S(2)}, u32[]{:S(2)}) collective-permute-start(bf16[32,1536]{1,0:T(8,128)(2,1)S(1)} %slice.7), channel_id=1, source_target_pairs={{0,14},{1,15},{2,4},{3,5},{4,2},{5,3},{6,8},{7,9},{8,6},{9,7},{10,... | collective-permute-start | bytes 294920 | tf_op jit(solution)/shard_map/ppermute | solution.py:180
  32.4 0.1 collective-permute-start.9
  32.5 3.9 %experts.9 = (bf16[64,1440]{1,0:T(8,128)(2,1)S(1)}, bf16[64,1440]{1,0:T(8,128)(2,1)S(1)}) custom-call(bf16[64,1536]{1,0:T(8,128)(2,1)S(1)} %collective-permute-done.4.refs_0_, bf16[64,1536]{1,0:T(8,128)(2,1)S(1)} %collective-permute-done.5.refs_1_, bf16[1440,1440]{1,0:T(8,128)(2,1)S(1)} %get-tuple-element.45.refs_2_, ...), custom_call_target="tpu_custom_call" | custom-call | flops 3185049600 | bytes 737280 | tf_op jit(solution)/shard_map/experts/pallas_call | solution.py:142
  36.3 0.0 collective-permute-done.10.refs_1_
  36.3 1.1 %collective-permute-done.9.refs_0_ = bf16[32,1536]{1,0:T(8,128)(2,1)S(1)} collective-permute-done((bf16[32,1536]{1,0:T(8,128)(2,1)S(1)}, bf16[32,1536]{1,0:T(8,128)(2,1)S(1)}, u32[]{:S(2)}, u32[]{:S(2)}) %collective-permute-start.9) | collective-permute-done | bytes 98336 | tf_op jit(solution)/shard_map/ppermute | solution.py:180
  37.4 1.0 %collective-permute-start.12 = (bf16[64,1440]{1,0:T(8,128)(2,1)S(1)}, bf16[64,1440]{1,0:T(8,128)(2,1)S(1)}, u32[]{:S(2)}, u32[]{:S(2)}) collective-permute-start(bf16[64,1440]{1,0:T(8,128)(2,1)S(1)} %get-tuple-element.61), channel_id=1, source_target_pairs={{0,2},{1,3},{2,0},{3,1},{4,6},{5,7},{6,4},{7,5},{8,10},{9,11},{10,... | collective-permute-start | bytes 552968 | tf_op jit(solution)/shard_map/ppermute | solution.py:180
  38.4 1.1 %collective-permute-start.11 = (bf16[64,1440]{1,0:T(8,128)(2,1)S(1)}, bf16[64,1440]{1,0:T(8,128)(2,1)S(1)}, u32[]{:S(2)}, u32[]{:S(2)}) collective-permute-start(bf16[64,1440]{1,0:T(8,128)(2,1)S(1)} %get-tuple-element.59), channel_id=1, source_target_pairs={{0,14},{1,15},{2,4},{3,5},{4,2},{5,3},{6,8},{7,9},{8,6},{9,7},{10,... | collective-permute-start | bytes 552968 | tf_op jit(solution)/shard_map/ppermute | solution.py:180
  39.5 3.9 %experts.10 = bf16[64,1440]{1,0:T(8,128)(2,1)S(1)} custom-call(bf16[32,1536]{1,0:T(8,128)(2,1)S(1)} %collective-permute-done.9.refs_0_, bf16[32,1536]{1,0:T(8,128)(2,1)S(1)} %collective-permute-done.10.refs_1_, bf16[1440,1440]{1,0:T(8,128)(2,1)S(1)} %get-tuple-element.45.refs_2_, bf16[1440,1440]{1,0:T(8,128)(2,1)S(1)} %get-tuple-element.46.refs_3_, ...), custom_call_target="tpu_custom_call" | custom-call | flops 1592524800 | bytes 368640 | tf_op jit(solution)/shard_map/experts/pallas_call | solution.py:142
  43.4 0.0 collective-permute-done.12
  43.5 1.9 %collective-permute-done.11 = bf16[64,1440]{1,0:T(8,128)(2,1)S(1)} collective-permute-done((bf16[64,1440]{1,0:T(8,128)(2,1)S(1)}, bf16[64,1440]{1,0:T(8,128)(2,1)S(1)}, u32[]{:S(2)}, u32[]{:S(2)}) %collective-permute-start.11) | collective-permute-done | bytes 184352 | tf_op jit(solution)/shard_map/ppermute | solution.py:180
  45.4 0.1 collective-permute-start.14
  45.5 1.2 %collective-permute-start.13 = (bf16[64,1440]{1,0:T(8,128)(2,1)S(1)}, bf16[64,1440]{1,0:T(8,128)(2,1)S(1)}, u32[]{:S(2)}, u32[]{:S(2)}) collective-permute-start(bf16[64,1440]{1,0:T(8,128)(2,1)S(1)} %add_convert_fusion.3), channel_id=1, source_target_pairs={{0,14},{1,15},{2,4},{3,5},{4,2},{5,3},{6,8},{7,9},{8,6},{9,7},{10,... | collective-permute-start | bytes 552968 | tf_op jit(solution)/shard_map/ppermute | solution.py:180
  46.6 3.5 %collective-permute-start.15 = (bf16[64,1440]{1,0:T(8,128)(2,1)S(1)}, bf16[64,1440]{1,0:T(8,128)(2,1)S(1)}, u32[]{:S(2)}, u32[]{:S(2)}) collective-permute-start(bf16[64,1440]{1,0:T(8,128)(2,1)S(1)} %experts.10), channel_id=1, source_target_pairs={{0,8},{1,9},{2,10},{3,11},{4,12},{5,13},{6,14},{7,15},{8,0},{9,1},... | collective-permute-start | bytes 552968 | tf_op jit(solution)/shard_map/ppermute | solution.py:180
  50.1 2.9 %experts.11 = (bf16[64,1440]{1,0:T(8,128)(2,1)S(1)}, bf16[64,1440]{1,0:T(8,128)(2,1)S(1)}, bf16[64,1440]{1,0:T(8,128)(2,1)S(1)}) custom-call(bf16[64,1536]{1,0:T(8,128)(2,1)S(1)} %route.1.refs_0_, bf16[64,1536]{1,0:T(8,128)(2,1)S(1)} %collective-permute-done.refs_0_.refs_1_, bf16[64,1536]{1,0:T(8,128)(2,1)S(1)} %collective-permute-done.1.refs_1_.refs_2_, ...), custom_call_target="tpu_custom_call" | custom-call | flops 2388787200 | bytes 1105920 | tf_op jit(solution)/shard_map/experts/pallas_call | solution.py:142
  53.1 1.6 %collective-permute-done.14 = bf16[64,1440]{1,0:T(8,128)(2,1)S(1)} collective-permute-done((bf16[64,1440]{1,0:T(8,128)(2,1)S(1)}, bf16[64,1440]{1,0:T(8,128)(2,1)S(1)}, u32[]{:S(2)}, u32[]{:S(2)}) %collective-permute-start.14) | collective-permute-done | bytes 184352 | tf_op jit(solution)/shard_map/ppermute | solution.py:180
  54.7 3.2 %collective-permute-done.13 = bf16[64,1440]{1,0:T(8,128)(2,1)S(1)} collective-permute-done((bf16[64,1440]{1,0:T(8,128)(2,1)S(1)}, bf16[64,1440]{1,0:T(8,128)(2,1)S(1)}, u32[]{:S(2)}, u32[]{:S(2)}) %collective-permute-start.13) | collective-permute-done | bytes 184352 | tf_op jit(solution)/shard_map/ppermute | solution.py:180
  57.9 1.2 %collective-permute-start.16 = (bf16[64,1440]{1,0:T(8,128)(2,1)S(1)}, bf16[64,1440]{1,0:T(8,128)(2,1)S(1)}, u32[]{:S(2)}, u32[]{:S(2)}) collective-permute-start(bf16[64,1440]{1,0:T(8,128)(2,1)S(1)} %add_convert_fusion.2), channel_id=1, source_target_pairs={{0,2},{1,3},{2,0},{3,1},{4,6},{5,7},{6,4},{7,5},{8,10},{9,11},{10,... | collective-permute-start | bytes 552968 | tf_op jit(solution)/shard_map/ppermute | solution.py:180
  59.1 2.4 %collective-permute-start.17 = (bf16[64,1440]{1,0:T(8,128)(2,1)S(1)}, bf16[64,1440]{1,0:T(8,128)(2,1)S(1)}, u32[]{:S(2)}, u32[]{:S(2)}) collective-permute-start(bf16[64,1440]{1,0:T(8,128)(2,1)S(1)} %add_convert_fusion.1), channel_id=1, source_target_pairs={{0,14},{1,15},{2,4},{3,5},{4,2},{5,3},{6,8},{7,9},{8,6},{9,7},{10,... | collective-permute-start | bytes 552968 | tf_op jit(solution)/shard_map/ppermute | solution.py:180
  61.5 0.0 collective-permute-done.15
  61.5 2.1 %collective-permute-done.16 = bf16[64,1440]{1,0:T(8,128)(2,1)S(1)} collective-permute-done((bf16[64,1440]{1,0:T(8,128)(2,1)S(1)}, bf16[64,1440]{1,0:T(8,128)(2,1)S(1)}, u32[]{:S(2)}, u32[]{:S(2)}) %collective-permute-start.16) | collective-permute-done | bytes 184352 | tf_op jit(solution)/shard_map/ppermute | solution.py:180
  63.7 2.3 %collective-permute-done.17 = bf16[64,1440]{1,0:T(8,128)(2,1)S(1)} collective-permute-done((bf16[64,1440]{1,0:T(8,128)(2,1)S(1)}, bf16[64,1440]{1,0:T(8,128)(2,1)S(1)}, u32[]{:S(2)}, u32[]{:S(2)}) %collective-permute-start.17) | collective-permute-done | bytes 184352 | tf_op jit(solution)/shard_map/ppermute | solution.py:180
  66.0 0.8 %add_convert_fusion = bf16[64,1440]{1,0:T(8,128)(2,1)} fusion(bf16[64,1440]{1,0:T(8,128)(2,1)S(1)} %collective-permute-done.17, bf16[64,1440]{1,0:T(8,128)(2,1)S(1)} %collective-permute-done.16, bf16[64,1440]{1,0:T(8,128)(2,1)S(1)} %collective-permute-done.15, bf16[64,1440]{1,0:T(8,128)(2,1)S(1)} %get-tuple-element.75), kind=kLoop, calls=%fused_computation | loop fusion | flops 737280 | bytes 921600 | tf_op jit(solution)/shard_map/convert_element_type | solution.py:169
  (6 shorter events, 0.2 us)
Async XLA Ops:
  0.0 25.4 %collective-permute-start.6 = (bf16[1440,1440]{1,0:T(8,128)(2,1)}, bf16[1440,1440]{1,0:T(8,128)(2,1)S(1)}, u32[]{:S(2)}, u32[]{:S(2)}) collective-permute-start(bf16[1440,1440]{1,0:T(8,128)(2,1)} %bitcast.5), channel_id=1, source_target_pairs={{0,1},{1,0},{2,3},{3,2},{4,5},{5,4},{6,7},{7,6},{8,9},{9,8},{10,11... | collective-permute-start | bytes 12441608 | tf_op jit(solution)/shard_map/ppermute | solution.py:180
  0.0 25.4 %collective-permute-start.7 = (bf16[1440,1440]{1,0:T(8,128)(2,1)}, bf16[1440,1440]{1,0:T(8,128)(2,1)S(1)}, u32[]{:S(2)}, u32[]{:S(2)}) collective-permute-start(bf16[1440,1440]{1,0:T(8,128)(2,1)} %bitcast.6), channel_id=1, source_target_pairs={{0,1},{1,0},{2,3},{3,2},{4,5},{5,4},{6,7},{7,6},{8,9},{9,8},{10,11... | collective-permute-start | bytes 12441608 | tf_op jit(solution)/shard_map/ppermute | solution.py:180
  0.5 24.9 %collective-permute-start.8 = (bf16[1440,1440]{1,0:T(8,128)(2,1)}, bf16[1440,1440]{1,0:T(8,128)(2,1)S(1)}, u32[]{:S(2)}, u32[]{:S(2)}) collective-permute-start(bf16[1440,1440]{1,0:T(8,128)(2,1)} %bitcast.7), channel_id=1, source_target_pairs={{0,1},{1,0},{2,3},{3,2},{4,5},{5,4},{6,7},{7,6},{8,9},{9,8},{10,11... | collective-permute-start | bytes 12441608 | tf_op jit(solution)/shard_map/ppermute | solution.py:180
  2.2 12.4 %collective-permute-start = (bf16[64,1536]{1,0:T(8,128)(2,1)S(1)}, bf16[64,1536]{1,0:T(8,128)(2,1)S(1)}, u32[]{:S(2)}, u32[]{:S(2)}) collective-permute-start(bf16[64,1536]{1,0:T(8,128)(2,1)S(1)} %route.1.refs_0_), channel_id=1, source_target_pairs={{0,2},{1,3},{2,0},{3,1},{4,6},{5,7},{6,4},{7,5},{8,10},{9,11},{10,... | collective-permute-start | bytes 589832 | tf_op jit(solution)/shard_map/ppermute | solution.py:180
  4.2 10.4 %collective-permute-start.1 = (bf16[64,1536]{1,0:T(8,128)(2,1)S(1)}, bf16[64,1536]{1,0:T(8,128)(2,1)S(1)}, u32[]{:S(2)}, u32[]{:S(2)}) collective-permute-start(bf16[64,1536]{1,0:T(8,128)(2,1)S(1)} %route.1.refs_0_), channel_id=1, source_target_pairs={{0,14},{1,15},{2,4},{3,5},{4,2},{5,3},{6,8},{7,9},{8,6},{9,7},{10,... | collective-permute-start | bytes 589832 | tf_op jit(solution)/shard_map/ppermute | solution.py:180
  14.6 6.8 %collective-permute-start.2 = (bf16[64,1536]{1,0:T(8,128)(2,1)S(1)}, bf16[64,1536]{1,0:T(8,128)(2,1)S(1)}, u32[]{:S(2)}, u32[]{:S(2)}) collective-permute-start(bf16[64,1536]{1,0:T(8,128)(2,1)S(1)} %collective-permute-done.1.refs_1_.refs_2_), channel_id=1, source_target_pairs={{0,2},{1,3},{2,0},{3,1},{4,6},{5,7},{6,4},{7,5},{8,10},{9,11},{10,... | collective-permute-start | bytes 589832 | tf_op jit(solution)/shard_map/ppermute | solution.py:180
  14.7 8.0 %collective-permute-start.3 = (bf16[64,1536]{1,0:T(8,128)(2,1)S(1)}, bf16[64,1536]{1,0:T(8,128)(2,1)S(1)}, u32[]{:S(2)}, u32[]{:S(2)}) collective-permute-start(bf16[64,1536]{1,0:T(8,128)(2,1)S(1)} %collective-permute-done.refs_0_.refs_1_), channel_id=1, source_target_pairs={{0,14},{1,15},{2,4},{3,5},{4,2},{5,3},{6,8},{7,9},{8,6},{9,7},{10,... | collective-permute-start | bytes 589832 | tf_op jit(solution)/shard_map/ppermute | solution.py:180
  22.8 6.5 %collective-permute-start.4 = (bf16[64,1536]{1,0:T(8,128)(2,1)S(1)}, bf16[64,1536]{1,0:T(8,128)(2,1)S(1)}, u32[]{:S(2)}, u32[]{:S(2)}) collective-permute-start(bf16[64,1536]{1,0:T(8,128)(2,1)S(1)} %collective-permute-done.3.refs_1_), channel_id=1, source_target_pairs={{0,2},{1,3},{2,0},{3,1},{4,6},{5,7},{6,4},{7,5},{8,10},{9,11},{10,... | collective-permute-start | bytes 589832 | tf_op jit(solution)/shard_map/ppermute | solution.py:180
  23.2 6.9 %collective-permute-start.5 = (bf16[64,1536]{1,0:T(8,128)(2,1)S(1)}, bf16[64,1536]{1,0:T(8,128)(2,1)S(1)}, u32[]{:S(2)}, u32[]{:S(2)}) collective-permute-start(bf16[64,1536]{1,0:T(8,128)(2,1)S(1)} %collective-permute-done.2.refs_0_), channel_id=1, source_target_pairs={{0,14},{1,15},{2,4},{3,5},{4,2},{5,3},{6,8},{7,9},{8,6},{9,7},{10,... | collective-permute-start | bytes 589832 | tf_op jit(solution)/shard_map/ppermute | solution.py:180
  30.1 6.2 %collective-permute-start.10 = (bf16[32,1536]{1,0:T(8,128)(2,1)S(1)}, bf16[32,1536]{1,0:T(8,128)(2,1)S(1)}, u32[]{:S(2)}, u32[]{:S(2)}) collective-permute-start(bf16[32,1536]{1,0:T(8,128)(2,1)S(1)} %slice.7), channel_id=1, source_target_pairs={{0,14},{1,15},{2,4},{3,5},{4,2},{5,3},{6,8},{7,9},{8,6},{9,7},{10,... | collective-permute-start | bytes 294920 | tf_op jit(solution)/shard_map/ppermute | solution.py:180
  32.4 5.1 %collective-permute-start.9 = (bf16[32,1536]{1,0:T(8,128)(2,1)S(1)}, bf16[32,1536]{1,0:T(8,128)(2,1)S(1)}, u32[]{:S(2)}, u32[]{:S(2)}) collective-permute-start(bf16[32,1536]{1,0:T(8,128)(2,1)S(1)} %slice.6), channel_id=1, source_target_pairs={{0,2},{1,3},{2,0},{3,1},{4,6},{5,7},{6,4},{7,5},{8,10},{9,11},{10,... | collective-permute-start | bytes 294920 | tf_op jit(solution)/shard_map/ppermute | solution.py:180
  37.4 6.0 %collective-permute-start.12 = (bf16[64,1440]{1,0:T(8,128)(2,1)S(1)}, bf16[64,1440]{1,0:T(8,128)(2,1)S(1)}, u32[]{:S(2)}, u32[]{:S(2)}) collective-permute-start(bf16[64,1440]{1,0:T(8,128)(2,1)S(1)} %get-tuple-element.61), channel_id=1, source_target_pairs={{0,2},{1,3},{2,0},{3,1},{4,6},{5,7},{6,4},{7,5},{8,10},{9,11},{10,... | collective-permute-start | bytes 552968 | tf_op jit(solution)/shard_map/ppermute | solution.py:180
  38.4 6.9 %collective-permute-start.11 = (bf16[64,1440]{1,0:T(8,128)(2,1)S(1)}, bf16[64,1440]{1,0:T(8,128)(2,1)S(1)}, u32[]{:S(2)}, u32[]{:S(2)}) collective-permute-start(bf16[64,1440]{1,0:T(8,128)(2,1)S(1)} %get-tuple-element.59), channel_id=1, source_target_pairs={{0,14},{1,15},{2,4},{3,5},{4,2},{5,3},{6,8},{7,9},{8,6},{9,7},{10,... | collective-permute-start | bytes 552968 | tf_op jit(solution)/shard_map/ppermute | solution.py:180
  45.4 9.3 %collective-permute-start.14 = (bf16[64,1440]{1,0:T(8,128)(2,1)S(1)}, bf16[64,1440]{1,0:T(8,128)(2,1)S(1)}, u32[]{:S(2)}, u32[]{:S(2)}) collective-permute-start(bf16[64,1440]{1,0:T(8,128)(2,1)S(1)} %add_convert_fusion.4), channel_id=1, source_target_pairs={{0,2},{1,3},{2,0},{3,1},{4,6},{5,7},{6,4},{7,5},{8,10},{9,11},{10,... | collective-permute-start | bytes 552968 | tf_op jit(solution)/shard_map/ppermute | solution.py:180
  45.5 12.4 %collective-permute-start.13 = (bf16[64,1440]{1,0:T(8,128)(2,1)S(1)}, bf16[64,1440]{1,0:T(8,128)(2,1)S(1)}, u32[]{:S(2)}, u32[]{:S(2)}) collective-permute-start(bf16[64,1440]{1,0:T(8,128)(2,1)S(1)} %add_convert_fusion.3), channel_id=1, source_target_pairs={{0,14},{1,15},{2,4},{3,5},{4,2},{5,3},{6,8},{7,9},{8,6},{9,7},{10,... | collective-permute-start | bytes 552968 | tf_op jit(solution)/shard_map/ppermute | solution.py:180
  46.6 14.9 %collective-permute-start.15 = (bf16[64,1440]{1,0:T(8,128)(2,1)S(1)}, bf16[64,1440]{1,0:T(8,128)(2,1)S(1)}, u32[]{:S(2)}, u32[]{:S(2)}) collective-permute-start(bf16[64,1440]{1,0:T(8,128)(2,1)S(1)} %experts.10), channel_id=1, source_target_pairs={{0,8},{1,9},{2,10},{3,11},{4,12},{5,13},{6,14},{7,15},{8,0},{9,1},... | collective-permute-start | bytes 552968 | tf_op jit(solution)/shard_map/ppermute | solution.py:180
  57.9 5.8 %collective-permute-start.16 = (bf16[64,1440]{1,0:T(8,128)(2,1)S(1)}, bf16[64,1440]{1,0:T(8,128)(2,1)S(1)}, u32[]{:S(2)}, u32[]{:S(2)}) collective-permute-start(bf16[64,1440]{1,0:T(8,128)(2,1)S(1)} %add_convert_fusion.2), channel_id=1, source_target_pairs={{0,2},{1,3},{2,0},{3,1},{4,6},{5,7},{6,4},{7,5},{8,10},{9,11},{10,... | collective-permute-start | bytes 552968 | tf_op jit(solution)/shard_map/ppermute | solution.py:180
  59.1 6.9 %collective-permute-start.17 = (bf16[64,1440]{1,0:T(8,128)(2,1)S(1)}, bf16[64,1440]{1,0:T(8,128)(2,1)S(1)}, u32[]{:S(2)}, u32[]{:S(2)}) collective-permute-start(bf16[64,1440]{1,0:T(8,128)(2,1)S(1)} %add_convert_fusion.1), channel_id=1, source_target_pairs={{0,14},{1,15},{2,4},{3,5},{4,2},{5,3},{6,8},{7,9},{8,6},{9,7},{10,... | collective-permute-start | bytes 552968 | tf_op jit(solution)/shard_map/ppermute | solution.py:180

commit v5 on v4

--- a/solution.py
+++ b/solution.py
@@ -201,11 +201,11 @@
     e3, o3 = send(o2, even), send(e2, odd)
     te2, to2 = experts_apply(experts, [e2, o2], near, far, [], rows, BF16)
     e3, o3, te2, to2 = fence((e3, o3, te2, to2))
-    e4, o4 = send(o3[:half], even), send(e3[half:], odd)
+    d4 = send(o3, even)
     te3, to3 = experts_apply(experts, [e3, o3], near, far, [], rows, BF16)
-    te3, to3, e4, o4 = fence((te3, to3, e4, o4))
+    te3, to3, d4 = fence((te3, to3, d4))
     re, ro = send(te3, even), send(to3, odd)
-    (t4,) = experts_apply(experts, [e4, o4], near, far, [], rows, BF16)
+    (t4,) = experts_apply(experts, [d4], near, far, [], rows, BF16)
     te2, to2, t4, p0, p1 = fence((add(te2, ro), add(to2, re), t4, p0, p1))
     re, ro = send(te2, even), send(to2, odd)
     r4 = send(t4, across)

time: 66.8 us -> 63 us (0.943)
  starting transfers between devices: 25.6 us -> 23.2 us
  waiting for transfers between devices: 16.3 us -> 15 us
    ppermute x18 -> x17, starting transfers between devices: 25.6 us -> 23.2 us  [send(): return lax.ppermute(x, 'ep', pairs)]
    ppermute x18 -> x17, waiting for transfers between devices: 16.3 us -> 15 us  [send(): return lax.ppermute(x, 'ep', pairs)]
  transfers between devices with their start and end apart: 18 -> 17, of which waited for: 9 -> 11; matrix products, arithmetic and copies ran while one was open for 0% -> 0% of each run, Pallas kernels for 34% -> 37%
where the time goes in v5:
time: 63 us; the launch traced here: 62.9 us
  starting transfers between devices  23.2 us (37%)
  Pallas kernels  23 us (37%)
  waiting for transfers between devices  15 us (24%)
  other arithmetic  0.97 us (2%)
  between operations  0.76 us (1%)
    ppermute x17, starting transfers between devices, send(): return lax.ppermute(x, 'ep', pairs)  23.2 us
    pallas_call x6, Pallas kernels, experts_apply(): pl.pallas_call(body, out_shape=out_shape, in_specs=[vmem] * (count + len(...  22 us
    ppermute x17, waiting for transfers between devices, send(): return lax.ppermute(x, 'ep', pairs)  15 us
  transfers between devices with their start and end apart: 17, of which 11 were waited for; matrix products, arithmetic and copies ran while one was open for 0% of the time, Pallas kernels for 37%

profile of v5, /device:TPU:26, one launch (start us, length us, event | category | flops | bytes accessed | tf_op | source)
XLA Modules:
  0.0 62.9 jit_solution(3620664585713674330)
XLA Ops:
  0.0 0.0 collective-permute-start.6
  0.0 0.5 collective-permute-start.7
  0.5 0.0 collective-permute-start.8
  1.2 1.0 %route.1.refs_0_ = bf16[64,1536]{1,0:T(8,128)(2,1)S(1)} custom-call(s32[1]{0:T(128)S(6)} %copy.8.refs_0_, bf16[64,1440]{1,0:T(8,128)(2,1)} %refs_1_.2, s32[4,64]{1,0:T(4,128)} %bitcast.8, f32[4,64]{1,0:T(4,128)} %bitcast.9), custom_call_target="tpu_custom_call" | custom-call | tf_op jit(solution)/shard_map/route/pallas_call | solution.py:183
  2.2 2.0 %collective-permute-start = (bf16[64,1536]{1,0:T(8,128)(2,1)S(1)}, bf16[64,1536]{1,0:T(8,128)(2,1)S(1)}, u32[]{:S(2)}, u32[]{:S(2)}) collective-permute-start(bf16[64,1536]{1,0:T(8,128)(2,1)S(1)} %route.1.refs_0_), channel_id=1, source_target_pairs={{0,2},{1,3},{2,0},{3,1},{4,6},{5,7},{6,4},{7,5},{8,10},{9,11},{10,... | collective-permute-start | bytes 589832 | tf_op jit(solution)/shard_map/ppermute | solution.py:180
  4.2 4.9 %collective-permute-start.1 = (bf16[64,1536]{1,0:T(8,128)(2,1)S(1)}, bf16[64,1536]{1,0:T(8,128)(2,1)S(1)}, u32[]{:S(2)}, u32[]{:S(2)}) collective-permute-start(bf16[64,1536]{1,0:T(8,128)(2,1)S(1)} %route.1.refs_0_), channel_id=1, source_target_pairs={{0,14},{1,15},{2,4},{3,5},{4,2},{5,3},{6,8},{7,9},{8,6},{9,7},{10,... | collective-permute-start | bytes 589832 | tf_op jit(solution)/shard_map/ppermute | solution.py:180
  9.2 5.4 %experts.6 = (f32[64,1440]{1,0:T(8,128)S(1)}, bf16[1440,1440]{1,0:T(8,128)(2,1)S(1)}, bf16[1440,1440]{1,0:T(8,128)(2,1)S(1)}, bf16[1440,1440]{1,0:T(8,128)(2,1)S(1)}) custom-call(bf16[64,1536]{1,0:T(8,128)(2,1)S(1)} %route.1.refs_0_, bf16[1,1440,1440]{2,1,0:T(8,128)(2,1)} %refs_1_.3, bf16[1,1440,1440]{2,1,0:T(8,128)(2,1)} %refs_2_.1, ...), custom_call_target="tpu_custom_call" | custom-call | flops 796262400 | bytes 368640 | tf_op jit(solution)/shard_map/experts/pallas_call | solution.py:142
  14.6 0.0 collective-permute-done.refs_0_.refs_1_
  14.6 0.0 collective-permute-done.1.refs_1_.refs_2_
  14.6 0.1 collective-permute-start.2
  14.7 2.7 %collective-permute-start.3 = (bf16[64,1536]{1,0:T(8,128)(2,1)S(1)}, bf16[64,1536]{1,0:T(8,128)(2,1)S(1)}, u32[]{:S(2)}, u32[]{:S(2)}) collective-permute-start(bf16[64,1536]{1,0:T(8,128)(2,1)S(1)} %collective-permute-done.refs_0_.refs_1_), channel_id=1, source_target_pairs={{0,14},{1,15},{2,4},{3,5},{4,2},{5,3},{6,8},{7,9},{8,6},{9,7},{10,... | collective-permute-start | bytes 589832 | tf_op jit(solution)/shard_map/ppermute | solution.py:180
  17.4 2.0 %experts.7 = (f32[64,1440]{1,0:T(8,128)S(1)}, f32[64,1440]{1,0:T(8,128)S(1)}) custom-call(bf16[64,1536]{1,0:T(8,128)(2,1)S(1)} %collective-permute-done.refs_0_.refs_1_, bf16[64,1536]{1,0:T(8,128)(2,1)S(1)} %collective-permute-done.1.refs_1_.refs_2_, bf16[1440,1440]{1,0:T(8,128)(2,1)S(1)} %get-tuple-element.44.refs_2_.refs_1_, ...), custom_call_target="tpu_custom_call" | custom-call | flops 1592524800 | bytes 737280 | tf_op jit(solution)/shard_map/experts/pallas_call | solution.py:142
  19.4 2.0 %collective-permute-done.2.refs_0_ = bf16[64,1536]{1,0:T(8,128)(2,1)S(1)} collective-permute-done((bf16[64,1536]{1,0:T(8,128)(2,1)S(1)}, bf16[64,1536]{1,0:T(8,128)(2,1)S(1)}, u32[]{:S(2)}, u32[]{:S(2)}) %collective-permute-start.2) | collective-permute-done | bytes 196640 | tf_op jit(solution)/shard_map/ppermute | solution.py:180
  21.5 1.3 %collective-permute-done.3.refs_1_ = bf16[64,1536]{1,0:T(8,128)(2,1)S(1)} collective-permute-done((bf16[64,1536]{1,0:T(8,128)(2,1)S(1)}, bf16[64,1536]{1,0:T(8,128)(2,1)S(1)}, u32[]{:S(2)}, u32[]{:S(2)}) %collective-permute-start.3) | collective-permute-done | bytes 196640 | tf_op jit(solution)/shard_map/ppermute | solution.py:180
  22.8 0.4 collective-permute-start.4
  23.2 2.2 %collective-permute-start.5 = (bf16[64,1536]{1,0:T(8,128)(2,1)S(1)}, bf16[64,1536]{1,0:T(8,128)(2,1)S(1)}, u32[]{:S(2)}, u32[]{:S(2)}) collective-permute-start(bf16[64,1536]{1,0:T(8,128)(2,1)S(1)} %collective-permute-done.2.refs_0_), channel_id=1, source_target_pairs={{0,14},{1,15},{2,4},{3,5},{4,2},{5,3},{6,8},{7,9},{8,6},{9,7},{10,... | collective-permute-start | bytes 589832 | tf_op jit(solution)/shard_map/ppermute | solution.py:180
  25.4 0.0 collective-permute-done.6.refs_5_.refs_4_.refs_6_
  25.4 0.0 collective-permute-done.7.refs_6_.refs_5_.refs_7_
  25.4 0.0 collective-permute-done.8.refs_7_.refs_6_.refs_8_
  25.4 3.9 %experts.8 = (bf16[64,1440]{1,0:T(8,128)(2,1)S(1)}, bf16[64,1440]{1,0:T(8,128)(2,1)S(1)}) custom-call(bf16[64,1536]{1,0:T(8,128)(2,1)S(1)} %collective-permute-done.2.refs_0_, bf16[64,1536]{1,0:T(8,128)(2,1)S(1)} %collective-permute-done.3.refs_1_, bf16[1440,1440]{1,0:T(8,128)(2,1)S(1)} %get-tuple-element.44.refs_2_.refs_1_, ...), custom_call_target="tpu_custom_call" | custom-call | flops 3185049600 | bytes 737280 | tf_op jit(solution)/shard_map/experts/pallas_call | solution.py:142
  29.2 0.0 collective-permute-done.4.refs_0_
  29.3 0.8 %collective-permute-done.5.refs_1_ = bf16[64,1536]{1,0:T(8,128)(2,1)S(1)} collective-permute-done((bf16[64,1536]{1,0:T(8,128)(2,1)S(1)}, bf16[64,1536]{1,0:T(8,128)(2,1)S(1)}, u32[]{:S(2)}, u32[]{:S(2)}) %collective-permute-start.5) | collective-permute-done | bytes 196640 | tf_op jit(solution)/shard_map/ppermute | solution.py:180
  30.1 0.4 collective-permute-start.9
  30.5 3.9 %experts.9 = (bf16[64,1440]{1,0:T(8,128)(2,1)S(1)}, bf16[64,1440]{1,0:T(8,128)(2,1)S(1)}) custom-call(bf16[64,1536]{1,0:T(8,128)(2,1)S(1)} %collective-permute-done.4.refs_0_, bf16[64,1536]{1,0:T(8,128)(2,1)S(1)} %collective-permute-done.5.refs_1_, bf16[1440,1440]{1,0:T(8,128)(2,1)S(1)} %get-tuple-element.44.refs_2_.refs_1_, ...), custom_call_target="tpu_custom_call" | custom-call | flops 3185049600 | bytes 737280 | tf_op jit(solution)/shard_map/experts/pallas_call | solution.py:142
  34.3 2.5 %collective-permute-done.9.refs_0_ = bf16[64,1536]{1,0:T(8,128)(2,1)S(1)} collective-permute-done((bf16[64,1536]{1,0:T(8,128)(2,1)S(1)}, bf16[64,1536]{1,0:T(8,128)(2,1)S(1)}, u32[]{:S(2)}, u32[]{:S(2)}) %collective-permute-start.9) | collective-permute-done | bytes 196640 | tf_op jit(solution)/shard_map/ppermute | solution.py:180
  36.8 0.0 collective-permute-start.11
  36.8 1.4 %collective-permute-start.10 = (bf16[64,1440]{1,0:T(8,128)(2,1)S(1)}, bf16[64,1440]{1,0:T(8,128)(2,1)S(1)}, u32[]{:S(2)}, u32[]{:S(2)}) collective-permute-start(bf16[64,1440]{1,0:T(8,128)(2,1)S(1)} %get-tuple-element.58), channel_id=1, source_target_pairs={{0,14},{1,15},{2,4},{3,5},{4,2},{5,3},{6,8},{7,9},{8,6},{9,7},{10,... | collective-permute-start | bytes 552968 | tf_op jit(solution)/shard_map/ppermute | solution.py:180
  38.2 3.9 %experts.10 = bf16[64,1440]{1,0:T(8,128)(2,1)S(1)} custom-call(bf16[64,1536]{1,0:T(8,128)(2,1)S(1)} %collective-permute-done.9.refs_0_, bf16[1440,1440]{1,0:T(8,128)(2,1)S(1)} %get-tuple-element.44.refs_2_.refs_1_, bf16[1440,1440]{1,0:T(8,128)(2,1)S(1)} %get-tuple-element.45.refs_3_.refs_2_, bf16[1440,1440]{1,0:T(8,128)(2,1)S(1)} %get-tuple-element.46.refs_4_.refs_3_, ...), custom_call_target="tpu_custom_call" | custom-call | flops 1592524800 | bytes 368640 | tf_op jit(solution)/shard_map/experts/pallas_call | solution.py:142
  42.1 0.7 %collective-permute-done.11 = bf16[64,1440]{1,0:T(8,128)(2,1)S(1)} collective-permute-done((bf16[64,1440]{1,0:T(8,128)(2,1)S(1)}, bf16[64,1440]{1,0:T(8,128)(2,1)S(1)}, u32[]{:S(2)}, u32[]{:S(2)}) %collective-permute-start.11) | collective-permute-done | bytes 184352 | tf_op jit(solution)/shard_map/ppermute | solution.py:180
  42.8 1.1 %collective-permute-done.10 = bf16[64,1440]{1,0:T(8,128)(2,1)S(1)} collective-permute-done((bf16[64,1440]{1,0:T(8,128)(2,1)S(1)}, bf16[64,1440]{1,0:T(8,128)(2,1)S(1)}, u32[]{:S(2)}, u32[]{:S(2)}) %collective-permute-start.10) | collective-permute-done | bytes 184352 | tf_op jit(solution)/shard_map/ppermute | solution.py:180
  43.9 1.3 %collective-permute-start.13 = (bf16[64,1440]{1,0:T(8,128)(2,1)S(1)}, bf16[64,1440]{1,0:T(8,128)(2,1)S(1)}, u32[]{:S(2)}, u32[]{:S(2)}) collective-permute-start(bf16[64,1440]{1,0:T(8,128)(2,1)S(1)} %add_convert_fusion.4), channel_id=1, source_target_pairs={{0,2},{1,3},{2,0},{3,1},{4,6},{5,7},{6,4},{7,5},{8,10},{9,11},{10,... | collective-permute-start | bytes 552968 | tf_op jit(solution)/shard_map/ppermute | solution.py:180
  45.2 0.8 %collective-permute-start.12 = (bf16[64,1440]{1,0:T(8,128)(2,1)S(1)}, bf16[64,1440]{1,0:T(8,128)(2,1)S(1)}, u32[]{:S(2)}, u32[]{:S(2)}) collective-permute-start(bf16[64,1440]{1,0:T(8,128)(2,1)S(1)} %add_convert_fusion.3), channel_id=1, source_target_pairs={{0,14},{1,15},{2,4},{3,5},{4,2},{5,3},{6,8},{7,9},{8,6},{9,7},{10,... | collective-permute-start | bytes 552968 | tf_op jit(solution)/shard_map/ppermute | solution.py:180
  46.0 3.8 %collective-permute-start.14 = (bf16[64,1440]{1,0:T(8,128)(2,1)S(1)}, bf16[64,1440]{1,0:T(8,128)(2,1)S(1)}, u32[]{:S(2)}, u32[]{:S(2)}) collective-permute-start(bf16[64,1440]{1,0:T(8,128)(2,1)S(1)} %experts.10), channel_id=1, source_target_pairs={{0,8},{1,9},{2,10},{3,11},{4,12},{5,13},{6,14},{7,15},{8,0},{9,1},... | collective-permute-start | bytes 552968 | tf_op jit(solution)/shard_map/ppermute | solution.py:180
  49.8 2.9 %experts.11 = (bf16[64,1440]{1,0:T(8,128)(2,1)S(1)}, bf16[64,1440]{1,0:T(8,128)(2,1)S(1)}, bf16[64,1440]{1,0:T(8,128)(2,1)S(1)}) custom-call(bf16[64,1536]{1,0:T(8,128)(2,1)S(1)} %route.1.refs_0_, bf16[64,1536]{1,0:T(8,128)(2,1)S(1)} %collective-permute-done.refs_0_.refs_1_, bf16[64,1536]{1,0:T(8,128)(2,1)S(1)} %collective-permute-done.1.refs_1_.refs_2_, ...), custom_call_target="tpu_custom_call" | custom-call | flops 2388787200 | bytes 1105920 | tf_op jit(solution)/shard_map/experts/pallas_call | solution.py:142
  52.7 0.2 collective-permute-done.13
  53.0 1.7 %collective-permute-done.12 = bf16[64,1440]{1,0:T(8,128)(2,1)S(1)} collective-permute-done((bf16[64,1440]{1,0:T(8,128)(2,1)S(1)}, bf16[64,1440]{1,0:T(8,128)(2,1)S(1)}, u32[]{:S(2)}, u32[]{:S(2)}) %collective-permute-start.12) | collective-permute-done | bytes 184352 | tf_op jit(solution)/shard_map/ppermute | solution.py:180
  54.8 0.5 collective-permute-start.15
  55.3 2.3 %collective-permute-start.16 = (bf16[64,1440]{1,0:T(8,128)(2,1)S(1)}, bf16[64,1440]{1,0:T(8,128)(2,1)S(1)}, u32[]{:S(2)}, u32[]{:S(2)}) collective-permute-start(bf16[64,1440]{1,0:T(8,128)(2,1)S(1)} %add_convert_fusion.1), channel_id=1, source_target_pairs={{0,14},{1,15},{2,4},{3,5},{4,2},{5,3},{6,8},{7,9},{8,6},{9,7},{10,... | collective-permute-start | bytes 552968 | tf_op jit(solution)/shard_map/ppermute | solution.py:180
  57.5 2.0 %collective-permute-done.14 = bf16[64,1440]{1,0:T(8,128)(2,1)S(1)} collective-permute-done((bf16[64,1440]{1,0:T(8,128)(2,1)S(1)}, bf16[64,1440]{1,0:T(8,128)(2,1)S(1)}, u32[]{:S(2)}, u32[]{:S(2)}) %collective-permute-start.14) | collective-permute-done | bytes 184352 | tf_op jit(solution)/shard_map/ppermute | solution.py:180
  59.6 1.2 %collective-permute-done.15 = bf16[64,1440]{1,0:T(8,128)(2,1)S(1)} collective-permute-done((bf16[64,1440]{1,0:T(8,128)(2,1)S(1)}, bf16[64,1440]{1,0:T(8,128)(2,1)S(1)}, u32[]{:S(2)}, u32[]{:S(2)}) %collective-permute-start.15) | collective-permute-done | bytes 184352 | tf_op jit(solution)/shard_map/ppermute | solution.py:180
  60.8 1.4 %collective-permute-done.16 = bf16[64,1440]{1,0:T(8,128)(2,1)S(1)} collective-permute-done((bf16[64,1440]{1,0:T(8,128)(2,1)S(1)}, bf16[64,1440]{1,0:T(8,128)(2,1)S(1)}, u32[]{:S(2)}, u32[]{:S(2)}) %collective-permute-start.16) | collective-permute-done | bytes 184352 | tf_op jit(solution)/shard_map/ppermute | solution.py:180
  62.1 0.8 %add_convert_fusion = bf16[64,1440]{1,0:T(8,128)(2,1)} fusion(bf16[64,1440]{1,0:T(8,128)(2,1)S(1)} %collective-permute-done.16, bf16[64,1440]{1,0:T(8,128)(2,1)S(1)} %collective-permute-done.15, bf16[64,1440]{1,0:T(8,128)(2,1)S(1)} %collective-permute-done.14, bf16[64,1440]{1,0:T(8,128)(2,1)S(1)} %get-tuple-element.73), kind=kLoop, calls=%fused_computation | loop fusion | flops 737280 | bytes 921600 | tf_op jit(solution)/shard_map/convert_element_type | solution.py:169
  (4 shorter events, 0.2 us)
Async XLA Ops:
  0.0 25.4 %collective-permute-start.6 = (bf16[1440,1440]{1,0:T(8,128)(2,1)}, bf16[1440,1440]{1,0:T(8,128)(2,1)S(1)}, u32[]{:S(2)}, u32[]{:S(2)}) collective-permute-start(bf16[1440,1440]{1,0:T(8,128)(2,1)} %bitcast.5), channel_id=1, source_target_pairs={{0,1},{1,0},{2,3},{3,2},{4,5},{5,4},{6,7},{7,6},{8,9},{9,8},{10,11... | collective-permute-start | bytes 12441608 | tf_op jit(solution)/shard_map/ppermute | solution.py:180
  0.0 25.4 %collective-permute-start.7 = (bf16[1440,1440]{1,0:T(8,128)(2,1)}, bf16[1440,1440]{1,0:T(8,128)(2,1)S(1)}, u32[]{:S(2)}, u32[]{:S(2)}) collective-permute-start(bf16[1440,1440]{1,0:T(8,128)(2,1)} %bitcast.6), channel_id=1, source_target_pairs={{0,1},{1,0},{2,3},{3,2},{4,5},{5,4},{6,7},{7,6},{8,9},{9,8},{10,11... | collective-permute-start | bytes 12441608 | tf_op jit(solution)/shard_map/ppermute | solution.py:180
  0.5 24.9 %collective-permute-start.8 = (bf16[1440,1440]{1,0:T(8,128)(2,1)}, bf16[1440,1440]{1,0:T(8,128)(2,1)S(1)}, u32[]{:S(2)}, u32[]{:S(2)}) collective-permute-start(bf16[1440,1440]{1,0:T(8,128)(2,1)} %bitcast.7), channel_id=1, source_target_pairs={{0,1},{1,0},{2,3},{3,2},{4,5},{5,4},{6,7},{7,6},{8,9},{9,8},{10,11... | collective-permute-start | bytes 12441608 | tf_op jit(solution)/shard_map/ppermute | solution.py:180
  2.2 12.4 %collective-permute-start = (bf16[64,1536]{1,0:T(8,128)(2,1)S(1)}, bf16[64,1536]{1,0:T(8,128)(2,1)S(1)}, u32[]{:S(2)}, u32[]{:S(2)}) collective-permute-start(bf16[64,1536]{1,0:T(8,128)(2,1)S(1)} %route.1.refs_0_), channel_id=1, source_target_pairs={{0,2},{1,3},{2,0},{3,1},{4,6},{5,7},{6,4},{7,5},{8,10},{9,11},{10,... | collective-permute-start | bytes 589832 | tf_op jit(solution)/shard_map/ppermute | solution.py:180
  4.2 10.4 %collective-permute-start.1 = (bf16[64,1536]{1,0:T(8,128)(2,1)S(1)}, bf16[64,1536]{1,0:T(8,128)(2,1)S(1)}, u32[]{:S(2)}, u32[]{:S(2)}) collective-permute-start(bf16[64,1536]{1,0:T(8,128)(2,1)S(1)} %route.1.refs_0_), channel_id=1, source_target_pairs={{0,14},{1,15},{2,4},{3,5},{4,2},{5,3},{6,8},{7,9},{8,6},{9,7},{10,... | collective-permute-start | bytes 589832 | tf_op jit(solution)/shard_map/ppermute | solution.py:180
  14.6 6.8 %collective-permute-start.2 = (bf16[64,1536]{1,0:T(8,128)(2,1)S(1)}, bf16[64,1536]{1,0:T(8,128)(2,1)S(1)}, u32[]{:S(2)}, u32[]{:S(2)}) collective-permute-start(bf16[64,1536]{1,0:T(8,128)(2,1)S(1)} %collective-permute-done.1.refs_1_.refs_2_), channel_id=1, source_target_pairs={{0,2},{1,3},{2,0},{3,1},{4,6},{5,7},{6,4},{7,5},{8,10},{9,11},{10,... | collective-permute-start | bytes 589832 | tf_op jit(solution)/shard_map/ppermute | solution.py:180
  14.7 8.0 %collective-permute-start.3 = (bf16[64,1536]{1,0:T(8,128)(2,1)S(1)}, bf16[64,1536]{1,0:T(8,128)(2,1)S(1)}, u32[]{:S(2)}, u32[]{:S(2)}) collective-permute-start(bf16[64,1536]{1,0:T(8,128)(2,1)S(1)} %collective-permute-done.refs_0_.refs_1_), channel_id=1, source_target_pairs={{0,14},{1,15},{2,4},{3,5},{4,2},{5,3},{6,8},{7,9},{8,6},{9,7},{10,... | collective-permute-start | bytes 589832 | tf_op jit(solution)/shard_map/ppermute | solution.py:180
  22.8 6.5 %collective-permute-start.4 = (bf16[64,1536]{1,0:T(8,128)(2,1)S(1)}, bf16[64,1536]{1,0:T(8,128)(2,1)S(1)}, u32[]{:S(2)}, u32[]{:S(2)}) collective-permute-start(bf16[64,1536]{1,0:T(8,128)(2,1)S(1)} %collective-permute-done.3.refs_1_), channel_id=1, source_target_pairs={{0,2},{1,3},{2,0},{3,1},{4,6},{5,7},{6,4},{7,5},{8,10},{9,11},{10,... | collective-permute-start | bytes 589832 | tf_op jit(solution)/shard_map/ppermute | solution.py:180
  23.2 6.9 %collective-permute-start.5 = (bf16[64,1536]{1,0:T(8,128)(2,1)S(1)}, bf16[64,1536]{1,0:T(8,128)(2,1)S(1)}, u32[]{:S(2)}, u32[]{:S(2)}) collective-permute-start(bf16[64,1536]{1,0:T(8,128)(2,1)S(1)} %collective-permute-done.2.refs_0_), channel_id=1, source_target_pairs={{0,14},{1,15},{2,4},{3,5},{4,2},{5,3},{6,8},{7,9},{8,6},{9,7},{10,... | collective-permute-start | bytes 589832 | tf_op jit(solution)/shard_map/ppermute | solution.py:180
  30.1 6.7 %collective-permute-start.9 = (bf16[64,1536]{1,0:T(8,128)(2,1)S(1)}, bf16[64,1536]{1,0:T(8,128)(2,1)S(1)}, u32[]{:S(2)}, u32[]{:S(2)}) collective-permute-start(bf16[64,1536]{1,0:T(8,128)(2,1)S(1)} %collective-permute-done.5.refs_1_), channel_id=1, source_target_pairs={{0,2},{1,3},{2,0},{3,1},{4,6},{5,7},{6,4},{7,5},{8,10},{9,11},{10,... | collective-permute-start | bytes 589832 | tf_op jit(solution)/shard_map/ppermute | solution.py:180
  36.8 5.9 %collective-permute-start.11 = (bf16[64,1440]{1,0:T(8,128)(2,1)S(1)}, bf16[64,1440]{1,0:T(8,128)(2,1)S(1)}, u32[]{:S(2)}, u32[]{:S(2)}) collective-permute-start(bf16[64,1440]{1,0:T(8,128)(2,1)S(1)} %get-tuple-element.60), channel_id=1, source_target_pairs={{0,2},{1,3},{2,0},{3,1},{4,6},{5,7},{6,4},{7,5},{8,10},{9,11},{10,... | collective-permute-start | bytes 552968 | tf_op jit(solution)/shard_map/ppermute | solution.py:180
  36.8 7.1 %collective-permute-start.10 = (bf16[64,1440]{1,0:T(8,128)(2,1)S(1)}, bf16[64,1440]{1,0:T(8,128)(2,1)S(1)}, u32[]{:S(2)}, u32[]{:S(2)}) collective-permute-start(bf16[64,1440]{1,0:T(8,128)(2,1)S(1)} %get-tuple-element.58), channel_id=1, source_target_pairs={{0,14},{1,15},{2,4},{3,5},{4,2},{5,3},{6,8},{7,9},{8,6},{9,7},{10,... | collective-permute-start | bytes 552968 | tf_op jit(solution)/shard_map/ppermute | solution.py:180
  43.9 9.0 %collective-permute-start.13 = (bf16[64,1440]{1,0:T(8,128)(2,1)S(1)}, bf16[64,1440]{1,0:T(8,128)(2,1)S(1)}, u32[]{:S(2)}, u32[]{:S(2)}) collective-permute-start(bf16[64,1440]{1,0:T(8,128)(2,1)S(1)} %add_convert_fusion.4), channel_id=1, source_target_pairs={{0,2},{1,3},{2,0},{3,1},{4,6},{5,7},{6,4},{7,5},{8,10},{9,11},{10,... | collective-permute-start | bytes 552968 | tf_op jit(solution)/shard_map/ppermute | solution.py:180
  45.2 9.5 %collective-permute-start.12 = (bf16[64,1440]{1,0:T(8,128)(2,1)S(1)}, bf16[64,1440]{1,0:T(8,128)(2,1)S(1)}, u32[]{:S(2)}, u32[]{:S(2)}) collective-permute-start(bf16[64,1440]{1,0:T(8,128)(2,1)S(1)} %add_convert_fusion.3), channel_id=1, source_target_pairs={{0,14},{1,15},{2,4},{3,5},{4,2},{5,3},{6,8},{7,9},{8,6},{9,7},{10,... | collective-permute-start | bytes 552968 | tf_op jit(solution)/shard_map/ppermute | solution.py:180
  46.0 13.6 %collective-permute-start.14 = (bf16[64,1440]{1,0:T(8,128)(2,1)S(1)}, bf16[64,1440]{1,0:T(8,128)(2,1)S(1)}, u32[]{:S(2)}, u32[]{:S(2)}) collective-permute-start(bf16[64,1440]{1,0:T(8,128)(2,1)S(1)} %experts.10), channel_id=1, source_target_pairs={{0,8},{1,9},{2,10},{3,11},{4,12},{5,13},{6,14},{7,15},{8,0},{9,1},... | collective-permute-start | bytes 552968 | tf_op jit(solution)/shard_map/ppermute | solution.py:180
  54.8 6.0 %collective-permute-start.15 = (bf16[64,1440]{1,0:T(8,128)(2,1)S(1)}, bf16[64,1440]{1,0:T(8,128)(2,1)S(1)}, u32[]{:S(2)}, u32[]{:S(2)}) collective-permute-start(bf16[64,1440]{1,0:T(8,128)(2,1)S(1)} %add_convert_fusion.2), channel_id=1, source_target_pairs={{0,2},{1,3},{2,0},{3,1},{4,6},{5,7},{6,4},{7,5},{8,10},{9,11},{10,... | collective-permute-start | bytes 552968 | tf_op jit(solution)/shard_map/ppermute | solution.py:180
  55.3 6.9 %collective-permute-start.16 = (bf16[64,1440]{1,0:T(8,128)(2,1)S(1)}, bf16[64,1440]{1,0:T(8,128)(2,1)S(1)}, u32[]{:S(2)}, u32[]{:S(2)}) collective-permute-start(bf16[64,1440]{1,0:T(8,128)(2,1)S(1)} %add_convert_fusion.1), channel_id=1, source_target_pairs={{0,14},{1,15},{2,4},{3,5},{4,2},{5,3},{6,8},{7,9},{8,6},{9,7},{10,... | collective-permute-start | bytes 552968 | tf_op jit(solution)/shard_map/ppermute | solution.py:180

commit v6 on v5

--- a/solution.py
+++ b/solution.py
@@ -209,9 +209,10 @@
     te2, to2, t4, p0, p1 = fence((add(te2, ro), add(to2, re), t4, p0, p1))
     re, ro = send(te2, even), send(to2, odd)
     r4 = send(t4, across)
-    t0, te1, to1 = experts_apply(experts, [own, e1, o1], None, far, [*p0, *p1], rows, BF16)
-    te1, to1, t0 = fence((add(te1, ro), add(to1, re), t0))
+    te1, to1 = experts_apply(experts, [e1, o1], None, far, p1, rows, BF16)
+    te1, to1, p0 = fence((add(te1, ro), add(to1, re), p0))
     re, ro = send(te1, even), send(to1, odd)
+    (t0,) = experts_apply(experts, [own], None, far, p0, rows, BF16)
     return add(t0, r4, re, ro)
 
 

time: 63 us -> 64.4 us (1.022)
  Pallas kernels: 23 us -> 24.1 us
    pallas_call x6 -> x7, Pallas kernels: 22 us -> 23.1 us  [experts_apply(): pl.pallas_call(body, out_shape=out_shape, in_specs=[vmem] * (count + len(...]
  transfers between devices with their start and end apart: 17 -> 17, of which waited for: 11 -> 10; matrix products, arithmetic and copies ran while one was open for 0% -> 0% of each run, Pallas kernels for 37% -> 37%
where the time goes in v6:
time: 64.4 us; the launch traced here: 64.3 us
  Pallas kernels  24.1 us (37%)
  starting transfers between devices  22.9 us (36%)
  waiting for transfers between devices  15.5 us (24%)
  other arithmetic  0.97 us (2%)
  between operations  0.79 us (1%)
    pallas_call x7, Pallas kernels, experts_apply(): pl.pallas_call(body, out_shape=out_shape, in_specs=[vmem] * (count + len(...  23.1 us
    ppermute x17, starting transfers between devices, send(): return lax.ppermute(x, 'ep', pairs)  22.9 us
    ppermute x17, waiting for transfers between devices, send(): return lax.ppermute(x, 'ep', pairs)  15.5 us
  transfers between devices with their start and end apart: 17, of which 10 were waited for; matrix products, arithmetic and copies ran while one was open for 0% of the time, Pallas kernels for 37%

profile of v6, /device:TPU:26, one launch (start us, length us, event | category | flops | bytes accessed | tf_op | source)
XLA Modules:
  0.0 64.3 jit_solution(80095031944426893)
XLA Ops:
  0.0 0.0 collective-permute-start.6
  0.0 0.5 collective-permute-start.7
  0.5 0.0 collective-permute-start.8
  1.2 1.0 %route.1.refs_0_ = bf16[64,1536]{1,0:T(8,128)(2,1)S(1)} custom-call(s32[1]{0:T(128)S(6)} %copy.8.refs_0_, bf16[64,1440]{1,0:T(8,128)(2,1)} %refs_1_.2, s32[4,64]{1,0:T(4,128)} %bitcast.8, f32[4,64]{1,0:T(4,128)} %bitcast.9), custom_call_target="tpu_custom_call" | custom-call | tf_op jit(solution)/shard_map/route/pallas_call | solution.py:183
  2.2 2.0 %collective-permute-start = (bf16[64,1536]{1,0:T(8,128)(2,1)S(1)}, bf16[64,1536]{1,0:T(8,128)(2,1)S(1)}, u32[]{:S(2)}, u32[]{:S(2)}) collective-permute-start(bf16[64,1536]{1,0:T(8,128)(2,1)S(1)} %route.1.refs_0_), channel_id=1, source_target_pairs={{0,2},{1,3},{2,0},{3,1},{4,6},{5,7},{6,4},{7,5},{8,10},{9,11},{10,... | collective-permute-start | bytes 589832 | tf_op jit(solution)/shard_map/ppermute | solution.py:180
  4.2 4.9 %collective-permute-start.1 = (bf16[64,1536]{1,0:T(8,128)(2,1)S(1)}, bf16[64,1536]{1,0:T(8,128)(2,1)S(1)}, u32[]{:S(2)}, u32[]{:S(2)}) collective-permute-start(bf16[64,1536]{1,0:T(8,128)(2,1)S(1)} %route.1.refs_0_), channel_id=1, source_target_pairs={{0,14},{1,15},{2,4},{3,5},{4,2},{5,3},{6,8},{7,9},{8,6},{9,7},{10,... | collective-permute-start | bytes 589832 | tf_op jit(solution)/shard_map/ppermute | solution.py:180
  9.2 5.4 %experts.7 = (f32[64,1440]{1,0:T(8,128)S(1)}, bf16[1440,1440]{1,0:T(8,128)(2,1)S(1)}, bf16[1440,1440]{1,0:T(8,128)(2,1)S(1)}, bf16[1440,1440]{1,0:T(8,128)(2,1)S(1)}) custom-call(bf16[64,1536]{1,0:T(8,128)(2,1)S(1)} %route.1.refs_0_, bf16[1,1440,1440]{2,1,0:T(8,128)(2,1)} %refs_1_.3, bf16[1,1440,1440]{2,1,0:T(8,128)(2,1)} %refs_2_.1, ...), custom_call_target="tpu_custom_call" | custom-call | flops 796262400 | bytes 368640 | tf_op jit(solution)/shard_map/experts/pallas_call | solution.py:142
  14.6 0.0 collective-permute-done.refs_0_
  14.6 0.0 collective-permute-done.1.refs_1_
  14.6 0.1 collective-permute-start.2
  14.7 2.7 %collective-permute-start.3 = (bf16[64,1536]{1,0:T(8,128)(2,1)S(1)}, bf16[64,1536]{1,0:T(8,128)(2,1)S(1)}, u32[]{:S(2)}, u32[]{:S(2)}) collective-permute-start(bf16[64,1536]{1,0:T(8,128)(2,1)S(1)} %collective-permute-done.refs_0_), channel_id=1, source_target_pairs={{0,14},{1,15},{2,4},{3,5},{4,2},{5,3},{6,8},{7,9},{8,6},{9,7},{10,... | collective-permute-start | bytes 589832 | tf_op jit(solution)/shard_map/ppermute | solution.py:180
  17.4 2.0 %experts.8 = (f32[64,1440]{1,0:T(8,128)S(1)}, f32[64,1440]{1,0:T(8,128)S(1)}) custom-call(bf16[64,1536]{1,0:T(8,128)(2,1)S(1)} %collective-permute-done.refs_0_, bf16[64,1536]{1,0:T(8,128)(2,1)S(1)} %collective-permute-done.1.refs_1_, bf16[1440,1440]{1,0:T(8,128)(2,1)S(1)} %get-tuple-element.43.refs_2_.refs_1_, ...), custom_call_target="tpu_custom_call" | custom-call | flops 1592524800 | bytes 737280 | tf_op jit(solution)/shard_map/experts/pallas_call | solution.py:142
  19.4 2.0 %collective-permute-done.2.refs_0_ = bf16[64,1536]{1,0:T(8,128)(2,1)S(1)} collective-permute-done((bf16[64,1536]{1,0:T(8,128)(2,1)S(1)}, bf16[64,1536]{1,0:T(8,128)(2,1)S(1)}, u32[]{:S(2)}, u32[]{:S(2)}) %collective-permute-start.2) | collective-permute-done | bytes 196640 | tf_op jit(solution)/shard_map/ppermute | solution.py:180
  21.5 1.3 %collective-permute-done.3.refs_1_ = bf16[64,1536]{1,0:T(8,128)(2,1)S(1)} collective-permute-done((bf16[64,1536]{1,0:T(8,128)(2,1)S(1)}, bf16[64,1536]{1,0:T(8,128)(2,1)S(1)}, u32[]{:S(2)}, u32[]{:S(2)}) %collective-permute-start.3) | collective-permute-done | bytes 196640 | tf_op jit(solution)/shard_map/ppermute | solution.py:180
  22.8 0.4 collective-permute-start.4
  23.2 2.2 %collective-permute-start.5 = (bf16[64,1536]{1,0:T(8,128)(2,1)S(1)}, bf16[64,1536]{1,0:T(8,128)(2,1)S(1)}, u32[]{:S(2)}, u32[]{:S(2)}) collective-permute-start(bf16[64,1536]{1,0:T(8,128)(2,1)S(1)} %collective-permute-done.2.refs_0_), channel_id=1, source_target_pairs={{0,14},{1,15},{2,4},{3,5},{4,2},{5,3},{6,8},{7,9},{8,6},{9,7},{10,... | collective-permute-start | bytes 589832 | tf_op jit(solution)/shard_map/ppermute | solution.py:180
  25.4 0.0 collective-permute-done.6.refs_5_.refs_4_.refs_2_
  25.4 0.0 collective-permute-done.7.refs_6_.refs_5_.refs_3_
  25.4 0.0 collective-permute-done.8.refs_7_.refs_6_.refs_4_
  25.4 3.9 %experts.9 = (bf16[64,1440]{1,0:T(8,128)(2,1)S(1)}, bf16[64,1440]{1,0:T(8,128)(2,1)S(1)}) custom-call(bf16[64,1536]{1,0:T(8,128)(2,1)S(1)} %collective-permute-done.2.refs_0_, bf16[64,1536]{1,0:T(8,128)(2,1)S(1)} %collective-permute-done.3.refs_1_, bf16[1440,1440]{1,0:T(8,128)(2,1)S(1)} %get-tuple-element.43.refs_2_.refs_1_, ...), custom_call_target="tpu_custom_call" | custom-call | flops 3185049600 | bytes 737280 | tf_op jit(solution)/shard_map/experts/pallas_call | solution.py:142
  29.2 0.0 collective-permute-done.4.refs_0_
  29.3 0.8 %collective-permute-done.5.refs_1_ = bf16[64,1536]{1,0:T(8,128)(2,1)S(1)} collective-permute-done((bf16[64,1536]{1,0:T(8,128)(2,1)S(1)}, bf16[64,1536]{1,0:T(8,128)(2,1)S(1)}, u32[]{:S(2)}, u32[]{:S(2)}) %collective-permute-start.5) | collective-permute-done | bytes 196640 | tf_op jit(solution)/shard_map/ppermute | solution.py:180
  30.1 0.4 collective-permute-start.9
  30.5 3.9 %experts.10 = (bf16[64,1440]{1,0:T(8,128)(2,1)S(1)}, bf16[64,1440]{1,0:T(8,128)(2,1)S(1)}) custom-call(bf16[64,1536]{1,0:T(8,128)(2,1)S(1)} %collective-permute-done.4.refs_0_, bf16[64,1536]{1,0:T(8,128)(2,1)S(1)} %collective-permute-done.5.refs_1_, bf16[1440,1440]{1,0:T(8,128)(2,1)S(1)} %get-tuple-element.43.refs_2_.refs_1_, ...), custom_call_target="tpu_custom_call" | custom-call | flops 3185049600 | bytes 737280 | tf_op jit(solution)/shard_map/experts/pallas_call | solution.py:142
  34.3 2.5 %collective-permute-done.9.refs_0_ = bf16[64,1536]{1,0:T(8,128)(2,1)S(1)} collective-permute-done((bf16[64,1536]{1,0:T(8,128)(2,1)S(1)}, bf16[64,1536]{1,0:T(8,128)(2,1)S(1)}, u32[]{:S(2)}, u32[]{:S(2)}) %collective-permute-start.9) | collective-permute-done | bytes 196640 | tf_op jit(solution)/shard_map/ppermute | solution.py:180
  36.8 0.0 collective-permute-start.11
  36.8 1.4 %collective-permute-start.10 = (bf16[64,1440]{1,0:T(8,128)(2,1)S(1)}, bf16[64,1440]{1,0:T(8,128)(2,1)S(1)}, u32[]{:S(2)}, u32[]{:S(2)}) collective-permute-start(bf16[64,1440]{1,0:T(8,128)(2,1)S(1)} %get-tuple-element.57), channel_id=1, source_target_pairs={{0,14},{1,15},{2,4},{3,5},{4,2},{5,3},{6,8},{7,9},{8,6},{9,7},{10,... | collective-permute-start | bytes 552968 | tf_op jit(solution)/shard_map/ppermute | solution.py:180
  38.2 3.9 %experts.11 = bf16[64,1440]{1,0:T(8,128)(2,1)S(1)} custom-call(bf16[64,1536]{1,0:T(8,128)(2,1)S(1)} %collective-permute-done.9.refs_0_, bf16[1440,1440]{1,0:T(8,128)(2,1)S(1)} %get-tuple-element.43.refs_2_.refs_1_, bf16[1440,1440]{1,0:T(8,128)(2,1)S(1)} %get-tuple-element.44.refs_3_.refs_2_, bf16[1440,1440]{1,0:T(8,128)(2,1)S(1)} %get-tuple-element.45.refs_4_.refs_3_, ...), custom_call_target="tpu_custom_call" | custom-call | flops 1592524800 | bytes 368640 | tf_op jit(solution)/shard_map/experts/pallas_call | solution.py:142
  42.1 0.7 %collective-permute-done.11 = bf16[64,1440]{1,0:T(8,128)(2,1)S(1)} collective-permute-done((bf16[64,1440]{1,0:T(8,128)(2,1)S(1)}, bf16[64,1440]{1,0:T(8,128)(2,1)S(1)}, u32[]{:S(2)}, u32[]{:S(2)}) %collective-permute-start.11) | collective-permute-done | bytes 184352 | tf_op jit(solution)/shard_map/ppermute | solution.py:180
  42.8 1.1 %collective-permute-done.10 = bf16[64,1440]{1,0:T(8,128)(2,1)S(1)} collective-permute-done((bf16[64,1440]{1,0:T(8,128)(2,1)S(1)}, bf16[64,1440]{1,0:T(8,128)(2,1)S(1)}, u32[]{:S(2)}, u32[]{:S(2)}) %collective-permute-start.10) | collective-permute-done | bytes 184352 | tf_op jit(solution)/shard_map/ppermute | solution.py:180
  43.9 1.3 %collective-permute-start.13 = (bf16[64,1440]{1,0:T(8,128)(2,1)S(1)}, bf16[64,1440]{1,0:T(8,128)(2,1)S(1)}, u32[]{:S(2)}, u32[]{:S(2)}) collective-permute-start(bf16[64,1440]{1,0:T(8,128)(2,1)S(1)} %add_convert_fusion.4), channel_id=1, source_target_pairs={{0,2},{1,3},{2,0},{3,1},{4,6},{5,7},{6,4},{7,5},{8,10},{9,11},{10,... | collective-permute-start | bytes 552968 | tf_op jit(solution)/shard_map/ppermute | solution.py:180
  45.2 0.8 %collective-permute-start.12 = (bf16[64,1440]{1,0:T(8,128)(2,1)S(1)}, bf16[64,1440]{1,0:T(8,128)(2,1)S(1)}, u32[]{:S(2)}, u32[]{:S(2)}) collective-permute-start(bf16[64,1440]{1,0:T(8,128)(2,1)S(1)} %add_convert_fusion.3), channel_id=1, source_target_pairs={{0,14},{1,15},{2,4},{3,5},{4,2},{5,3},{6,8},{7,9},{8,6},{9,7},{10,... | collective-permute-start | bytes 552968 | tf_op jit(solution)/shard_map/ppermute | solution.py:180
  46.0 3.8 %collective-permute-start.14 = (bf16[64,1440]{1,0:T(8,128)(2,1)S(1)}, bf16[64,1440]{1,0:T(8,128)(2,1)S(1)}, u32[]{:S(2)}, u32[]{:S(2)}) collective-permute-start(bf16[64,1440]{1,0:T(8,128)(2,1)S(1)} %experts.11), channel_id=1, source_target_pairs={{0,8},{1,9},{2,10},{3,11},{4,12},{5,13},{6,14},{7,15},{8,0},{9,1},... | collective-permute-start | bytes 552968 | tf_op jit(solution)/shard_map/ppermute | solution.py:180
  49.8 2.0 %experts.12 = (bf16[64,1440]{1,0:T(8,128)(2,1)S(1)}, bf16[64,1440]{1,0:T(8,128)(2,1)S(1)}) custom-call(bf16[64,1536]{1,0:T(8,128)(2,1)S(1)} %collective-permute-done.refs_0_, bf16[64,1536]{1,0:T(8,128)(2,1)S(1)} %collective-permute-done.1.refs_1_, f32[64,1440]{1,0:T(8,128)S(1)} %get-tuple-element.64.refs_2_, f32[64,1440]{1,0:T(8,128)S(1)} %get-tuple-element.65.refs_3_, ...), custom_call_target="tpu_custom_call" | custom-call | flops 1592524800 | bytes 737280 | tf_op jit(solution)/shard_map/experts/pallas_call | solution.py:142
  51.8 1.1 %collective-permute-done.13 = bf16[64,1440]{1,0:T(8,128)(2,1)S(1)} collective-permute-done((bf16[64,1440]{1,0:T(8,128)(2,1)S(1)}, bf16[64,1440]{1,0:T(8,128)(2,1)S(1)}, u32[]{:S(2)}, u32[]{:S(2)}) %collective-permute-start.13) | collective-permute-done | bytes 184352 | tf_op jit(solution)/shard_map/ppermute | solution.py:180
  53.0 3.4 %collective-permute-done.12 = bf16[64,1440]{1,0:T(8,128)(2,1)S(1)} collective-permute-done((bf16[64,1440]{1,0:T(8,128)(2,1)S(1)}, bf16[64,1440]{1,0:T(8,128)(2,1)S(1)}, u32[]{:S(2)}, u32[]{:S(2)}) %collective-permute-start.12) | collective-permute-done | bytes 184352 | tf_op jit(solution)/shard_map/ppermute | solution.py:180
  56.4 0.1 collective-permute-start.15
  56.5 2.3 %collective-permute-start.16 = (bf16[64,1440]{1,0:T(8,128)(2,1)S(1)}, bf16[64,1440]{1,0:T(8,128)(2,1)S(1)}, u32[]{:S(2)}, u32[]{:S(2)}) collective-permute-start(bf16[64,1440]{1,0:T(8,128)(2,1)S(1)} %add_convert_fusion.1), channel_id=1, source_target_pairs={{0,14},{1,15},{2,4},{3,5},{4,2},{5,3},{6,8},{7,9},{8,6},{9,7},{10,... | collective-permute-start | bytes 552968 | tf_op jit(solution)/shard_map/ppermute | solution.py:180
  58.9 2.0 %experts.13 = bf16[64,1440]{1,0:T(8,128)(2,1)S(1)} custom-call(bf16[64,1536]{1,0:T(8,128)(2,1)S(1)} %route.1.refs_0_, f32[64,1440]{1,0:T(8,128)S(1)} %get-tuple-element.71.refs_1_, bf16[1440,1440]{1,0:T(8,128)(2,1)S(1)} %collective-permute-done.6.refs_5_.refs_4_.refs_2_, bf16[1440,1440]{1,0:T(8,128)(2,1)S(1)} %collective-permute-done.7.refs_6_.refs_5_.refs_3_, ...), custom_call_target="tpu_custom_call" | custom-call | flops 796262400 | bytes 368640 | tf_op jit(solution)/shard_map/experts/pallas_call | solution.py:142
  60.9 0.0 collective-permute-done.14
  60.9 1.3 %collective-permute-done.15 = bf16[64,1440]{1,0:T(8,128)(2,1)S(1)} collective-permute-done((bf16[64,1440]{1,0:T(8,128)(2,1)S(1)}, bf16[64,1440]{1,0:T(8,128)(2,1)S(1)}, u32[]{:S(2)}, u32[]{:S(2)}) %collective-permute-start.15) | collective-permute-done | bytes 184352 | tf_op jit(solution)/shard_map/ppermute | solution.py:180
  62.2 1.3 %collective-permute-done.16 = bf16[64,1440]{1,0:T(8,128)(2,1)S(1)} collective-permute-done((bf16[64,1440]{1,0:T(8,128)(2,1)S(1)}, bf16[64,1440]{1,0:T(8,128)(2,1)S(1)}, u32[]{:S(2)}, u32[]{:S(2)}) %collective-permute-start.16) | collective-permute-done | bytes 184352 | tf_op jit(solution)/shard_map/ppermute | solution.py:180
  63.5 0.8 %add_convert_fusion = bf16[64,1440]{1,0:T(8,128)(2,1)} fusion(bf16[64,1440]{1,0:T(8,128)(2,1)S(1)} %collective-permute-done.16, bf16[64,1440]{1,0:T(8,128)(2,1)S(1)} %collective-permute-done.15, bf16[64,1440]{1,0:T(8,128)(2,1)S(1)} %collective-permute-done.14, bf16[64,1440]{1,0:T(8,128)(2,1)S(1)} %experts.13), kind=kLoop, calls=%fused_computation | loop fusion | flops 737280 | bytes 921600 | tf_op jit(solution)/shard_map/convert_element_type | solution.py:169
  (4 shorter events, 0.2 us)
Async XLA Ops:
  0.0 25.4 %collective-permute-start.6 = (bf16[1440,1440]{1,0:T(8,128)(2,1)}, bf16[1440,1440]{1,0:T(8,128)(2,1)S(1)}, u32[]{:S(2)}, u32[]{:S(2)}) collective-permute-start(bf16[1440,1440]{1,0:T(8,128)(2,1)} %bitcast.5), channel_id=1, source_target_pairs={{0,1},{1,0},{2,3},{3,2},{4,5},{5,4},{6,7},{7,6},{8,9},{9,8},{10,11... | collective-permute-start | bytes 12441608 | tf_op jit(solution)/shard_map/ppermute | solution.py:180
  0.0 25.4 %collective-permute-start.7 = (bf16[1440,1440]{1,0:T(8,128)(2,1)}, bf16[1440,1440]{1,0:T(8,128)(2,1)S(1)}, u32[]{:S(2)}, u32[]{:S(2)}) collective-permute-start(bf16[1440,1440]{1,0:T(8,128)(2,1)} %bitcast.6), channel_id=1, source_target_pairs={{0,1},{1,0},{2,3},{3,2},{4,5},{5,4},{6,7},{7,6},{8,9},{9,8},{10,11... | collective-permute-start | bytes 12441608 | tf_op jit(solution)/shard_map/ppermute | solution.py:180
  0.5 24.9 %collective-permute-start.8 = (bf16[1440,1440]{1,0:T(8,128)(2,1)}, bf16[1440,1440]{1,0:T(8,128)(2,1)S(1)}, u32[]{:S(2)}, u32[]{:S(2)}) collective-permute-start(bf16[1440,1440]{1,0:T(8,128)(2,1)} %bitcast.7), channel_id=1, source_target_pairs={{0,1},{1,0},{2,3},{3,2},{4,5},{5,4},{6,7},{7,6},{8,9},{9,8},{10,11... | collective-permute-start | bytes 12441608 | tf_op jit(solution)/shard_map/ppermute | solution.py:180
  2.2 12.4 %collective-permute-start = (bf16[64,1536]{1,0:T(8,128)(2,1)S(1)}, bf16[64,1536]{1,0:T(8,128)(2,1)S(1)}, u32[]{:S(2)}, u32[]{:S(2)}) collective-permute-start(bf16[64,1536]{1,0:T(8,128)(2,1)S(1)} %route.1.refs_0_), channel_id=1, source_target_pairs={{0,2},{1,3},{2,0},{3,1},{4,6},{5,7},{6,4},{7,5},{8,10},{9,11},{10,... | collective-permute-start | bytes 589832 | tf_op jit(solution)/shard_map/ppermute | solution.py:180
  4.2 10.4 %collective-permute-start.1 = (bf16[64,1536]{1,0:T(8,128)(2,1)S(1)}, bf16[64,1536]{1,0:T(8,128)(2,1)S(1)}, u32[]{:S(2)}, u32[]{:S(2)}) collective-permute-start(bf16[64,1536]{1,0:T(8,128)(2,1)S(1)} %route.1.refs_0_), channel_id=1, source_target_pairs={{0,14},{1,15},{2,4},{3,5},{4,2},{5,3},{6,8},{7,9},{8,6},{9,7},{10,... | collective-permute-start | bytes 589832 | tf_op jit(solution)/shard_map/ppermute | solution.py:180
  14.6 6.8 %collective-permute-start.2 = (bf16[64,1536]{1,0:T(8,128)(2,1)S(1)}, bf16[64,1536]{1,0:T(8,128)(2,1)S(1)}, u32[]{:S(2)}, u32[]{:S(2)}) collective-permute-start(bf16[64,1536]{1,0:T(8,128)(2,1)S(1)} %collective-permute-done.1.refs_1_), channel_id=1, source_target_pairs={{0,2},{1,3},{2,0},{3,1},{4,6},{5,7},{6,4},{7,5},{8,10},{9,11},{10,... | collective-permute-start | bytes 589832 | tf_op jit(solution)/shard_map/ppermute | solution.py:180
  14.7 8.0 %collective-permute-start.3 = (bf16[64,1536]{1,0:T(8,128)(2,1)S(1)}, bf16[64,1536]{1,0:T(8,128)(2,1)S(1)}, u32[]{:S(2)}, u32[]{:S(2)}) collective-permute-start(bf16[64,1536]{1,0:T(8,128)(2,1)S(1)} %collective-permute-done.refs_0_), channel_id=1, source_target_pairs={{0,14},{1,15},{2,4},{3,5},{4,2},{5,3},{6,8},{7,9},{8,6},{9,7},{10,... | collective-permute-start | bytes 589832 | tf_op jit(solution)/shard_map/ppermute | solution.py:180
  22.8 6.5 %collective-permute-start.4 = (bf16[64,1536]{1,0:T(8,128)(2,1)S(1)}, bf16[64,1536]{1,0:T(8,128)(2,1)S(1)}, u32[]{:S(2)}, u32[]{:S(2)}) collective-permute-start(bf16[64,1536]{1,0:T(8,128)(2,1)S(1)} %collective-permute-done.3.refs_1_), channel_id=1, source_target_pairs={{0,2},{1,3},{2,0},{3,1},{4,6},{5,7},{6,4},{7,5},{8,10},{9,11},{10,... | collective-permute-start | bytes 589832 | tf_op jit(solution)/shard_map/ppermute | solution.py:180
  23.2 6.9 %collective-permute-start.5 = (bf16[64,1536]{1,0:T(8,128)(2,1)S(1)}, bf16[64,1536]{1,0:T(8,128)(2,1)S(1)}, u32[]{:S(2)}, u32[]{:S(2)}) collective-permute-start(bf16[64,1536]{1,0:T(8,128)(2,1)S(1)} %collective-permute-done.2.refs_0_), channel_id=1, source_target_pairs={{0,14},{1,15},{2,4},{3,5},{4,2},{5,3},{6,8},{7,9},{8,6},{9,7},{10,... | collective-permute-start | bytes 589832 | tf_op jit(solution)/shard_map/ppermute | solution.py:180
  30.1 6.7 %collective-permute-start.9 = (bf16[64,1536]{1,0:T(8,128)(2,1)S(1)}, bf16[64,1536]{1,0:T(8,128)(2,1)S(1)}, u32[]{:S(2)}, u32[]{:S(2)}) collective-permute-start(bf16[64,1536]{1,0:T(8,128)(2,1)S(1)} %collective-permute-done.5.refs_1_), channel_id=1, source_target_pairs={{0,2},{1,3},{2,0},{3,1},{4,6},{5,7},{6,4},{7,5},{8,10},{9,11},{10,... | collective-permute-start | bytes 589832 | tf_op jit(solution)/shard_map/ppermute | solution.py:180
  36.8 5.9 %collective-permute-start.11 = (bf16[64,1440]{1,0:T(8,128)(2,1)S(1)}, bf16[64,1440]{1,0:T(8,128)(2,1)S(1)}, u32[]{:S(2)}, u32[]{:S(2)}) collective-permute-start(bf16[64,1440]{1,0:T(8,128)(2,1)S(1)} %get-tuple-element.59), channel_id=1, source_target_pairs={{0,2},{1,3},{2,0},{3,1},{4,6},{5,7},{6,4},{7,5},{8,10},{9,11},{10,... | collective-permute-start | bytes 552968 | tf_op jit(solution)/shard_map/ppermute | solution.py:180
  36.8 7.1 %collective-permute-start.10 = (bf16[64,1440]{1,0:T(8,128)(2,1)S(1)}, bf16[64,1440]{1,0:T(8,128)(2,1)S(1)}, u32[]{:S(2)}, u32[]{:S(2)}) collective-permute-start(bf16[64,1440]{1,0:T(8,128)(2,1)S(1)} %get-tuple-element.57), channel_id=1, source_target_pairs={{0,14},{1,15},{2,4},{3,5},{4,2},{5,3},{6,8},{7,9},{8,6},{9,7},{10,... | collective-permute-start | bytes 552968 | tf_op jit(solution)/shard_map/ppermute | solution.py:180
  43.9 9.0 %collective-permute-start.13 = (bf16[64,1440]{1,0:T(8,128)(2,1)S(1)}, bf16[64,1440]{1,0:T(8,128)(2,1)S(1)}, u32[]{:S(2)}, u32[]{:S(2)}) collective-permute-start(bf16[64,1440]{1,0:T(8,128)(2,1)S(1)} %add_convert_fusion.4), channel_id=1, source_target_pairs={{0,2},{1,3},{2,0},{3,1},{4,6},{5,7},{6,4},{7,5},{8,10},{9,11},{10,... | collective-permute-start | bytes 552968 | tf_op jit(solution)/shard_map/ppermute | solution.py:180
  45.2 11.2 %collective-permute-start.12 = (bf16[64,1440]{1,0:T(8,128)(2,1)S(1)}, bf16[64,1440]{1,0:T(8,128)(2,1)S(1)}, u32[]{:S(2)}, u32[]{:S(2)}) collective-permute-start(bf16[64,1440]{1,0:T(8,128)(2,1)S(1)} %add_convert_fusion.3), channel_id=1, source_target_pairs={{0,14},{1,15},{2,4},{3,5},{4,2},{5,3},{6,8},{7,9},{8,6},{9,7},{10,... | collective-permute-start | bytes 552968 | tf_op jit(solution)/shard_map/ppermute | solution.py:180
  46.0 14.9 %collective-permute-start.14 = (bf16[64,1440]{1,0:T(8,128)(2,1)S(1)}, bf16[64,1440]{1,0:T(8,128)(2,1)S(1)}, u32[]{:S(2)}, u32[]{:S(2)}) collective-permute-start(bf16[64,1440]{1,0:T(8,128)(2,1)S(1)} %experts.11), channel_id=1, source_target_pairs={{0,8},{1,9},{2,10},{3,11},{4,12},{5,13},{6,14},{7,15},{8,0},{9,1},... | collective-permute-start | bytes 552968 | tf_op jit(solution)/shard_map/ppermute | solution.py:180
  56.4 5.8 %collective-permute-start.15 = (bf16[64,1440]{1,0:T(8,128)(2,1)S(1)}, bf16[64,1440]{1,0:T(8,128)(2,1)S(1)}, u32[]{:S(2)}, u32[]{:S(2)}) collective-permute-start(bf16[64,1440]{1,0:T(8,128)(2,1)S(1)} %add_convert_fusion.2), channel_id=1, source_target_pairs={{0,2},{1,3},{2,0},{3,1},{4,6},{5,7},{6,4},{7,5},{8,10},{9,11},{10,... | collective-permute-start | bytes 552968 | tf_op jit(solution)/shard_map/ppermute | solution.py:180
  56.5 7.0 %collective-permute-start.16 = (bf16[64,1440]{1,0:T(8,128)(2,1)S(1)}, bf16[64,1440]{1,0:T(8,128)(2,1)S(1)}, u32[]{:S(2)}, u32[]{:S(2)}) collective-permute-start(bf16[64,1440]{1,0:T(8,128)(2,1)S(1)} %add_convert_fusion.1), channel_id=1, source_target_pairs={{0,14},{1,15},{2,4},{3,5},{4,2},{5,3},{6,8},{7,9},{8,6},{9,7},{10,... | collective-permute-start | bytes 552968 | tf_op jit(solution)/shard_map/ppermute | solution.py:180
